TPU v7x, 128 devices: a whole 4x4x4 slice. The times are simulated.
128 devices in a mesh: wide: 32 (over z, y, core), narrow: 4 (over x).
Axes of the slice: x: 4, y: 4, z: 4, core: 2. Of those that a mesh axis runs over, the one named last changes fastest.
Arguments:
- desc_a: bfloat16 [16384, 128], P('wide'), may hold values from -6 to 6
- desc_b: bfloat16 [32768, 128], P('narrow'), may hold values from -6 to 6
- logmass_a: float32 [16384], P('wide'), may hold values from -6 to 6
- logmass_b: float32 [32768], P('narrow'), may hold values from -6 to 6
- g_start: float32 [32768], P('narrow'), may hold values from -1 to 16, as said below
Outputs:
- potential_a: float32 [16384], P('wide')
- potential_b: float32 [32768], P('narrow')
- flow_a: float32 [16384, 128], P('wide')
- flow_b: float32 [32768, 128], P(('narrow', 'wide'))
Inputs may be any that keep to these rules, and one draw needn't show every extreme that they name: `g_start`: potentials of view B carried over from the previous pair of views.
All inputs are finite; a program needn't handle non-finite values.
Results may differ from a plain program's by a relative error of at most 0.01.
Values may be sent and summed in bfloat16 or wider, within the bound.
No kernel may reach another device: no remote copies, remote signals or barrier semaphores. Data moves between devices by JAX's collectives and lax.ppermute only.
A program may use at most 64 MiB of HBM per device.

v0:
```python
import jax
import jax.numpy as jnp
from jax import lax
from jax.sharding import PartitionSpec as P

ITERS = 2


EPS = 0.05


def unit_rows(desc):
    wide32 = desc.astype(jnp.float32)
    return (wide32 / jnp.sqrt(jnp.sum(wide32 * wide32, axis=1, keepdims=True) + 1e-06)).astype(
        jnp.bfloat16
    )


def cost_of(left, right):
    return 2.0 - 2.0 * lax.dot_general(
        left, right, (((1,), (1,)), ((), ())), preferred_element_type=jnp.float32
    )


def left_product(weights, tile_a):
    return lax.dot_general(
        weights, tile_a, (((0,), (0,)), ((), ())), preferred_element_type=jnp.float32
    )


def finish_rows(highest, summed):
    overall = lax.pmax(highest, "narrow")
    summed = lax.psum(summed * jnp.exp(highest - overall), "narrow")
    highest = overall
    return highest + jnp.log(summed)


def finish_cols(highest, summed):
    overall = lax.pmax(highest.astype(jnp.bfloat16), "wide").astype(highest.dtype)
    summed = lax.psum((summed * jnp.exp(highest - overall)).astype(jnp.bfloat16), "wide").astype(
        jnp.float32
    )
    highest = overall
    return highest + jnp.log(summed)


def row_update(state_now, pot_part, cost):
    highest, summed = state_now
    scores = (pot_part[None, :] - cost) / EPS
    new_high = jnp.maximum(highest, jnp.max(scores, axis=1))
    summed = summed * jnp.exp(highest - new_high) + jnp.sum(
        jnp.exp(scores - new_high[:, None]), axis=1
    )
    return (new_high, summed)


def on_device(desc_a, desc_b, logmass_a, logmass_b, g_start):
    unit_a = unit_rows(desc_a)
    unit_b = unit_rows(desc_b)
    n_rows, feat_width = unit_a.shape
    n_cols = unit_b.shape[0]
    col_span = min(n_cols, 2048)
    n_tiles = n_cols // col_span
    b_tiles = unit_b.reshape(n_tiles, col_span, feat_width)
    row_init = (jnp.full((n_rows,), -jnp.inf, jnp.float32), jnp.zeros((n_rows,), jnp.float32))

    def row_partial(potential):

        def row_one_tile(state_now, inputs):
            tile_b, pot_part = inputs
            return (row_update(state_now, pot_part, cost_of(unit_a, tile_b)), None)

        result, _ = lax.scan(
            row_one_tile, row_init, (b_tiles, potential.reshape(n_tiles, col_span))
        )
        return result

    potential_b = g_start
    for sweep_index in range(ITERS):
        row_pot = EPS * logmass_a - EPS * finish_rows(*row_partial(potential_b))

        def col_one_tile(tile_b):
            scores = (row_pot[:, None] - cost_of(unit_a, tile_b)) / EPS
            highest = jnp.max(scores, axis=0)
            return (highest, jnp.sum(jnp.exp(scores - highest[None, :]), axis=0))

        highest, summed = lax.map(col_one_tile, b_tiles)
        lse_b = finish_cols(*(highest.reshape(n_cols), summed.reshape(n_cols)))
        potential_b = EPS * logmass_b - EPS * lse_b
    my_share = n_cols // lax.axis_size("wide")
    first_row = lax.axis_index("wide") * my_share
    own_cols = lax.dynamic_slice_in_dim(unit_b, first_row, my_share, 0)

    def joint_tile(state_now, inputs):
        tile_b, pot_part, lse_part = inputs
        cost = cost_of(unit_a, tile_b)
        weights = jnp.exp((row_pot[:, None] - cost) / EPS - lse_part[None, :]).astype(jnp.bfloat16)
        return (row_update(state_now, pot_part, cost), left_product(weights, unit_a))

    row_stats, tile_sums = lax.scan(
        joint_tile,
        row_init,
        (b_tiles, potential_b.reshape(n_tiles, col_span), lse_b.reshape(n_tiles, col_span)),
    )
    lse_a = finish_rows(*row_stats)
    sums_b = lax.psum_scatter(
        tile_sums.reshape(n_cols, feat_width).astype(jnp.bfloat16),
        "wide",
        scatter_dimension=0,
        tiled=True,
    ).astype(jnp.float32)
    flow_b = sums_b - own_cols.astype(jnp.float32)
    potential_a = EPS * logmass_a - EPS * lse_a

    def flow_tile(acc_now, inputs):
        tile_b, pot_part = inputs
        weights = jnp.exp(
            (pot_part[None, :] - cost_of(unit_a, tile_b)) / EPS - lse_a[:, None]
        ).astype(jnp.bfloat16)
        return (acc_now + jnp.dot(weights, tile_b, preferred_element_type=jnp.float32), None)

    sums_a, _ = lax.scan(
        flow_tile,
        jnp.zeros((n_rows, feat_width), jnp.float32),
        (b_tiles, potential_b.reshape(n_tiles, col_span)),
    )
    sums_a = lax.psum(sums_a.astype(jnp.bfloat16), "narrow").astype(jnp.float32)
    flow_a = sums_a - unit_a.astype(jnp.float32)
    return (potential_a, potential_b, flow_a, flow_b)


def solution(mesh):
    return jax.shard_map(
        on_device,
        mesh=mesh,
        in_specs=(P("wide", None), P("narrow", None), P("wide"), P("narrow"), P("narrow")),
        out_specs=(P("wide"), P("narrow"), P("wide", None), P(("narrow", "wide"), None)),
        check_vma=False,
    )
```

profile of v0, /device:TPU:0, one launch (start us, length us, event | category | flops | bytes accessed | tf_op | source)
XLA Modules:
  0.0 756.5 jit_solution(1473939241529023798)
XLA Ops:
  8.1 2.7 fusion.36
  10.9 4.6 fusion.37
  15.9 22.7 %while.78 = (s32[]{:T(128)}, f32[512]{0:T(512)S(1)}, f32[512]{0:T(512)S(1)}, f32[4,2048]{1,0:T(4,128)S(1)}, bf16[4,2048,128]{2,1,0:T(8,128)(2,1)S(1)}, /*index=5*/bf16[512,128]{1,0:T(8,128)(2,1)S(1)}, s32[]{:T(128)}, s32[]{:T(128)}) while((s32[]{:T(128)}, f32[512]{0:T(512)S(1)}, f32[512]{0:T(512)S(1)}, f32[4,2048]{1,0:T(4,128)S(1)}, ...), condition=%wide.region_5.6_spmd.clone, body=%wide.region_2.5_spmd.clone.sunk | while | flops 275778048 | bytes 9095272 | solution.py:73
  15.9 2.8 fusion.83
  18.7 2.8 exponential_reduce_fusion.12
  21.6 2.8 fusion.83
  24.4 2.8 exponential_reduce_fusion.12
  27.3 2.8 fusion.83
  30.1 2.8 exponential_reduce_fusion.12
  32.9 2.8 fusion.83
  35.7 2.8 exponential_reduce_fusion.12
  38.6 10.6 %pmax.35 = f32[512]{0:T(512)S(1)} all-reduce(f32[512]{0:T(512)S(1)} %get-tuple-element.217), channel_id=1, replica_groups=mesh['wide'=32,'narrow'=4] {'narrow'}, use_global_device_ids=true, to_apply=%region_6.7 | all-reduce | flops 512 | bytes 4096 | tf_op jit(solution)/shard_map/pmax | solution.py:32
  49.2 7.7 %psum.42 = f32[512]{0:T(512)S(1)} all-reduce(f32[512]{0:T(512)S(1)} %exponential_multiply_fusion.2), channel_id=1, replica_groups=mesh['wide'=32,'narrow'=4] {'narrow'}, use_global_device_ids=true, to_apply=%region_7.8 | all-reduce | flops 512 | bytes 4096 | tf_op jit(solution)/shard_map/psum | solution.py:33
  57.0 7.3 while.76
  57.0 0.9 fusion.79
  58.8 0.9 fusion.79
  60.6 0.9 fusion.79
  62.4 0.9 fusion.79
  64.3 126.0 %pmax.36 = bf16[8192]{0:T(1024)(128)(2,1)S(1)} all-reduce(bf16[8192]{0:T(1024)(128)(2,1)S(1)} %convert_element_type.67), channel_id=1, replica_groups=mesh['wide'=32,'narrow'=4] {'wide'}, use_global_device_ids=true, to_apply=%region_12.13 | all-reduce | flops 8192 | bytes 32768 | tf_op jit(solution)/shard_map/pmax | solution.py:39
  190.3 123.8 %psum.43 = bf16[8192]{0:T(1024)(128)(2,1)S(1)} all-reduce(bf16[8192]{0:T(1024)(128)(2,1)S(1)} %fusion.42), channel_id=1, replica_groups=mesh['wide'=32,'narrow'=4] {'wide'}, use_global_device_ids=true, to_apply=%region_13.14 | all-reduce | flops 8192 | bytes 32768 | tf_op jit(solution)/shard_map/psum | solution.py:40
  314.1 22.7 %while.79 = (s32[]{:T(128)}, f32[512]{0:T(512)S(1)}, f32[512]{0:T(512)S(1)}, f32[4,2048]{1,0:T(4,128)S(1)}, bf16[4,2048,128]{2,1,0:T(8,128)(2,1)S(1)}, /*index=5*/bf16[512,128]{1,0:T(8,128)(2,1)S(1)}, s32[]{:T(128)}, s32[]{:T(128)}) while((s32[]{:T(128)}, f32[512]{0:T(512)S(1)}, f32[512]{0:T(512)S(1)}, ...), condition=%wide.region_17.18_spmd.clone, body=%wide.region_14.17_spmd.clone.sunk | while | flops 275778048 | bytes 9095272 | solution.py:73
  314.2 2.8 fusion.86
  317.0 2.8 exponential_reduce_fusion.13
  319.8 2.8 fusion.86
  322.6 2.8 exponential_reduce_fusion.13
  325.5 2.8 fusion.86
  328.3 2.8 exponential_reduce_fusion.13
  331.2 2.8 fusion.86
  334.0 2.8 exponential_reduce_fusion.13
  336.8 9.8 %pmax.37 = f32[512]{0:T(512)S(1)} all-reduce(f32[512]{0:T(512)S(1)} %get-tuple-element.221), channel_id=1, replica_groups=mesh['wide'=32,'narrow'=4] {'narrow'}, use_global_device_ids=true, to_apply=%region_18.19 | all-reduce | flops 512 | bytes 4096 | tf_op jit(solution)/shard_map/pmax | solution.py:32
  346.6 7.7 %psum.44 = f32[512]{0:T(512)S(1)} all-reduce(f32[512]{0:T(512)S(1)} %exponential_multiply_fusion.1), channel_id=1, replica_groups=mesh['wide'=32,'narrow'=4] {'narrow'}, use_global_device_ids=true, to_apply=%region_19.20 | all-reduce | flops 512 | bytes 4096 | tf_op jit(solution)/shard_map/psum | solution.py:33
  354.4 7.3 while.77
  354.4 0.9 fusion.81
  356.2 0.9 fusion.81
  358.0 0.9 fusion.81
  359.8 0.9 fusion.81
  360.7 0.6 exponential_reduce_fusion.11
  361.7 123.8 %pmax.38 = bf16[8192]{0:T(1024)(128)(2,1)S(1)} all-reduce(bf16[8192]{0:T(1024)(128)(2,1)S(1)} %convert_element_type.71), channel_id=1, replica_groups=mesh['wide'=32,'narrow'=4] {'wide'}, use_global_device_ids=true, to_apply=%region_24.25 | all-reduce | flops 8192 | bytes 32768 | tf_op jit(solution)/shard_map/pmax | solution.py:39
  485.5 124.0 %psum.45 = bf16[8192]{0:T(1024)(128)(2,1)S(1)} all-reduce(bf16[8192]{0:T(1024)(128)(2,1)S(1)} %fusion.47), channel_id=1, replica_groups=mesh['wide'=32,'narrow'=4] {'wide'}, use_global_device_ids=true, to_apply=%region_25.26 | all-reduce | flops 8192 | bytes 32768 | tf_op jit(solution)/shard_map/psum | solution.py:40
  610.2 32.9 %while.80 = (s32[]{:T(128)}, f32[512]{0:T(512)S(1)}, f32[512]{0:T(512)S(1)}, bf16[4,2048,128]{2,1,0:T(8,128)(2,1)}, f32[4,2048]{1,0:T(4,128)S(1)}, /*index=5*/bf...) while((s32[]{:T(128)}, f32[512]{0:T(512)S(1)}, ...), condition=%wide.region_29.30_spmd.clone, body=%wide.region_26.29_spmd.clone.sunk | while | flops 554699264 | bytes 31281820 | solution.py:100
  610.2 2.7 fusion.90
  612.9 3.1 exponential_reduce_fusion.14
  616.4 2.0 fusion.92
  618.4 2.7 fusion.90
  621.1 3.1 exponential_reduce_fusion.14
  624.6 2.1 fusion.92
  626.7 2.7 fusion.90
  629.4 3.1 exponential_reduce_fusion.14
  632.8 2.1 fusion.92
  634.9 2.7 fusion.90
  637.6 3.1 exponential_reduce_fusion.14
  641.1 2.1 fusion.92
  643.1 9.7 %pmax.39 = f32[512]{0:T(512)S(1)} all-reduce(f32[512]{0:T(512)S(1)} %get-tuple-element.225), channel_id=1, replica_groups=mesh['wide'=32,'narrow'=4] {'narrow'}, use_global_device_ids=true, to_apply=%region_30.31 | all-reduce | flops 512 | bytes 4096 | tf_op jit(solution)/shard_map/pmax | solution.py:32
  652.8 7.7 %psum.46 = f32[512]{0:T(512)S(1)} all-reduce(f32[512]{0:T(512)S(1)} %exponential_multiply_fusion), channel_id=1, replica_groups=mesh['wide'=32,'narrow'=4] {'narrow'}, use_global_device_ids=true, to_apply=%region_31.32 | all-reduce | flops 512 | bytes 4096 | tf_op jit(solution)/shard_map/psum | solution.py:33
  661.2 7.0 while.81
  661.2 1.7 fusion.96
  662.9 1.7 fusion.96
  664.7 1.7 fusion.96
  666.5 1.7 fusion.96
  668.2 0.7 convert_element_type.75
  669.5 35.9 %all-reduce.2.cloned.1.call-done = bf16[512,128]{1,0:T(8,128)(2,1)} async-done(((bf16[512,128]{1,0:T(8,128)(2,1)}), bf16[512,128]{1,0:T(8,128)(2,1)}) %all-reduce.2.cloned.1.call-update) | async-done | bytes 131088 | tf_op jit(solution)/shard_map/psum | solution.py:127
  705.4 1.7 convert_subtract_fusion
  707.2 40.3 %reduce-scatter.2.cloned.1.call-done = bf16[256,128]{1,0:T(8,128)(2,1)} async-done(((bf16[8192,128]{1,0:T(8,128)(2,1)}), bf16[256,128]{1,0:T(8,128)(2,1)}) %reduce-scatter.2.cloned.1.call-update) | async-done | bytes 65552 | tf_op jit(solution)/shard_map/reduce_scatter | solution.py:106
  747.5 1.5 convert_subtract_fusion.1
  (133 shorter events, 10.9 us)
Async XLA Ops:
  8.0 7.5 copy-start.1
  8.0 7.9 %copy-start.4 = (f32[8192]{0:T(1024)S(1)}, f32[8192]{0:T(1024)}, u32[]{:S(2)}) copy-start(f32[8192]{0:T(1024)} %param.21) | copy-start | bytes 98308
  8.0 697.4 %all-reduce.2.cloned.1.call-start = ((), (), s32[]{:S(2)}) async-start(), calls=%async_computation.1 | async-start | bytes 262144 | tf_op jit(solution)/shard_map/psum | solution.py:127
  15.9 41.0 %copy-start.5 = (f32[512]{0:T(512)S(1)}, f32[512]{0:T(512)}, u32[]{:S(2)}) copy-start(f32[512]{0:T(512)} %param.19) | copy-start | bytes 6148
  56.9 257.1 %copy-start.2 = (f32[8192]{0:T(1024)S(1)}, f32[8192]{0:T(1024)}, u32[]{:S(2)}) copy-start(f32[8192]{0:T(1024)} %param.20) | copy-start | bytes 98308
  609.5 0.6 copy-start.3
  612.9 3.4 copy-start
  621.1 3.4 copy-start
  629.4 3.4 copy-start
  637.6 3.4 copy-start
  668.9 78.6 %reduce-scatter.2.cloned.1.call-start = ((), (), s32[]{:S(2)}) async-start(), calls=%async_computation.2 | async-start | bytes 2162688 | tf_op jit(solution)/shard_map/reduce_scatter | solution.py:106
Sparse Core Ops, SparseCore 0:
  669.0 36.3 all-reduce.1
Sparse Core Ops, SparseCore 1:
  673.3 74.1 reduce-scatter.1
where the time goes:
time: 757 us; the launch traced here: 756 us
  blocking collectives  551 us (73%)
  waiting for transfers between devices  76.8 us (10%)
  matrix products  55.3 us (7%)
  other arithmetic  52.5 us (7%)
  between operations  15.8 us (2%)
    pmax x2, blocking collectives, finish_cols(): lax.pmax(highest.astype(jnp.bfloat16), 'wide').astype(highest.dtype)  250 us
    psum x2, blocking collectives, finish_cols(): lax.psum((summed * jnp.exp(highest - overall)).astype(jnp.bfloat16), 'wide')  248 us
    reduce_scatter x1, waiting for transfers between devices, on_device(): lax.psum_scatter(tile_sums.reshape(n_cols, feat_width).astype(jnp.bfloat1...  40.3 us
    dot_general x20, matrix products, cost_of(): lax.dot_general(left, right, (((1,), (1,)), ((), ())), preferred_element_...  40.2 us
    psum x1, waiting for transfers between devices, on_device(): sums_a = lax.psum(sums_a.astype(jnp.bfloat16), 'narrow').astype(jnp.float32)  35.9 us
    reduce_sum x12, other arithmetic, row_update(): jnp.sum(jnp.exp(scores - new_high[:, None]), axis=1)  34.8 us
    pmax x3, blocking collectives, finish_rows(): overall = lax.pmax(highest, 'narrow')  30.1 us
    psum x3, blocking collectives, finish_rows(): summed = lax.psum(summed * jnp.exp(highest - overall), 'narrow')  23.2 us
  transfers between devices with their start and end apart: 2, of which 2 were waited for; matrix products, arithmetic and copies ran while one was open for 0% of the time, Pallas kernels for 0%

commit v1 on v0

v1 whole, which is shorter than its diff:
```python
import functools
import math

import jax
import jax.numpy as jnp
from jax import lax
from jax.experimental import pallas as pl
from jax.experimental.pallas import tpu as pltpu
from jax.sharding import Mesh, PartitionSpec as P

EPS = 0.05
LOG2E = math.log2(math.e)
C2 = LOG2E / EPS
TOP = 50.0
DIM = 128
F32 = jnp.float32
BF16 = jnp.bfloat16


NR = 1024
NC = 4096
CH = 256
NK = NC // CH
NPEER = 8
NZY = 16


def nt(left, right):
    return lax.dot_general(left, right, (((1,), (1,)), ((), ())), preferred_element_type=F32)


def nn(left, right):
    return lax.dot_general(left, right, (((1,), (0,)), ((), ())), preferred_element_type=F32)


def split_rows(vec, rows_ref):
    high = vec.astype(BF16).astype(F32)
    low = vec - high
    for r in range(vec.shape[0]):
        rows_ref[0:1, r * 128 : (r + 1) * 128] = high[r : r + 1, :]
        rows_ref[1:2, r * 128 : (r + 1) * 128] = low[r : r + 1, :]


def combine(parts_ref, count, rows):
    shifts = [parts_ref[d, rows : rows + 8, :] for d in range(count)]
    top = functools.reduce(jnp.maximum, shifts)
    total = None
    for d in range(count):
        half = jnp.exp2(0.5 * (shifts[d][0:1, :] - top[0:1, :]))
        term = parts_ref[d, 0:rows, :] * half * half
        total = term if total is None else total + term
    return total, top


def pick_cols(ref, core, out_ref):
    for k in range(NK):
        first = ref[4 * k : 4 * k + 2, :]
        second = ref[4 * k + 2 : 4 * k + 4, :]
        out_ref[2 * k : 2 * k + 2, :] = jnp.where(core == 0, first, second)


def send_all(msg_ref, count, sums, shift):
    rows = sums.shape[0]
    for d in range(count):
        msg_ref[d, 0:rows, :] = sums
        msg_ref[d, rows : rows + 8, :] = jnp.broadcast_to(shift, (8, 128))


def unit_t(raw):
    norm = jnp.sqrt(jnp.sum(raw * raw, axis=0, keepdims=True) + 1e-06)
    return (raw / norm).astype(BF16)


def first_kernel(place, desc_a, other_a, desc_b, g_all, lb_all,
                 k_out, at_out, bt_out, lb_out, msg,
                 a_unit, b_raw, vec, rows, acc, sems):
    core = place[0]
    for k in range(NK):
        pltpu.make_async_copy(desc_b.at[k, core], b_raw.at[k], sems.at[k]).start()
    for half, src in ((core, desc_a), (1 - core, other_a)):
        for m in range(2):
            raw_t = src[m * 256 : (m + 1) * 256, :].astype(F32).T
            unit = unit_t(raw_t)
            at = pl.multiple_of(half * 512 + m * 256, 256)
            at_out[:, pl.ds(at, 256)] = unit
            a_unit[pl.ds(at, 256), :] = unit.astype(F32).T.astype(BF16)
    pick_cols(lb_all, core, lb_out)
    pick_cols(g_all, core, vec)
    pot = vec[...] * C2
    shift = jnp.max(jnp.max(pot, axis=0, keepdims=True), axis=1, keepdims=True)
    rows[...] = jnp.zeros_like(rows)
    split_rows(jnp.exp2(pot - shift + TOP), rows)
    acc[...] = jnp.zeros_like(acc)

    def chunk(k, carry):
        pltpu.make_async_copy(desc_b.at[k, core], b_raw.at[k], sems.at[k]).wait()
        at = pl.multiple_of(k * CH, CH)
        bt = unit_t(b_raw[k].astype(F32).T)
        bt_out[:, pl.ds(at, CH)] = bt
        lhs = rows[:, pl.ds(at, CH)].astype(BF16)
        for m in range(NR // 256):
            span = slice(m * 256, (m + 1) * 256)
            cos = nn(a_unit[span, :], bt)
            kb = jnp.exp2(cos * (2.0 * C2)).astype(BF16)
            k_out[span, pl.ds(at, CH)] = kb
            acc[:, span] += nt(lhs, kb)
        return carry

    lax.fori_loop(0, NK, chunk, 0)
    sums = jnp.concatenate(
        [acc[0:1, r * 128 : (r + 1) * 128] + acc[1:2, r * 128 : (r + 1) * 128] for r in range(8)], axis=0
    )
    send_all(msg, NPEER, sums, shift)


def row_scales(parts, la, rows):
    total, top = combine(parts, NPEER, 8)
    level = la[...] * LOG2E - jnp.log2(total)
    shift = jnp.max(jnp.max(level, axis=0, keepdims=True), axis=1, keepdims=True)
    rows[...] = jnp.zeros_like(rows)
    split_rows(jnp.exp2(level - shift + TOP), rows)
    return shift, top


def col_kernel(parts, la, k_mat, base, msg, base_out, rows, vec):
    shift, top = row_scales(parts, la, rows)
    base_out[...] = base[...] + top

    def chunk(k, carry):
        at = pl.multiple_of(k * 512, 512)
        part = nn(rows[...].astype(BF16), k_mat[:, pl.ds(at, 512)])
        part = part[0:1, :] + part[1:2, :]
        for r in range(4):
            vec[pl.ds(k * 4 + r, 1), :] = part[:, r * 128 : (r + 1) * 128]
        return carry

    lax.fori_loop(0, NC // 512, chunk, 0)
    send_all(msg, NZY, vec[...], shift)


def col_flow_kernel(parts, la, k_mat, base, a_t, msg, sums_out, base_out, rows, vec, lhs):
    shift, top = row_scales(parts, la, rows)
    base_out[...] = base[...] + top
    scale = rows[0:1, :] + rows[1:2, :]
    lhs[0:128, :] = (a_t[...].astype(F32) * scale).astype(BF16)
    lhs[128:144, :] = rows[...].astype(BF16)

    def chunk(k, carry):
        at = pl.multiple_of(k * CH, CH)
        part = nn(lhs[...], k_mat[:, pl.ds(at, CH)])
        sums_out[k] = part[0:128, :].astype(BF16)
        total = part[128:129, :] + part[129:130, :]
        for r in range(2):
            vec[pl.ds(k * 2 + r, 1), :] = total[:, r * 128 : (r + 1) * 128]
        return carry

    lax.fori_loop(0, NK, chunk, 0)
    send_all(msg, NZY, vec[...], shift)


def col_scales(parts, lb, rows):
    total, top = combine(parts, NZY, 32)
    log_total = jnp.log2(total)
    level = lb[...] * LOG2E - log_total
    shift = jnp.max(jnp.max(level, axis=0, keepdims=True), axis=1, keepdims=True)
    shift = jnp.ceil(shift)
    rows[...] = jnp.zeros_like(rows)
    split_rows(jnp.exp2(level - shift + TOP), rows)
    return level, total, shift, top


def row_kernel(parts, lb, k_mat, base, msg, base_out, rows, acc):
    level, total, shift, top = col_scales(parts, lb, rows)
    base_out[...] = base[...] - top
    acc[...] = jnp.zeros_like(acc)

    def chunk(k, carry):
        at = pl.multiple_of(k * 512, 512)
        lhs = rows[:, pl.ds(at, 512)].astype(BF16)
        acc[...] += nt(lhs, k_mat[:, pl.ds(at, 512)])
        return carry

    lax.fori_loop(0, NC // 512, chunk, 0)
    sums = jnp.concatenate(
        [acc[0:1, r * 128 : (r + 1) * 128] + acc[1:2, r * 128 : (r + 1) * 128] for r in range(8)], axis=0
    )
    send_all(msg, NPEER, sums, shift)


def pack_rows(out_ref, flow, total, shift):
    n = flow.shape[1]
    out_ref[0:128, :] = flow.astype(BF16)
    high = total.astype(BF16).astype(F32)
    kind = lax.broadcasted_iota(jnp.int32, (16, n), 0)
    tail = jnp.where(kind == 0, high, jnp.where(kind == 1, total - high, jnp.where(kind == 2, shift, 0.0)))
    out_ref[128:144, :] = tail.astype(BF16)


def row_flow_kernel(place, parts, lb, k_mat, base, b_t, own_out, other_out, pot_out, total_out, base_out, rows, lhs, acc):
    core = place[0]
    level, total, shift, top = col_scales(parts, lb, rows)
    level_base = base[...] - top
    base_out[...] = level_base
    pot_out[...] = (level + level_base[0:1, :]) * (1.0 / C2)
    total_out[...] = total
    scale = rows[0:1, :] + rows[1:2, :]
    lhs[0:128, :] = (b_t[...].astype(F32) * scale).astype(BF16)
    lhs[128:144, :] = rows[...].astype(BF16)
    acc[...] = jnp.zeros_like(acc)

    def chunk(k, carry):
        at = pl.multiple_of(k * 512, 512)
        acc[...] += nt(lhs[:, pl.ds(at, 512)], k_mat[:, pl.ds(at, 512)])
        return carry

    lax.fori_loop(0, NC // 512, chunk, 0)
    for half, out in ((core, own_out), (1 - core, other_out)):
        part = acc[:, pl.ds(pl.multiple_of(half * 512, 512), 512)]
        pack_rows(out, part[0:128, :], part[128:129, :] + part[129:130, :], shift)


def pair_sum(terms):
    while len(terms) > 1:
        terms = [terms[i] + terms[i + 1] for i in range(0, len(terms), 2)]
    return terms[0]


def merge(parts):
    tails = [p[128:144, :].astype(F32) for p in parts]
    shifts = [t[2:3, :] for t in tails]
    top = functools.reduce(jnp.maximum, shifts)
    flows, totals = [], []
    for p, t, s in zip(parts, tails, shifts):
        half = jnp.exp2(0.5 * (s - top))
        flows.append(p[0:128, :].astype(F32) * half * half)
        totals.append((t[0:1, :] + t[1:2, :]) * half * half)
    return pair_sum(flows), pair_sum(totals), top


def merge_kernel(own, received, out):
    flow, total, top = merge([own, received])
    pack_rows(out, flow, total, top)


def final_a_kernel(p0, p1, p2, p3, desc_a, la, base, flow_out, pot_out):
    flow, total, top = merge([p0, p2, p1, p3])
    flow_t = flow / total
    level = jnp.log2(total) + (top - TOP - 2.0 * C2)
    for r in range(4):
        here = slice(r * 128, (r + 1) * 128)
        unit = unit_t(desc_a[here, :].astype(F32).T).astype(F32)
        flow_out[here, :] = (flow_t[:, here] - unit).T
        pot_out[r : r + 1, :] = (la[r : r + 1, :] * LOG2E - level[:, here] - base[0:1, :]) * (1.0 / C2)


def final_b_kernel(place, sums, parts, total, b_t, own_pot, other_pot, flow_out, pot_out):
    core = place[0]
    chunk = place[1]
    shifts = [parts[d, 32:40, :] for d in range(NZY)]
    top = functools.reduce(jnp.maximum, shifts)
    acc = 0.0
    for d in range(NZY):
        half = jnp.exp2(0.5 * (shifts[d][0:1, 0:1] - top[0:1, 0:1]))
        acc = acc + sums[d].astype(F32) * half * half
    at = pl.multiple_of(chunk * CH, CH)
    unit = b_t[:, pl.ds(at, CH)].astype(F32)
    for r in range(2):
        here = slice(r * 128, (r + 1) * 128)
        denom = total[pl.ds(chunk * 2 + r, 1), :]
        flow_out[here, :] = (acc[:, here] / denom - unit[:, here]).T
    for k in range(NK):
        mine = own_pot[2 * k : 2 * k + 2, :]
        theirs = other_pot[2 * k : 2 * k + 2, :]
        pot_out[4 * k : 4 * k + 2, :] = jnp.where(core == 0, mine, theirs)
        pot_out[4 * k + 2 : 4 * k + 4, :] = jnp.where(core == 0, theirs, mine)


def sds(*shape, dtype=F32):
    return jax.ShapeDtypeStruct(shape, dtype)


VM = pl.BlockSpec(memory_space=pltpu.VMEM)
SM = pl.BlockSpec(memory_space=pltpu.SMEM)
ANY = pl.BlockSpec(memory_space=pl.ANY)


def call(kernel, ins, outs, scratch, flops=0, bytes_accessed=0, trans=0):
    return pl.pallas_call(
        kernel,
        in_specs=ins,
        out_specs=[VM] * len(outs),
        out_shape=outs,
        scratch_shapes=scratch,
        compiler_params=pltpu.CompilerParams(vmem_limit_bytes=40 * 1024 * 1024),
        cost_estimate=pl.CostEstimate(flops=flops, bytes_accessed=bytes_accessed, transcendentals=trans),
    )


PASS = NR * NC


def on_device(desc_a, desc_b, logmass_a, logmass_b, g_start):
    core = lax.axis_index("core")
    place = jnp.stack([core, lax.axis_index("zy")]).astype(jnp.int32)
    swap = [(0, 1), (1, 0)]
    la_own = logmass_a.reshape(4, 128)
    other_a = lax.ppermute(desc_a, "core", swap)
    la_other = lax.ppermute(la_own, "core", swap)
    la = jnp.where(
        core == 0,
        jnp.concatenate([la_own, la_other], axis=0),
        jnp.concatenate([la_other, la_own], axis=0),
    )
    k_mat, a_t, b_t, lb, msg = call(
        first_kernel,
        [SM, VM, VM, ANY, VM, VM],
        [pltpu.VMEM((NR, NC), BF16), sds(DIM, NR, dtype=BF16), sds(DIM, NC, dtype=BF16), sds(32, 128), sds(NPEER, 16, 128)],
        [
            pltpu.VMEM((NR, DIM), BF16),
            pltpu.VMEM((NK, CH, DIM), BF16),
            pltpu.VMEM((32, 128), F32),
            pltpu.VMEM((16, NC), F32),
            pltpu.VMEM((16, NR), F32),
            pltpu.SemaphoreType.DMA((NK,)),
        ],
        flops=2 * PASS * DIM,
        trans=PASS,
    )(place, desc_a, other_a, desc_b.reshape(NK, 2, CH, DIM), g_start.reshape(64, 128), logmass_b.reshape(64, 128))
    keep = lambda x: pltpu.with_memory_space_constraint(x, pltpu.VMEM)

    parts = lax.all_to_all(msg, ("core", "x"), 0, 0)
    base = jnp.zeros((8, 128), F32)
    msg, base = call(
        col_kernel,
        [VM] * 4,
        [sds(NZY, 40, 128), sds(8, 128)],
        [pltpu.VMEM((16, NR), F32), pltpu.VMEM((32, 128), F32)],
        flops=2 * PASS * 16,
    )(parts, la, keep(k_mat), base)

    parts = lax.all_to_all(msg, "zy", 0, 0)
    msg, base = call(
        row_kernel,
        [VM] * 4,
        [sds(NPEER, 16, 128), sds(8, 128)],
        [pltpu.VMEM((16, NC), F32), pltpu.VMEM((16, NR), F32)],
        flops=2 * PASS * 16,
    )(parts, lb, keep(k_mat), base)

    parts = lax.all_to_all(msg, ("core", "x"), 0, 0)
    msg, sums, base = call(
        col_flow_kernel,
        [VM] * 5,
        [sds(NZY, 40, 128), sds(NZY, DIM, CH, dtype=BF16), sds(8, 128)],
        [pltpu.VMEM((16, NR), F32), pltpu.VMEM((32, 128), F32), pltpu.VMEM((144, NR), BF16)],
        flops=2 * PASS * 144,
    )(parts, la, keep(k_mat), base, a_t)

    parts = lax.all_to_all(msg, "zy", 0, 0)
    sums = lax.all_to_all(sums, "zy", 0, 0)
    own, other, own_pot, total, base = call(
        row_flow_kernel,
        [SM] + [VM] * 5,
        [sds(144, 512, dtype=BF16), sds(144, 512, dtype=BF16), sds(32, 128), sds(32, 128), sds(8, 128)],
        [pltpu.VMEM((16, NC), F32), pltpu.VMEM((144, NC), BF16), pltpu.VMEM((144, NR), F32)],
        flops=2 * PASS * 144,
    )(place, parts, lb, keep(k_mat), base, b_t)

    received = lax.ppermute(other, "core", swap)
    other_pot = lax.ppermute(own_pot, "core", swap)
    mine = call(merge_kernel, [VM] * 2, [sds(144, 512, dtype=BF16)], [])(own, received)[0]
    others = [lax.ppermute(mine, "x", [(i, (i + s) % 4) for i in range(4)]) for s in (1, 2, 3)]
    flow_a, pot_a = call(
        final_a_kernel, [VM] * 7, [sds(512, DIM), sds(4, 128)], []
    )(mine, *others, desc_a, la_own, base)
    flow_b, pot_b = call(
        final_b_kernel, [SM] + [VM] * 6, [sds(CH, DIM), sds(64, 128)], []
    )(place, sums, parts, total, b_t, own_pot, other_pot)
    return (pot_a.reshape(512), pot_b.reshape(8192), flow_a, flow_b)


def solution(mesh):
    fine = Mesh(mesh.devices.reshape(NZY, 2, 4), ("zy", "core", "x"))
    wide = ("zy", "core")
    return jax.shard_map(
        on_device,
        mesh=fine,
        in_specs=(P(wide, None), P("x", None), P(wide), P("x"), P("x")),
        out_specs=(P(wide), P("x"), P(wide, None), P(("x", "zy", "core"), None)),
        check_vma=False,
    )
```

time: 757 us -> 114 us (0.15)
  blocking collectives: 551 us -> 37.9 us
  waiting for transfers between devices: 76.8 us -> 15.4 us
  matrix products: 55.3 us -> 0 us
  other arithmetic: 52.5 us -> 0.85 us
  Pallas kernels: 0 us -> 32.5 us
  between operations: 15.8 us -> 0.73 us
  starting transfers between devices: 0.08 us -> 11.6 us
  local copies, waits for them, and re-layouts: 4.42 us -> 14 us
    pmax x5 -> x0, blocking collectives: 280 us -> none  [the longest x2 250 us: finish_cols(): lax.pmax(highest.astype(jnp.bfloat16), 'wide').astype(highest.dtype)]
    psum x5 -> x0, blocking collectives: 271 us -> none  [the longest x2 248 us: finish_cols(): lax.psum((summed * jnp.exp(highest - overall)).astype(jnp.bfloat16), 'wide')]
    dot_general x28 -> x0, matrix products: 55.3 us -> none  [the longest x20 40.2 us: cost_of(): lax.dot_general(left, right, (((1,), (1,)), ((), ())), preferred_element_...]
    reduce_sum x22 -> x0, other arithmetic: 42.8 us -> none  [the longest x12 34.8 us: row_update(): jnp.sum(jnp.exp(scores - new_high[:, None]), axis=1)]
    reduce_scatter x1 -> x0, waiting for transfers between devices: 40.3 us -> none  [on_device(): lax.psum_scatter(tile_sums.reshape(n_cols, feat_width).astype(jnp.bfloat1...]
    all_to_all x0 -> x3, blocking collectives: none -> 37.9 us  [the longest x2 30.2 us: on_device(): parts = lax.all_to_all(msg, 'zy', 0, 0)]
    psum x1 -> x0, waiting for transfers between devices: 35.9 us -> none  [on_device(): sums_a = lax.psum(sums_a.astype(jnp.bfloat16), 'narrow').astype(jnp.float32)]
    pallas_call x0 -> x8, Pallas kernels: none -> 32.5 us  [the longest x1 13.7 us: on_device(): call(first_kernel, [SM, VM, VM, ANY, VM, VM], [pltpu.VMEM((NR, NC), BF16)...]
  transfers between devices with their start and end apart: 2 -> 9, of which waited for: 2 -> 6; matrix products, arithmetic and copies ran while one was open for 0% -> 1% of each run, Pallas kernels for 0% -> 18%
where the time goes in v1:
time: 114 us; the launch traced here: 113 us
  blocking collectives  37.9 us (33%)
  Pallas kernels  32.5 us (29%)
  waiting for transfers between devices  15.4 us (14%)
  local copies, waits for them, and re-layouts  14 us (12%)
  starting transfers between devices  11.6 us (10%)
    all_to_all x2, blocking collectives, on_device(): parts = lax.all_to_all(msg, 'zy', 0, 0)  30.2 us
    unnamed x18, local copies, waits for them, and re-layouts  14 us
    pallas_call x1, Pallas kernels, on_device(): call(first_kernel, [SM, VM, VM, ANY, VM, VM], [pltpu.VMEM((NR, NC), BF16)...  13.7 us
    ppermute x3, waiting for transfers between devices, on_device(): lax.ppermute(mine, 'x', [(i, (i + s) % 4) for i in range(4)])  8.52 us
    all_to_all x1, blocking collectives, on_device(): parts = lax.all_to_all(msg, ('core', 'x'), 0, 0)  7.73 us
    pallas_call x1, Pallas kernels, on_device(): call(col_flow_kernel, [VM] * 5, [sds(NZY, 40, 128), sds(NZY, DIM, CH, dty...  5.45 us
    pallas_call x1, Pallas kernels, on_device(): call(row_flow_kernel, [SM] + [VM] * 5, [sds(144, 512, dtype=BF16), sds(14...  5.03 us
    all_to_all x1, waiting for transfers between devices, on_device(): parts = lax.all_to_all(msg, ('core', 'x'), 0, 0)  4.58 us
  transfers between devices with their start and end apart: 9, of which 6 were waited for; matrix products, arithmetic and copies ran while one was open for 1% of the time, Pallas kernels for 18%

profile of v1, /device:TPU:0, one launch (start us, length us, event | category | flops | bytes accessed | tf_op | source)
XLA Modules:
  0.0 113.0 jit_solution(18076787866535748438)
XLA Ops:
  0.6 0.1 collective-permute-start
  0.7 0.5 collective-permute-start.1
  1.2 0.1 pad_add_fusion.place
  1.3 1.0 collective-permute-done.other_a
  2.3 0.0 copy-start.3
  2.3 0.9 copy-done.3
  3.2 0.0 copy-start.6
  3.2 1.6 %copy-done.6 = bf16[8192,128]{1,0:T(8,128)(2,1)S(1)} copy-done((bf16[8192,128]{1,0:T(8,128)(2,1)S(1)}, bf16[8192,128]{1,0:T(8,128)(2,1)}, u32[]{:S(2)}) %copy-start.6) | copy-done | bytes 2097176
  4.8 0.0 copy-start.7
  4.8 0.8 copy-done.7
  5.5 0.0 copy-start.8
  5.5 0.8 copy-done.8
  6.3 13.7 %shard_map.84 = (bf16[1024,4096]{1,0:T(8,128)(2,1)S(1)}, bf16[128,1024]{1,0:T(8,128)(2,1)S(1)}, bf16[128,4096]{1,0:T(8,128)(2,1)S(1)}, f32[32,128]{1,0:T(8,128)S(1)}, f32[8,16,128]{2,1,0:T(8,128)}) custom-call(s32[2]{0:T(128)S(1)} %pad_add_fusion.place, bf16[512,128]{1,0:T(8,128)(2,1)S(1)} %copy-done.3, bf16[512,128]{1,0:T(8,128)(2,1)S(1)} %collective-permute-done.other_a, ...), custom_call_target="tpu_custom_call" | custom-call | flops 1073741824 | tf_op jit(solution)/shard_map/pallas_call | solution.py:314
  20.0 0.0 copy-start
  20.0 3.3 %copy-done = bf16[1024,4096]{1,0:T(8,128)(2,1)} copy-done((bf16[1024,4096]{1,0:T(8,128)(2,1)}, bf16[1024,4096]{1,0:T(8,128)(2,1)S(1)}, u32[]{:S(2)}) %copy-start) | copy-done | bytes 8388632
  23.3 4.4 %all-to-all-start = ((f32[8,16,128]{2,1,0:T(8,128)}), f32[8,16,128]{2,1,0:T(8,128)S(1)}, u32[]{:S(2)}, u32[]{:S(2)}) async-start(f32[8,16,128]{2,1,0:T(8,128)} %get-tuple-element.25), calls=%async_computation | async-start | bytes 131072 | tf_op jit(solution)/shard_map/all_to_all | solution.py:331
  27.7 0.0 collective-permute-done.1
  27.7 0.8 maximum_select_fusion.la
  28.5 4.6 %all-to-all-done.parts = f32[8,16,128]{2,1,0:T(8,128)S(1)} async-done(((f32[8,16,128]{2,1,0:T(8,128)}), f32[8,16,128]{2,1,0:T(8,128)S(1)}, u32[]{:S(2)}, u32[]{:S(2)}) %all-to-all-start) | async-done | bytes 65568 | tf_op jit(solution)/shard_map/all_to_all | solution.py:331
  33.1 0.0 copy-start.1
  33.1 3.4 %copy-done.1 = bf16[1024,4096]{1,0:T(8,128)(2,1)S(1)} copy-done((bf16[1024,4096]{1,0:T(8,128)(2,1)S(1)}, bf16[1024,4096]{1,0:T(8,128)(2,1)}, u32[]{:S(2)}) %copy-start.1) | copy-done | bytes 8388632
  36.4 2.2 %shard_map.85 = (f32[16,40,128]{2,1,0:T(8,128)S(1)}, f32[8,128]{1,0:T(8,128)S(1)}) custom-call(f32[8,16,128]{2,1,0:T(8,128)S(1)} %all-to-all-done.parts, f32[8,128]{1,0:T(8,128)S(1)} %maximum_select_fusion.la, bf16[1024,4096]{1,0:T(8,128)(2,1)S(1)} %copy-done.1, f32[8,128]{1,0:T(8,128)S(1)} %broadcast_in_dim.3.base), custom_call_target="tpu_custom_call" | custom-call | flops 134217728 | tf_op jit(solution)/shard_map/pallas_call | solution.py:333
  38.6 17.5 %all_to_all.25.parts = f32[16,40,128]{2,1,0:T(8,128)S(1)} all-to-all(f32[16,40,128]{2,1,0:T(8,128)S(1)} %get-tuple-element.27), channel_id=1, replica_groups=mesh['zy'=16,'core'=2,'x'=4] {'zy'}, dimensions={0} | all-to-all | bytes 655360 | tf_op jit(solution)/shard_map/all_to_all | solution.py:341
  56.1 3.3 %shard_map.86 = (f32[8,16,128]{2,1,0:T(8,128)S(1)}, f32[8,128]{1,0:T(8,128)S(1)}) custom-call(f32[16,40,128]{2,1,0:T(8,128)S(1)} %all_to_all.25.parts, f32[32,128]{1,0:T(8,128)S(1)} %get-tuple-element.28.lb, bf16[1024,4096]{1,0:T(8,128)(2,1)S(1)} %copy-done.1, f32[8,128]{1,0:T(8,128)S(1)} %get-tuple-element.29.base), custom_call_target="tpu_custom_call" | custom-call | flops 134217728 | tf_op jit(solution)/shard_map/pallas_call | solution.py:342
  59.5 7.7 %all_to_all.26.parts = f32[8,16,128]{2,1,0:T(8,128)S(1)} all-to-all(f32[8,16,128]{2,1,0:T(8,128)S(1)} %get-tuple-element.30), channel_id=1, replica_groups=mesh['zy'=16,'core'=2,'x'=4] {'core','x'}, dimensions={0} | all-to-all | bytes 131072 | tf_op jit(solution)/shard_map/all_to_all | solution.py:350
  67.2 5.4 %shard_map.87 = (f32[16,40,128]{2,1,0:T(8,128)S(1)}, bf16[16,128,256]{2,1,0:T(8,128)(2,1)}, f32[8,128]{1,0:T(8,128)S(1)}) custom-call(f32[8,16,128]{2,1,0:T(8,128)S(1)} %all_to_all.26.parts, f32[8,128]{1,0:T(8,128)S(1)} %maximum_select_fusion.la, bf16[1024,4096]{1,0:T(8,128)(2,1)S(1)} %copy-done.1, f32[8,128]{1,0:T(8,128)S(1)} %get-tuple-element.31.base, ...), custom_call_target="tpu_custom_call" | custom-call | flops 1207959552 | tf_op jit(solution)/shard_map/pallas_call | solution.py:351
  72.6 0.0 copy-start.4
  72.6 0.0 copy-start.5
  72.6 12.7 %all_to_all.27.parts = f32[16,40,128]{2,1,0:T(8,128)S(1)} all-to-all(f32[16,40,128]{2,1,0:T(8,128)S(1)} %get-tuple-element.33), channel_id=1, replica_groups=mesh['zy'=16,'core'=2,'x'=4] {'zy'}, dimensions={0} | all-to-all | bytes 655360 | tf_op jit(solution)/shard_map/all_to_all | solution.py:359
  85.3 3.7 %all-to-all-start.4 = ((bf16[16,128,256]{2,1,0:T(8,128)(2,1)}), bf16[16,128,256]{2,1,0:T(8,128)(2,1)S(1)}, u32[]{:S(2)}, u32[]{:S(2)}) async-start(bf16[16,128,256]{2,1,0:T(8,128)(2,1)} %get-tuple-element.40), calls=%async_computation.4 | async-start | bytes 2097152 | tf_op jit(solution)/shard_map/all_to_all | solution.py:360
  89.0 0.0 copy-start.2
  89.0 3.4 %copy-done.2 = bf16[1024,4096]{1,0:T(8,128)(2,1)S(1)} copy-done((bf16[1024,4096]{1,0:T(8,128)(2,1)S(1)}, bf16[1024,4096]{1,0:T(8,128)(2,1)}, u32[]{:S(2)}) %copy-start.2) | copy-done | bytes 8388632
  92.4 5.0 %shard_map.88 = (bf16[144,512]{1,0:T(8,128)(2,1)S(1)}, bf16[144,512]{1,0:T(8,128)(2,1)S(1)}, f32[32,128]{1,0:T(8,128)S(1)}, f32[32,128]{1,0:T(8,128)S(1)}, f32[8,128]{1,0:T(8,128)S(1)}) custom-call(s32[2]{0:T(128)S(1)} %pad_add_fusion.place, f32[16,40,128]{2,1,0:T(8,128)S(1)} %all_to_all.27.parts, f32[32,128]{1,0:T(8,128)S(1)} %get-tuple-element.28.lb, ...), custom_call_target="tpu_custom_call" | custom-call | flops 1207959552 | tf_op jit(solution)/shard_map/pallas_call | solution.py:361
  97.4 0.1 collective-permute-start.2
  97.5 1.4 %collective-permute-done.2.received = bf16[144,512]{1,0:T(8,128)(2,1)S(1)} collective-permute-done((bf16[144,512]{1,0:T(8,128)(2,1)S(1)}, bf16[144,512]{1,0:T(8,128)(2,1)S(1)}, u32[]{:S(2)}, u32[]{:S(2)}) %collective-permute-start.2) | collective-permute-done | bytes 147488 | tf_op jit(solution)/shard_map/ppermute | solution.py:369
  98.8 0.1 shard_map.89.p0
  98.9 1.1 collective-permute-start.5
  100.1 1.8 %collective-permute-start.4 = (bf16[144,512]{1,0:T(8,128)(2,1)S(1)}, bf16[144,512]{1,0:T(8,128)(2,1)S(1)}, u32[]{:S(2)}, u32[]{:S(2)}) collective-permute-start(bf16[144,512]{1,0:T(8,128)(2,1)S(1)} %shard_map.89.p0), channel_id=1, source_target_pairs={{0,2},{1,3},{2,0},{3,1},{4,6},{5,7},{6,4},{7,5},{8,10},{9,11},{10,... | collective-permute-start | bytes 442376 | tf_op jit(solution)/shard_map/ppermute | solution.py:372
  101.8 0.0 collective-permute-start.3
  101.8 0.0 collective-permute-start.6
  101.8 3.9 %collective-permute-done.5.p3 = bf16[144,512]{1,0:T(8,128)(2,1)S(1)} collective-permute-done((bf16[144,512]{1,0:T(8,128)(2,1)S(1)}, bf16[144,512]{1,0:T(8,128)(2,1)S(1)}, u32[]{:S(2)}, u32[]{:S(2)}) %collective-permute-start.5) | collective-permute-done | bytes 147488 | tf_op jit(solution)/shard_map/ppermute | solution.py:372
  105.7 2.6 %collective-permute-done.4.p2 = bf16[144,512]{1,0:T(8,128)(2,1)S(1)} collective-permute-done((bf16[144,512]{1,0:T(8,128)(2,1)S(1)}, bf16[144,512]{1,0:T(8,128)(2,1)S(1)}, u32[]{:S(2)}, u32[]{:S(2)}) %collective-permute-start.4) | collective-permute-done | bytes 147488 | tf_op jit(solution)/shard_map/ppermute | solution.py:372
  108.3 2.0 %collective-permute-done.3.p1 = bf16[144,512]{1,0:T(8,128)(2,1)S(1)} collective-permute-done((bf16[144,512]{1,0:T(8,128)(2,1)S(1)}, bf16[144,512]{1,0:T(8,128)(2,1)S(1)}, u32[]{:S(2)}, u32[]{:S(2)}) %collective-permute-start.3) | collective-permute-done | bytes 147488 | tf_op jit(solution)/shard_map/ppermute | solution.py:372
  110.3 0.0 copy-done.4
  110.3 0.0 copy-done.5
  110.3 1.1 shard_map.90
  111.4 0.0 collective-permute-done.6.other_pot
  111.4 0.0 all-to-all-done.4.sums
  111.4 1.6 %shard_map.91 = (f32[256,128]{1,0:T(8,128)}, f32[64,128]{1,0:T(8,128)}) custom-call(s32[2]{0:T(128)S(1)} %pad_add_fusion.place, bf16[16,128,256]{2,1,0:T(8,128)(2,1)S(1)} %all-to-all-done.4.sums, f32[16,40,128]{2,1,0:T(8,128)S(1)} %all_to_all.27.parts, f32[32,128]{1,0:T(8,128)S(1)} %get-tuple-element.41.total, bf16[128,4096]{1,0:T(8,128)(2,1)S(1)} %get-tuple-element.35.b_t, ...), custom_call_target="tpu_custom_call" | custom-call | tf_op jit(solution)/shard_map/pallas_call | solution.py:376
  (1 shorter events, 0.0 us)
Async XLA Ops:
  0.6 1.6 %collective-permute-start = (bf16[512,128]{1,0:T(8,128)(2,1)}, bf16[512,128]{1,0:T(8,128)(2,1)S(1)}, u32[]{:S(2)}, u32[]{:S(2)}) collective-permute-start(bf16[512,128]{1,0:T(8,128)(2,1)} %desc_a.3), channel_id=1, source_target_pairs={{0,4},{4,0},{1,5},{5,1},{2,6},{6,2},{3,7},{7,3},{8,12},{12,8},{9,1... | collective-permute-start | bytes 393224 | tf_op jit(solution)/shard_map/ppermute | solution.py:307
  0.7 27.0 %collective-permute-start.1 = (f32[4,128]{1,0:T(4,128)}, f32[4,128]{1,0:T(4,128)S(1)}, u32[]{:S(2)}, u32[]{:S(2)}) collective-permute-start(f32[4,128]{1,0:T(4,128)} %bitcast.8), channel_id=1, source_target_pairs={{0,4},{4,0},{1,5},{5,1},{2,6},{6,2},{3,7},{7,3},{8,12},{12,8},{9,1... | collective-permute-start | bytes 6152 | tf_op jit(solution)/shard_map/ppermute | solution.py:308
  2.3 0.9 copy-start.3
  3.2 1.6 %copy-start.6 = (bf16[8192,128]{1,0:T(8,128)(2,1)S(1)}, bf16[8192,128]{1,0:T(8,128)(2,1)}, u32[]{:S(2)}) copy-start(bf16[8192,128]{1,0:T(8,128)(2,1)} %param.6) | copy-start | bytes 6291460
  4.8 0.8 copy-start.7
  5.5 0.8 copy-start.8
  20.0 3.3 %copy-start = (bf16[1024,4096]{1,0:T(8,128)(2,1)}, bf16[1024,4096]{1,0:T(8,128)(2,1)S(1)}, u32[]{:S(2)}) copy-start(bf16[1024,4096]{1,0:T(8,128)(2,1)S(1)} %get-tuple-element.26.k_mat) | copy-start | bytes 25165828
  23.3 9.7 %all-to-all-start = ((f32[8,16,128]{2,1,0:T(8,128)}), f32[8,16,128]{2,1,0:T(8,128)S(1)}, u32[]{:S(2)}, u32[]{:S(2)}) async-start(f32[8,16,128]{2,1,0:T(8,128)} %get-tuple-element.25), calls=%async_computation | async-start | bytes 131072 | tf_op jit(solution)/shard_map/all_to_all | solution.py:331
  33.1 3.4 %copy-start.1 = (bf16[1024,4096]{1,0:T(8,128)(2,1)S(1)}, bf16[1024,4096]{1,0:T(8,128)(2,1)}, u32[]{:S(2)}) copy-start(bf16[1024,4096]{1,0:T(8,128)(2,1)} %copy-done) | copy-start | bytes 25165828
  72.6 37.7 %copy-start.4 = (bf16[512,128]{1,0:T(8,128)(2,1)S(1)}, bf16[512,128]{1,0:T(8,128)(2,1)}, u32[]{:S(2)}) copy-start(bf16[512,128]{1,0:T(8,128)(2,1)} %desc_a.3) | copy-start | bytes 393220
  72.6 37.7 %copy-start.5 = (f32[512]{0:T(512)S(1)}, f32[512]{0:T(512)}, u32[]{:S(2)}) copy-start(f32[512]{0:T(512)} %param.7) | copy-start | bytes 6148
  85.3 26.1 %all-to-all-start.4 = ((bf16[16,128,256]{2,1,0:T(8,128)(2,1)}), bf16[16,128,256]{2,1,0:T(8,128)(2,1)S(1)}, u32[]{:S(2)}, u32[]{:S(2)}) async-start(bf16[16,128,256]{2,1,0:T(8,128)(2,1)} %get-tuple-element.40), calls=%async_computation.4 | async-start | bytes 2097152 | tf_op jit(solution)/shard_map/all_to_all | solution.py:360
  89.0 3.4 %copy-start.2 = (bf16[1024,4096]{1,0:T(8,128)(2,1)S(1)}, bf16[1024,4096]{1,0:T(8,128)(2,1)}, u32[]{:S(2)}) copy-start(bf16[1024,4096]{1,0:T(8,128)(2,1)} %copy-done) | copy-start | bytes 25165828
  97.4 1.5 %collective-permute-start.2 = (bf16[144,512]{1,0:T(8,128)(2,1)S(1)}, bf16[144,512]{1,0:T(8,128)(2,1)S(1)}, u32[]{:S(2)}, u32[]{:S(2)}) collective-permute-start(bf16[144,512]{1,0:T(8,128)(2,1)S(1)} %get-tuple-element.37), channel_id=1, source_target_pairs={{0,4},{4,0},{1,5},{5,1},{2,6},{6,2},{3,7},{7,3},{8,12},{12,8},{9,1... | collective-permute-start | bytes 442376 | tf_op jit(solution)/shard_map/ppermute | solution.py:369
  98.9 6.8 %collective-permute-start.5 = (bf16[144,512]{1,0:T(8,128)(2,1)S(1)}, bf16[144,512]{1,0:T(8,128)(2,1)S(1)}, u32[]{:S(2)}, u32[]{:S(2)}) collective-permute-start(bf16[144,512]{1,0:T(8,128)(2,1)S(1)} %shard_map.89.p0), channel_id=1, source_target_pairs={{0,3},{1,0},{2,1},{3,2},{4,7},{5,4},{6,5},{7,6},{8,11},{9,8},{10,9... | collective-permute-start | bytes 442376 | tf_op jit(solution)/shard_map/ppermute | solution.py:372
  100.1 8.2 %collective-permute-start.4 = (bf16[144,512]{1,0:T(8,128)(2,1)S(1)}, bf16[144,512]{1,0:T(8,128)(2,1)S(1)}, u32[]{:S(2)}, u32[]{:S(2)}) collective-permute-start(bf16[144,512]{1,0:T(8,128)(2,1)S(1)} %shard_map.89.p0), channel_id=1, source_target_pairs={{0,2},{1,3},{2,0},{3,1},{4,6},{5,7},{6,4},{7,5},{8,10},{9,11},{10,... | collective-permute-start | bytes 442376 | tf_op jit(solution)/shard_map/ppermute | solution.py:372
  101.8 8.5 %collective-permute-start.3 = (bf16[144,512]{1,0:T(8,128)(2,1)S(1)}, bf16[144,512]{1,0:T(8,128)(2,1)S(1)}, u32[]{:S(2)}, u32[]{:S(2)}) collective-permute-start(bf16[144,512]{1,0:T(8,128)(2,1)S(1)} %shard_map.89.p0), channel_id=1, source_target_pairs={{0,1},{1,2},{2,3},{3,0},{4,5},{5,6},{6,7},{7,4},{8,9},{9,10},{10,1... | collective-permute-start | bytes 442376 | tf_op jit(solution)/shard_map/ppermute | solution.py:372
  101.8 9.6 %collective-permute-start.6 = (f32[32,128]{1,0:T(8,128)S(1)}, f32[32,128]{1,0:T(8,128)S(1)}, u32[]{:S(2)}, u32[]{:S(2)}) collective-permute-start(f32[32,128]{1,0:T(8,128)S(1)} %get-tuple-element.42.own_pot), channel_id=1, source_target_pairs={{0,4},{4,0},{1,5},{5,1},{2,6},{6,2},{3,7},{7,3},{8,12},{12,8},{9,1... | collective-permute-start | bytes 49160 | tf_op jit(solution)/shard_map/ppermute | solution.py:370

commit v2 on v1

v2 whole, which is shorter than its diff:
```python
import functools
import math

import jax
import jax.numpy as jnp
from jax import lax
from jax.experimental import pallas as pl
from jax.experimental.pallas import tpu as pltpu
from jax.sharding import Mesh, PartitionSpec as P

EPS = 0.05
LOG2E = math.log2(math.e)
C2 = LOG2E / EPS
TOP = 50.0
DIM = 128
F32 = jnp.float32
BF16 = jnp.bfloat16


NR = 1024
NC = 4096
CH = 256
NK = NC // CH
NPEER = 8
NZY = 16


def nt(left, right):
    return lax.dot_general(left, right, (((1,), (1,)), ((), ())), preferred_element_type=F32)


def nn(left, right):
    return lax.dot_general(left, right, (((1,), (0,)), ((), ())), preferred_element_type=F32)


def split_rows(vec, rows_ref):
    high = vec.astype(BF16).astype(F32)
    low = vec - high
    for r in range(vec.shape[0]):
        rows_ref[0:1, r * 128 : (r + 1) * 128] = high[r : r + 1, :]
        rows_ref[1:2, r * 128 : (r + 1) * 128] = low[r : r + 1, :]


def combine(parts_ref, count, rows):
    shifts = [parts_ref[d, rows : rows + 8, :] for d in range(count)]
    top = functools.reduce(jnp.maximum, shifts)
    total = None
    for d in range(count):
        half = jnp.exp2(0.5 * (shifts[d][0:1, :] - top[0:1, :]))
        term = parts_ref[d, 0:rows, :] * half * half
        total = term if total is None else total + term
    return total, top


def pair_sum(terms):
    while len(terms) > 1:
        terms = [terms[i] + terms[i + 1] for i in range(0, len(terms), 2)]
    return terms[0]


def pick_cols(ref, core, out_ref):
    for k in range(NK):
        first = ref[4 * k : 4 * k + 2, :]
        second = ref[4 * k + 2 : 4 * k + 4, :]
        out_ref[2 * k : 2 * k + 2, :] = jnp.where(core == 0, first, second)


def unit_t(raw):
    norm = jnp.sqrt(jnp.sum(raw * raw, axis=0, keepdims=True) + 1e-06)
    return (raw / norm).astype(BF16)


def prep_kernel(place, desc_b, g_all, lb_all, desc_a, a_out, b_out, bt_out, at_out, rows_out, shift_out, lb_out,
                b_raw, a_raw, g_raw, lb_raw, vec, rows, sems):
    core = place[0]
    copies = [
        pltpu.make_async_copy(g_all, g_raw, sems.at[NK]),
        pltpu.make_async_copy(desc_a, a_raw, sems.at[NK + 1]),
        pltpu.make_async_copy(lb_all, lb_raw, sems.at[NK + 2]),
    ]
    loads = [pltpu.make_async_copy(desc_b.at[k, core], b_raw.at[k], sems.at[k]) for k in range(NK)]
    for copy in copies + loads:
        copy.start()
    rows[...] = jnp.zeros_like(rows)
    for copy in copies:
        copy.wait()
    pick_cols(lb_raw, core, lb_out)
    pick_cols(g_raw, core, vec)
    pot = vec[...] * C2
    shift = jnp.max(jnp.max(pot, axis=0, keepdims=True), axis=1, keepdims=True)
    shift_out[...] = jnp.broadcast_to(shift, (8, 128))
    split_rows(jnp.exp2(pot - shift + TOP), rows)
    rows_out[...] = rows[...].astype(BF16)
    for m in range(2):
        span = slice(m * 256, (m + 1) * 256)
        unit = unit_t(a_raw[span, :].T.astype(F32))
        at_out[:, span] = unit
        a_out[span, :] = unit.T
    for k in range(NK):
        loads[k].wait()
        span = slice(k * CH, (k + 1) * CH)
        unit = unit_t(b_raw[k].T.astype(F32))
        bt_out[:, span] = unit
        b_out[span, :] = unit.T


def first_kernel(place, at_own, other_a, la_own, b_unit, rows, shift, kt_out, at_out, a_out, msg):
    core = place[0]
    for m in range(2):
        span = slice(m * 256, (m + 1) * 256)
        for half, unit in ((core, at_own[:, span]), (1 - core, unit_t(other_a[span, :].T.astype(F32)))):
            at = pl.multiple_of(half * 512 + m * 256, 256)
            at_out[:, pl.ds(at, 256)] = unit
            a_out[pl.ds(at, 256), :] = unit.T
    msg[16:20, :] = la_own[...]
    msg[20:24, :] = la_own[...]

    def block(j, carry):
        at = pl.multiple_of(j * 2048, 2048)
        for q in range(4):
            left = b_unit[pl.ds(at + q * 512, 512), :]
            for m in range(NR // 256):
                span = slice(m * 256, (m + 1) * 256)
                kt_out[pl.ds(at + q * 512, 512), span] = jnp.exp2(nn(left, at_out[:, span]) * (2.0 * C2)).astype(BF16)
        return carry

    lax.fori_loop(0, NC // 2048, block, 0)
    put_rows(msg, nn(rows[...], kt_out[...]), shift[0:1, :])


def put_rows(msg, part, shift):
    part = part[0:1, :] + part[1:2, :]
    for r in range(8):
        msg[r : r + 1, :] = part[:, r * 128 : (r + 1) * 128]
    msg[8:16, :] = jnp.broadcast_to(shift, (8, 128))


def merge_rows(parts):
    shifts = [p[8:16, :] for p in parts]
    top = functools.reduce(jnp.maximum, shifts)
    terms = []
    for part, shift in zip(parts, shifts):
        half = jnp.exp2(0.5 * (shift - top))
        terms.append(part[0:8, :] * half * half)
    return pair_sum(terms), top


def first_pair_kernel(place, own, received, out, la_out):
    pair_kernel(own, received, out)
    mine, theirs = own[16:20, :], received[16:20, :]
    la_out[0:4, :] = jnp.where(place[0] == 0, mine, theirs)
    la_out[4:8, :] = jnp.where(place[0] == 0, theirs, mine)


def pair_kernel(own, received, out):
    total, top = merge_rows([own, received])
    out[0:8, :] = total
    out[8:16, :] = top


def kernel_matrix(a_unit, b_t, k_out):
    def block(j, carry):
        at = pl.multiple_of(j * 512, 512)
        left = a_unit[pl.ds(at, 512), :]
        for m in range(NK):
            span = slice(m * CH, (m + 1) * CH)
            k_out[pl.ds(at, 512), span] = jnp.exp2(nn(left, b_t[:, span]) * (2.0 * C2)).astype(BF16)
        return carry

    lax.fori_loop(0, NR // 512, block, 0)


def row_scales(parts, la, rows):
    total, top = merge_rows(parts)
    level = la[...] * LOG2E - jnp.log2(total)
    shift = jnp.max(jnp.max(level, axis=0, keepdims=True), axis=1, keepdims=True)
    rows[...] = jnp.zeros_like(rows)
    scale = jnp.exp2(level - shift + TOP)
    split_rows(scale, rows)
    return scale, shift, top


def send_all(msg, shift):
    sums = msg[0, 0:32, :]
    for d in range(NZY):
        msg[d, 0:32, :] = sums
        msg[d, 32:40, :] = jnp.broadcast_to(shift, (8, 128))


def send_cols(msg, part, shift):
    part = part[0:1, :] + part[1:2, :]
    for r in range(32):
        msg[0, r : r + 1, :] = part[:, r * 128 : (r + 1) * 128]
    send_all(msg, shift)


def col_kernel(p0, p1, p2, p3, la, k_mat, msg, base_out, rows):
    scale, shift, top = row_scales([p0, p2, p1, p3], la, rows)
    base_out[...] = top
    send_cols(msg, nn(rows[...].astype(BF16), k_mat[...]), shift)


def last_col_kernel(p0, p1, p2, p3, la, k_mat, base, a_t, msg, sums_out, base_out, rows, lhs):
    scale, shift, top = row_scales([p0, p2, p1, p3], la, rows)
    base_out[...] = base[...] + top
    scale = rows[0:1, :] + rows[1:2, :]
    lhs[0:128, :] = (a_t[...].astype(F32) * scale).astype(BF16)
    lhs[128:144, :] = rows[...].astype(BF16)
    for k in range(NK):
        part = nn(lhs[...], k_mat[:, k * CH : (k + 1) * CH])
        sums_out[k] = part[0:128, :].astype(BF16)
        total = part[128:129, :] + part[129:130, :]
        msg[0, 2 * k : 2 * k + 1, :] = total[:, 0:128]
        msg[0, 2 * k + 1 : 2 * k + 2, :] = total[:, 128:256]
    send_all(msg, shift)


def col_scales(parts, lb, rows):
    total, top = combine(parts, NZY, 32)
    log_total = jnp.log2(total)
    level = lb[...] * LOG2E - log_total
    shift = jnp.max(jnp.max(level, axis=0, keepdims=True), axis=1, keepdims=True)
    shift = jnp.ceil(shift)
    rows[...] = jnp.zeros_like(rows)
    split_rows(jnp.exp2(level - shift + TOP), rows)
    return level, total, shift, top


def row_kernel(parts, lb, kt_mat, base, msg, base_out, rows):
    level, total, shift, top = col_scales(parts, lb, rows)
    base_out[...] = base[...] - top
    put_rows(msg, nn(rows[...].astype(BF16), kt_mat[...]), shift)


def pack_rows(out_ref, flow, total, shift):
    n = flow.shape[1]
    out_ref[0:128, :] = flow.astype(BF16)
    high = total.astype(BF16).astype(F32)
    kind = lax.broadcasted_iota(jnp.int32, (16, n), 0)
    tail = jnp.where(kind == 0, high, jnp.where(kind == 1, total - high, jnp.where(kind == 2, shift, 0.0)))
    out_ref[128:144, :] = tail.astype(BF16)


def row_flow_kernel(place, parts, lb, kt_mat, base, b_t, held, own_out, other_out, pot_out, total_out, base_out, held_out,
                    rows, lhs, acc):
    core = place[0]
    level, total, shift, top = col_scales(parts, lb, rows)
    level_base = base[...] - top
    base_out[...] = level_base
    pot_out[...] = (level + level_base[0:1, :]) * (1.0 / C2)
    total_out[...] = total
    scale = rows[0:1, :] + rows[1:2, :]
    lhs[0:128, :] = (b_t[...].astype(F32) * scale).astype(BF16)
    lhs[128:144, :] = rows[...].astype(BF16)
    acc[...] = nn(lhs[...], kt_mat[...])
    for half, out in ((core, own_out), (1 - core, other_out)):
        part = acc[:, pl.ds(pl.multiple_of(half * 512, 512), 512)]
        pack_rows(out, part[0:128, :], part[128:129, :] + part[129:130, :], shift)


def merge(parts):
    tails = [p[128:144, :].astype(F32) for p in parts]
    shifts = [t[2:3, :] for t in tails]
    top = functools.reduce(jnp.maximum, shifts)
    flows, totals = [], []
    for p, t, s in zip(parts, tails, shifts):
        half = jnp.exp2(0.5 * (s - top))
        flows.append(p[0:128, :].astype(F32) * half * half)
        totals.append((t[0:1, :] + t[1:2, :]) * half * half)
    return pair_sum(flows), pair_sum(totals), top


def merge_kernel(own, received, out):
    flow, total, top = merge([own, received])
    pack_rows(out, flow, total, top)


def final_a_kernel(p0, p1, p2, p3, a_own, la, base, flow_out, pot_out):
    flow, total, top = merge([p0, p2, p1, p3])
    flow_t = flow / total
    level = jnp.log2(total) + (top - TOP - 2.0 * C2)
    for r in range(4):
        here = slice(r * 128, (r + 1) * 128)
        flow_out[here, :] = flow_t[:, here].T - a_own[here, :].astype(F32)
        pot_out[r : r + 1, :] = (la[r : r + 1, :] * LOG2E - level[:, here] - base[0:1, :]) * (1.0 / C2)


def final_b_kernel(place, sums, parts, total, b_t, own_pot, other_pot, flow_out, pot_out):
    core = place[0]
    chunk = place[1]
    shifts = [parts[d, 32:40, :] for d in range(NZY)]
    top = functools.reduce(jnp.maximum, shifts)
    acc = 0.0
    for d in range(NZY):
        half = jnp.exp2(0.5 * (shifts[d][0:1, 0:1] - top[0:1, 0:1]))
        acc = acc + sums[d].astype(F32) * half * half
    at = pl.multiple_of(chunk * CH, CH)
    unit = b_t[:, pl.ds(at, CH)].astype(F32)
    for r in range(2):
        here = slice(r * 128, (r + 1) * 128)
        denom = total[pl.ds(chunk * 2 + r, 1), :]
        flow_out[here, :] = (acc[:, here] / denom - unit[:, here]).T
    for k in range(NK):
        mine = own_pot[2 * k : 2 * k + 2, :]
        theirs = other_pot[2 * k : 2 * k + 2, :]
        pot_out[4 * k : 4 * k + 2, :] = jnp.where(core == 0, mine, theirs)
        pot_out[4 * k + 2 : 4 * k + 4, :] = jnp.where(core == 0, theirs, mine)


def sds(*shape, dtype=F32):
    return jax.ShapeDtypeStruct(shape, dtype)


VM = pl.BlockSpec(memory_space=pltpu.VMEM)
SM = pl.BlockSpec(memory_space=pltpu.SMEM)
HB = pl.BlockSpec(memory_space=pltpu.HBM)
ANY = pl.BlockSpec(memory_space=pl.ANY)


def call(kernel, ins, outs, scratch=(), flops=0, bytes_accessed=0, trans=0, passes=None):
    return pl.pallas_call(
        kernel,
        in_specs=ins,
        out_specs=[ANY if i in (passes or {}).values() else VM for i in range(len(outs))],
        input_output_aliases=passes or {},
        out_shape=outs,
        scratch_shapes=list(scratch),
        compiler_params=pltpu.CompilerParams(vmem_limit_bytes=16 * 1024 * 1024),
        cost_estimate=pl.CostEstimate(flops=flops, bytes_accessed=bytes_accessed, transcendentals=trans),
    )


PASS = NR * NC


def on_device(desc_a, desc_b, logmass_a, logmass_b, g_start):
    core = lax.axis_index("core")
    place = jnp.stack([core, lax.axis_index("zy")]).astype(jnp.int32)
    swap = [(0, 1), (1, 0)]
    ring = [[(i, (i + s) % 4) for i in range(4)] for s in range(4)]
    keep = lambda x: pltpu.with_memory_space_constraint(x, pltpu.VMEM)
    stay = lambda x: pltpu.with_memory_space_constraint(x, pltpu.HBM)
    la_own = logmass_a.reshape(4, 128)
    other_a = lax.ppermute(desc_a, "core", swap)

    a_own, b_unit, b_t, at_own, rows, shift, lb = call(
        prep_kernel,
        [SM, HB, HB, HB, HB],
        [
            sds(512, DIM, dtype=BF16),
            sds(NC, DIM, dtype=BF16),
            sds(DIM, NC, dtype=BF16),
            sds(DIM, 512, dtype=BF16),
            sds(16, NC, dtype=BF16),
            sds(8, 128),
            sds(32, 128),
        ],
        [
            pltpu.VMEM((NK, CH, DIM), BF16),
            pltpu.VMEM((512, DIM), BF16),
            pltpu.VMEM((64, 128), F32),
            pltpu.VMEM((64, 128), F32),
            pltpu.VMEM((32, 128), F32),
            pltpu.VMEM((16, NC), F32),
            pltpu.SemaphoreType.DMA((NK + 3,)),
        ],
        flops=8 * NC * DIM,
        bytes_accessed=2 * NC * DIM,
    )(
        place,
        stay(desc_b.reshape(NK, 2, CH, DIM)),
        stay(g_start.reshape(64, 128)),
        stay(logmass_b.reshape(64, 128)),
        stay(desc_a),
    )


    kt_mat, a_t, a_unit, msg = call(
        first_kernel,
        [SM] + [VM] * 6,
        [pltpu.VMEM((NC, NR), BF16), sds(DIM, NR, dtype=BF16), sds(NR, DIM, dtype=BF16), sds(24, 128)],
        flops=2 * PASS * DIM,
        trans=PASS,
    )(place, at_own, other_a, la_own, b_unit, rows, shift)

    def over_x(pair):
        return [pair] + [lax.ppermute(pair, "x", ring[s]) for s in (1, 2, 3)]

    pair, la = call(first_pair_kernel, [SM] + [VM] * 2, [sds(16, 128), sds(8, 128)])(
        place, msg, lax.ppermute(msg, "core", swap)
    )
    k_mat = call(
        kernel_matrix, [VM] * 2, [pltpu.VMEM((NR, NC), BF16)], flops=2 * PASS * DIM, trans=PASS
    )(a_unit, b_t)[0]
    msg, base = call(
        col_kernel,
        [VM] * 6,
        [sds(NZY, 40, 128), sds(8, 128)],
        [pltpu.VMEM((16, NR), F32)],
        flops=2 * PASS * 16,
    )(*over_x(pair), la, keep(k_mat))

    parts = lax.all_to_all(msg, "zy", 0, 0)
    msg, base = call(
        row_kernel,
        [VM] * 4,
        [sds(16, 128), sds(8, 128)],
        [pltpu.VMEM((16, NC), F32)],
        flops=2 * PASS * 16,
    )(parts, lb, keep(kt_mat), base)

    pair = call(pair_kernel, [VM] * 2, [sds(16, 128)])(msg, lax.ppermute(msg, "core", swap))[0]
    msg, sums, base = call(
        last_col_kernel,
        [VM] * 8,
        [sds(NZY, 40, 128), sds(NZY, DIM, CH, dtype=BF16), sds(8, 128)],
        [pltpu.VMEM((16, NR), F32), pltpu.VMEM((144, NR), BF16)],
        flops=2 * PASS * 144,
    )(*over_x(pair), la, keep(k_mat), base, a_t)
    parts = lax.all_to_all(msg, "zy", 0, 0)
    own, other, own_pot, total, base, sums = call(
        row_flow_kernel,
        [SM] + [VM] * 5 + [ANY],
        [
            sds(144, 512, dtype=BF16),
            sds(144, 512, dtype=BF16),
            sds(32, 128),
            sds(32, 128),
            sds(8, 128),
            sds(NZY, DIM, CH, dtype=BF16),
        ],
        [pltpu.VMEM((16, NC), F32), pltpu.VMEM((144, NC), BF16), pltpu.VMEM((144, NR), F32)],
        flops=2 * PASS * 144,
        passes={6: 5},
    )(place, parts, lb, keep(kt_mat), base, b_t, sums)

    received = lax.ppermute(other, "core", swap)
    sums = lax.all_to_all(sums, "zy", 0, 0)
    other_pot = lax.ppermute(own_pot, "core", swap)
    mine = call(merge_kernel, [VM] * 2, [sds(144, 512, dtype=BF16)])(own, received)[0]
    others = over_x(mine)[1:]
    flow_a, pot_a = call(
        final_a_kernel, [VM] * 7, [sds(512, DIM), sds(4, 128)]
    )(mine, *others, a_own, la_own, base)
    flow_b, pot_b = call(
        final_b_kernel, [SM] + [VM] * 6, [sds(CH, DIM), sds(64, 128)]
    )(place, sums, parts, total, b_t, own_pot, other_pot)
    return (pot_a.reshape(512), pot_b.reshape(8192), flow_a, flow_b)


def solution(mesh):
    fine = Mesh(mesh.devices.reshape(NZY, 2, 4), ("zy", "core", "x"))
    wide = ("zy", "core")
    return jax.shard_map(
        on_device,
        mesh=fine,
        in_specs=(P(wide, None), P("x", None), P(wide), P("x"), P("x")),
        out_specs=(P(wide), P("x"), P(wide, None), P(("x", "zy", "core"), None)),
        check_vma=False,
    )
```

time: 114 us -> 86.8 us (0.76)
  local copies, waits for them, and re-layouts: 14 us -> 0.68 us
  Pallas kernels: 32.5 us -> 22 us
  blocking collectives: 37.9 us -> 28.9 us
  waiting for transfers between devices: 15.4 us -> 19.9 us
  starting transfers between devices: 11.6 us -> 14.2 us
    unnamed x18 -> x4, local copies, waits for them, and re-layouts: 14 us -> 0.68 us
    pallas_call x8 -> x12, Pallas kernels: 32.5 us -> 22 us  [the longest x1 4.55 us: on_device(): call(prep_kernel, [SM, HB, HB, HB, HB], [sds(512, DIM, dtype=BF16), sds(N...]
    ppermute x4 -> x11, waiting for transfers between devices: 8.52 us -> 17 us  [the longest x9 15 us: over_x(): return [pair] + [lax.ppermute(pair, 'x', ring[s]) for s in (1, 2, 3)]]
    all_to_all x1 -> x0, blocking collectives: 7.73 us -> none  [on_device(): parts = lax.all_to_all(msg, ('core', 'x'), 0, 0)]
    ppermute x4 -> x11, starting transfers between devices: 3.36 us -> 10.4 us  [the longest x9 9.89 us: over_x(): return [pair] + [lax.ppermute(pair, 'x', ring[s]) for s in (1, 2, 3)]]
    all_to_all x1 -> x0, waiting for transfers between devices: 4.58 us -> none  [on_device(): parts = lax.all_to_all(msg, ('core', 'x'), 0, 0)]
    all_to_all x1 -> x0, starting transfers between devices: 4.38 us -> none  [on_device(): parts = lax.all_to_all(msg, ('core', 'x'), 0, 0)]
    all_to_all x1, waiting for transfers between devices: 0.01 us -> 1.52 us  [on_device(): sums = lax.all_to_all(sums, 'zy', 0, 0)]
  transfers between devices with their start and end apart: 9 -> 15, of which waited for: 6 -> 12; matrix products, arithmetic and copies ran while one was open for 1% -> 0% of each run, Pallas kernels for 18% -> 9%
where the time goes in v2:
time: 86.8 us; the launch traced here: 86.5 us
  blocking collectives  28.9 us (33%)
  Pallas kernels  22 us (25%)
  waiting for transfers between devices  19.9 us (23%)
  starting transfers between devices  14.2 us (16%)
    all_to_all x2, blocking collectives, on_device(): parts = lax.all_to_all(msg, 'zy', 0, 0)  28.9 us
    ppermute x9, waiting for transfers between devices, over_x(): return [pair] + [lax.ppermute(pair, 'x', ring[s]) for s in (1, 2, 3)]  15 us
    ppermute x9, starting transfers between devices, over_x(): return [pair] + [lax.ppermute(pair, 'x', ring[s]) for s in (1, 2, 3)]  9.89 us
    pallas_call x1, Pallas kernels, on_device(): call(prep_kernel, [SM, HB, HB, HB, HB], [sds(512, DIM, dtype=BF16), sds(N...  4.55 us
    pallas_call x1, Pallas kernels, on_device(): call(first_kernel, [SM] + [VM] * 6, [pltpu.VMEM((NC, NR), BF16), sds(DIM,...  4.4 us
    all_to_all x1, starting transfers between devices, on_device(): sums = lax.all_to_all(sums, 'zy', 0, 0)  3.66 us
    pallas_call x1, Pallas kernels, on_device(): call(last_col_kernel, [VM] * 8, [sds(NZY, 40, 128), sds(NZY, DIM, CH, dty...  2.54 us
    pallas_call x1, Pallas kernels, on_device(): call(kernel_matrix, [VM] * 2, [pltpu.VMEM((NR, NC), BF16)], flops=2 * PAS...  2.47 us
  transfers between devices with their start and end apart: 15, of which 12 were waited for; matrix products, arithmetic and copies ran while one was open for 0% of the time, Pallas kernels for 9%

profile of v2, /device:TPU:0, one launch (start us, length us, event | category | flops | bytes accessed | tf_op | source)
XLA Modules:
  0.0 86.5 jit_solution(11939887546130255103)
XLA Ops:
  0.6 0.1 collective-permute-start
  0.7 0.1 pad_add_fusion.place
  0.8 4.5 %shard_map.84 = (bf16[512,128]{1,0:T(8,128)(2,1)S(1)}, bf16[4096,128]{1,0:T(8,128)(2,1)S(1)}, bf16[128,4096]{1,0:T(8,128)(2,1)S(1)}, bf16[128,512]{1,0:T(8,128)(...) custom-call(s32[2]{0:T(128)S(1)} %pad_add_fusion.place, ...), custom_call_target="tpu_custom_call" | custom-call | flops 4194304 | bytes 1048576 | tf_op jit(solution)/shard_map/pallas_call | solution.py:346
  5.4 0.0 collective-permute-done.other_a
  5.4 0.0 copy-start
  5.4 0.7 copy-done
  6.1 4.4 %shard_map.85 = (bf16[4096,1024]{1,0:T(8,128)(2,1)S(1)}, bf16[128,1024]{1,0:T(8,128)(2,1)S(1)}, bf16[1024,128]{1,0:T(8,128)(2,1)S(1)}, f32[24,128]{1,0:T(8,128)S(1)}) custom-call(s32[2]{0:T(128)S(1)} %pad_add_fusion.place, bf16[128,512]{1,0:T(8,128)(2,1)S(1)} %get-tuple-element.34.at_own, bf16[512,128]{1,0:T(8,128)(2,1)S(1)} %collective-permute-done.other_a, ...), custom_call_target="tpu_custom_call" | custom-call | flops 1073741824 | tf_op jit(solution)/shard_map/pallas_call | solution.py:378
  10.5 0.5 collective-permute-start.1
  11.0 0.8 collective-permute-done.1.received
  11.8 0.6 shard_map.86
  12.4 2.9 %collective-permute-start.4 = (f32[16,128]{1,0:T(8,128)S(1)}, f32[16,128]{1,0:T(8,128)S(1)}, u32[]{:S(2)}, u32[]{:S(2)}) collective-permute-start(f32[16,128]{1,0:T(8,128)S(1)} %get-tuple-element.39.p0), channel_id=1, source_target_pairs={{0,3},{1,0},{2,1},{3,2},{4,7},{5,4},{6,5},{7,6},{8,11},{9,8},{10,9... | collective-permute-start | bytes 24584 | tf_op jit(solution)/shard_map/ppermute | solution.py:387
  15.3 0.8 collective-permute-start.3
  16.1 0.9 %collective-permute-start.2 = (f32[16,128]{1,0:T(8,128)S(1)}, f32[16,128]{1,0:T(8,128)S(1)}, u32[]{:S(2)}, u32[]{:S(2)}) collective-permute-start(f32[16,128]{1,0:T(8,128)S(1)} %get-tuple-element.39.p0), channel_id=1, source_target_pairs={{0,1},{1,2},{2,3},{3,0},{4,5},{5,6},{6,7},{7,4},{8,9},{9,10},{10,1... | collective-permute-start | bytes 24584 | tf_op jit(solution)/shard_map/ppermute | solution.py:387
  17.0 2.5 %shard_map.87.k_mat = bf16[1024,4096]{1,0:T(8,128)(2,1)S(1)} custom-call(bf16[1024,128]{1,0:T(8,128)(2,1)S(1)} %get-tuple-element.41.a_unit, bf16[128,4096]{1,0:T(8,128)(2,1)S(1)} %get-tuple-element.42.b_t), custom_call_target="tpu_custom_call" | custom-call | flops 1073741824 | tf_op jit(solution)/shard_map/pallas_call | solution.py:392
  19.4 0.0 collective-permute-done.4.p3
  19.4 1.0 %collective-permute-done.3.p2 = f32[16,128]{1,0:T(8,128)S(1)} collective-permute-done((f32[16,128]{1,0:T(8,128)S(1)}, f32[16,128]{1,0:T(8,128)S(1)}, u32[]{:S(2)}, u32[]{:S(2)}) %collective-permute-start.3) | collective-permute-done | bytes 8224 | tf_op jit(solution)/shard_map/ppermute | solution.py:387
  20.4 0.5 collective-permute-done.2.p1
  20.9 1.3 %shard_map.88 = (f32[16,40,128]{2,1,0:T(8,128)S(1)}, f32[8,128]{1,0:T(8,128)S(1)}) custom-call(f32[16,128]{1,0:T(8,128)S(1)} %get-tuple-element.39.p0, f32[16,128]{1,0:T(8,128)S(1)} %collective-permute-done.2.p1, f32[16,128]{1,0:T(8,128)S(1)} %collective-permute-done.3.p2, f32[16,128]{1,0:T(8,128)S(1)} %collective-permute-done.4.p3, ...), custom_call_target="tpu_custom_call" | custom-call | flops 134217728 | tf_op jit(solution)/shard_map/pallas_call | solution.py:395
  22.2 16.9 %all_to_all.15.parts = f32[16,40,128]{2,1,0:T(8,128)S(1)} all-to-all(f32[16,40,128]{2,1,0:T(8,128)S(1)} %get-tuple-element.43), channel_id=1, replica_groups=mesh['zy'=16,'core'=2,'x'=4] {'zy'}, dimensions={0} | all-to-all | bytes 655360 | tf_op jit(solution)/shard_map/all_to_all | solution.py:403
  39.1 1.3 %shard_map.89 = (f32[16,128]{1,0:T(8,128)S(1)}, f32[8,128]{1,0:T(8,128)S(1)}) custom-call(f32[16,40,128]{2,1,0:T(8,128)S(1)} %all_to_all.15.parts, f32[32,128]{1,0:T(8,128)S(1)} %get-tuple-element.44.lb, bf16[4096,1024]{1,0:T(8,128)(2,1)S(1)} %get-tuple-element.45.kt_mat, f32[8,128]{1,0:T(8,128)S(1)} %get-tuple-element.46.base), custom_call_target="tpu_custom_call" | custom-call | flops 134217728 | tf_op jit(solution)/shard_map/pallas_call | solution.py:404
  40.5 0.0 collective-permute-start.5
  40.5 1.2 %collective-permute-done.5.received = f32[16,128]{1,0:T(8,128)S(1)} collective-permute-done((f32[16,128]{1,0:T(8,128)S(1)}, f32[16,128]{1,0:T(8,128)S(1)}, u32[]{:S(2)}, u32[]{:S(2)}) %collective-permute-start.5) | collective-permute-done | bytes 8224 | tf_op jit(solution)/shard_map/ppermute | solution.py:412
  41.6 1.0 %collective-permute-start.8 = (f32[16,128]{1,0:T(8,128)S(1)}, f32[16,128]{1,0:T(8,128)S(1)}, u32[]{:S(2)}, u32[]{:S(2)}) collective-permute-start(f32[16,128]{1,0:T(8,128)S(1)} %shard_map.90.p0), channel_id=1, source_target_pairs={{0,3},{1,0},{2,1},{3,2},{4,7},{5,4},{6,5},{7,6},{8,11},{9,8},{10,9... | collective-permute-start | bytes 24584 | tf_op jit(solution)/shard_map/ppermute | solution.py:387
  42.6 1.5 %collective-permute-start.7 = (f32[16,128]{1,0:T(8,128)S(1)}, f32[16,128]{1,0:T(8,128)S(1)}, u32[]{:S(2)}, u32[]{:S(2)}) collective-permute-start(f32[16,128]{1,0:T(8,128)S(1)} %shard_map.90.p0), channel_id=1, source_target_pairs={{0,2},{1,3},{2,0},{3,1},{4,6},{5,7},{6,4},{7,5},{8,10},{9,11},{10,... | collective-permute-start | bytes 24584 | tf_op jit(solution)/shard_map/ppermute | solution.py:387
  44.1 0.5 collective-permute-start.6
  44.7 0.7 collective-permute-done.8.p3
  45.4 2.4 %collective-permute-done.7.p2 = f32[16,128]{1,0:T(8,128)S(1)} collective-permute-done((f32[16,128]{1,0:T(8,128)S(1)}, f32[16,128]{1,0:T(8,128)S(1)}, u32[]{:S(2)}, u32[]{:S(2)}) %collective-permute-start.7) | collective-permute-done | bytes 8224 | tf_op jit(solution)/shard_map/ppermute | solution.py:387
  47.8 1.2 %collective-permute-done.6.p1 = f32[16,128]{1,0:T(8,128)S(1)} collective-permute-done((f32[16,128]{1,0:T(8,128)S(1)}, f32[16,128]{1,0:T(8,128)S(1)}, u32[]{:S(2)}, u32[]{:S(2)}) %collective-permute-start.6) | collective-permute-done | bytes 8224 | tf_op jit(solution)/shard_map/ppermute | solution.py:387
  49.0 2.5 %shard_map.91 = (f32[16,40,128]{2,1,0:T(8,128)S(1)}, bf16[16,128,256]{2,1,0:T(8,128)(2,1)}, f32[8,128]{1,0:T(8,128)S(1)}) custom-call(f32[16,128]{1,0:T(8,128)S(1)} %shard_map.90.p0, f32[16,128]{1,0:T(8,128)S(1)} %collective-permute-done.6.p1, f32[16,128]{1,0:T(8,128)S(1)} %collective-permute-done.7.p2, f32[16,128]{1,0:T(8,128)S(1)} %collective-permute-done.8.p3, ...), custom_call_target="tpu_custom_call" | custom-call | flops 1207959552 | tf_op jit(solution)/shard_map/pallas_call | solution.py:413
  51.5 0.0 copy-start.1
  51.5 12.0 %all_to_all.16.parts = f32[16,40,128]{2,1,0:T(8,128)S(1)} all-to-all(f32[16,40,128]{2,1,0:T(8,128)S(1)} %get-tuple-element.50), channel_id=1, replica_groups=mesh['zy'=16,'core'=2,'x'=4] {'zy'}, dimensions={0} | all-to-all | bytes 655360 | tf_op jit(solution)/shard_map/all_to_all | solution.py:420
  63.6 2.2 %shard_map.92 = (bf16[144,512]{1,0:T(8,128)(2,1)S(1)}, bf16[144,512]{1,0:T(8,128)(2,1)S(1)}, f32[32,128]{1,0:T(8,128)S(1)}, f32[32,128]{1,0:T(8,128)S(1)}, f32[8...) custom-call(s32[2]{0:T(128)S(1)} %pad_add_fusion.place, ...), custom_call_target="tpu_custom_call", output_to_operand_aliasing={{5}: (6, {})} | custom-call | flops 1207959552 | tf_op jit(solution)/shard_map/pallas_call | solution.py:421
  65.8 3.7 %all-to-all-start.2 = ((bf16[16,128,256]{2,1,0:T(8,128)(2,1)}), bf16[16,128,256]{2,1,0:T(8,128)(2,1)S(1)}, u32[]{:S(2)}, u32[]{:S(2)}) async-start(bf16[16,128,256]{2,1,0:T(8,128)(2,1)} %get-tuple-element.58), calls=%async_computation.2 | async-start | bytes 2097152 | tf_op jit(solution)/shard_map/all_to_all | solution.py:438
  69.4 0.1 collective-permute-start.9
  69.5 1.4 %collective-permute-done.9.received = bf16[144,512]{1,0:T(8,128)(2,1)S(1)} collective-permute-done((bf16[144,512]{1,0:T(8,128)(2,1)S(1)}, bf16[144,512]{1,0:T(8,128)(2,1)S(1)}, u32[]{:S(2)}, u32[]{:S(2)}) %collective-permute-start.9) | collective-permute-done | bytes 147488 | tf_op jit(solution)/shard_map/ppermute | solution.py:437
  70.9 0.1 shard_map.93.p0
  71.0 1.1 %collective-permute-start.12 = (bf16[144,512]{1,0:T(8,128)(2,1)S(1)}, bf16[144,512]{1,0:T(8,128)(2,1)S(1)}, u32[]{:S(2)}, u32[]{:S(2)}) collective-permute-start(bf16[144,512]{1,0:T(8,128)(2,1)S(1)} %shard_map.93.p0), channel_id=1, source_target_pairs={{0,3},{1,0},{2,1},{3,2},{4,7},{5,4},{6,5},{7,6},{8,11},{9,8},{10,9... | collective-permute-start | bytes 442376 | tf_op jit(solution)/shard_map/ppermute | solution.py:387
  72.1 0.9 %collective-permute-start.11 = (bf16[144,512]{1,0:T(8,128)(2,1)S(1)}, bf16[144,512]{1,0:T(8,128)(2,1)S(1)}, u32[]{:S(2)}, u32[]{:S(2)}) collective-permute-start(bf16[144,512]{1,0:T(8,128)(2,1)S(1)} %shard_map.93.p0), channel_id=1, source_target_pairs={{0,2},{1,3},{2,0},{3,1},{4,6},{5,7},{6,4},{7,5},{8,10},{9,11},{10,... | collective-permute-start | bytes 442376 | tf_op jit(solution)/shard_map/ppermute | solution.py:387
  73.0 0.3 collective-permute-start.10
  73.3 0.0 collective-permute-start.13
  73.3 4.5 %collective-permute-done.12.p3 = bf16[144,512]{1,0:T(8,128)(2,1)S(1)} collective-permute-done((bf16[144,512]{1,0:T(8,128)(2,1)S(1)}, bf16[144,512]{1,0:T(8,128)(2,1)S(1)}, u32[]{:S(2)}, u32[]{:S(2)}) %collective-permute-start.12) | collective-permute-done | bytes 147488 | tf_op jit(solution)/shard_map/ppermute | solution.py:387
  77.7 2.6 %collective-permute-done.11.p2 = bf16[144,512]{1,0:T(8,128)(2,1)S(1)} collective-permute-done((bf16[144,512]{1,0:T(8,128)(2,1)S(1)}, bf16[144,512]{1,0:T(8,128)(2,1)S(1)}, u32[]{:S(2)}, u32[]{:S(2)}) %collective-permute-start.11) | collective-permute-done | bytes 147488 | tf_op jit(solution)/shard_map/ppermute | solution.py:387
  80.4 2.0 %collective-permute-done.10.p1 = bf16[144,512]{1,0:T(8,128)(2,1)S(1)} collective-permute-done((bf16[144,512]{1,0:T(8,128)(2,1)S(1)}, bf16[144,512]{1,0:T(8,128)(2,1)S(1)}, u32[]{:S(2)}, u32[]{:S(2)}) %collective-permute-start.10) | collective-permute-done | bytes 147488 | tf_op jit(solution)/shard_map/ppermute | solution.py:387
  82.4 0.0 copy-done.1
  82.4 0.9 %shard_map.94 = (f32[512,128]{1,0:T(8,128)}, f32[4,128]{1,0:T(4,128)}) custom-call(bf16[144,512]{1,0:T(8,128)(2,1)S(1)} %shard_map.93.p0, bf16[144,512]{1,0:T(8,128)(2,1)S(1)} %collective-permute-done.10.p1, bf16[144,512]{1,0:T(8,128)(2,1)S(1)} %collective-permute-done.11.p2, bf16[144,512]{1,0:T(8,128)(2,1)S(1)} %collective-permute-done.12.p3, ...), custom_call_target="tpu_custom_call" | custom-call | tf_op jit(solution)/shard_map/pallas_call | solution.py:442
  83.3 0.0 collective-permute-done.13.other_pot
  83.3 1.5 %all-to-all-done.2.sums = bf16[16,128,256]{2,1,0:T(8,128)(2,1)S(1)} async-done(((bf16[16,128,256]{2,1,0:T(8,128)(2,1)}), bf16[16,128,256]{2,1,0:T(8,128)(2,1)S(1)}, u32[]{:S(2)}, u32[]{:S(2)}) %all-to-all-start.2) | async-done | bytes 1048608 | tf_op jit(solution)/shard_map/all_to_all | solution.py:438
  84.9 1.6 %shard_map.95 = (f32[256,128]{1,0:T(8,128)}, f32[64,128]{1,0:T(8,128)}) custom-call(s32[2]{0:T(128)S(1)} %pad_add_fusion.place, bf16[16,128,256]{2,1,0:T(8,128)(2,1)S(1)} %all-to-all-done.2.sums, f32[16,40,128]{2,1,0:T(8,128)S(1)} %all_to_all.16.parts, f32[32,128]{1,0:T(8,128)S(1)} %get-tuple-element.59.total, bf16[128,4096]{1,0:T(8,128)(2,1)S(1)} %get-tuple-element.42.b_t, ...), custom_call_target="tpu_custom_call" | custom-call | tf_op jit(solution)/shard_map/pallas_call | solution.py:445
  (1 shorter events, 0.0 us)
Async XLA Ops:
  0.6 4.7 %collective-permute-start = (bf16[512,128]{1,0:T(8,128)(2,1)}, bf16[512,128]{1,0:T(8,128)(2,1)S(1)}, u32[]{:S(2)}, u32[]{:S(2)}) collective-permute-start(bf16[512,128]{1,0:T(8,128)(2,1)} %desc_a.1), channel_id=1, source_target_pairs={{0,4},{4,0},{1,5},{5,1},{2,6},{6,2},{3,7},{7,3},{8,12},{12,8},{9,1... | collective-permute-start | bytes 393224 | tf_op jit(solution)/shard_map/ppermute | solution.py:344
  5.4 0.7 copy-start
  10.5 1.3 %collective-permute-start.1 = (f32[24,128]{1,0:T(8,128)S(1)}, f32[24,128]{1,0:T(8,128)S(1)}, u32[]{:S(2)}, u32[]{:S(2)}) collective-permute-start(f32[24,128]{1,0:T(8,128)S(1)} %get-tuple-element.38.own), channel_id=1, source_target_pairs={{0,4},{4,0},{1,5},{5,1},{2,6},{6,2},{3,7},{7,3},{8,12},{12,8},{9,1... | collective-permute-start | bytes 36872 | tf_op jit(solution)/shard_map/ppermute | solution.py:390
  12.4 7.1 %collective-permute-start.4 = (f32[16,128]{1,0:T(8,128)S(1)}, f32[16,128]{1,0:T(8,128)S(1)}, u32[]{:S(2)}, u32[]{:S(2)}) collective-permute-start(f32[16,128]{1,0:T(8,128)S(1)} %get-tuple-element.39.p0), channel_id=1, source_target_pairs={{0,3},{1,0},{2,1},{3,2},{4,7},{5,4},{6,5},{7,6},{8,11},{9,8},{10,9... | collective-permute-start | bytes 24584 | tf_op jit(solution)/shard_map/ppermute | solution.py:387
  15.3 5.2 %collective-permute-start.3 = (f32[16,128]{1,0:T(8,128)S(1)}, f32[16,128]{1,0:T(8,128)S(1)}, u32[]{:S(2)}, u32[]{:S(2)}) collective-permute-start(f32[16,128]{1,0:T(8,128)S(1)} %get-tuple-element.39.p0), channel_id=1, source_target_pairs={{0,2},{1,3},{2,0},{3,1},{4,6},{5,7},{6,4},{7,5},{8,10},{9,11},{10,... | collective-permute-start | bytes 24584 | tf_op jit(solution)/shard_map/ppermute | solution.py:387
  16.1 4.9 %collective-permute-start.2 = (f32[16,128]{1,0:T(8,128)S(1)}, f32[16,128]{1,0:T(8,128)S(1)}, u32[]{:S(2)}, u32[]{:S(2)}) collective-permute-start(f32[16,128]{1,0:T(8,128)S(1)} %get-tuple-element.39.p0), channel_id=1, source_target_pairs={{0,1},{1,2},{2,3},{3,0},{4,5},{5,6},{6,7},{7,4},{8,9},{9,10},{10,1... | collective-permute-start | bytes 24584 | tf_op jit(solution)/shard_map/ppermute | solution.py:387
  40.5 1.2 %collective-permute-start.5 = (f32[16,128]{1,0:T(8,128)S(1)}, f32[16,128]{1,0:T(8,128)S(1)}, u32[]{:S(2)}, u32[]{:S(2)}) collective-permute-start(f32[16,128]{1,0:T(8,128)S(1)} %get-tuple-element.47.own), channel_id=1, source_target_pairs={{0,4},{4,0},{1,5},{5,1},{2,6},{6,2},{3,7},{7,3},{8,12},{12,8},{9,1... | collective-permute-start | bytes 24584 | tf_op jit(solution)/shard_map/ppermute | solution.py:412
  41.6 3.7 %collective-permute-start.8 = (f32[16,128]{1,0:T(8,128)S(1)}, f32[16,128]{1,0:T(8,128)S(1)}, u32[]{:S(2)}, u32[]{:S(2)}) collective-permute-start(f32[16,128]{1,0:T(8,128)S(1)} %shard_map.90.p0), channel_id=1, source_target_pairs={{0,3},{1,0},{2,1},{3,2},{4,7},{5,4},{6,5},{7,6},{8,11},{9,8},{10,9... | collective-permute-start | bytes 24584 | tf_op jit(solution)/shard_map/ppermute | solution.py:387
  42.6 5.2 %collective-permute-start.7 = (f32[16,128]{1,0:T(8,128)S(1)}, f32[16,128]{1,0:T(8,128)S(1)}, u32[]{:S(2)}, u32[]{:S(2)}) collective-permute-start(f32[16,128]{1,0:T(8,128)S(1)} %shard_map.90.p0), channel_id=1, source_target_pairs={{0,2},{1,3},{2,0},{3,1},{4,6},{5,7},{6,4},{7,5},{8,10},{9,11},{10,... | collective-permute-start | bytes 24584 | tf_op jit(solution)/shard_map/ppermute | solution.py:387
  44.1 4.9 %collective-permute-start.6 = (f32[16,128]{1,0:T(8,128)S(1)}, f32[16,128]{1,0:T(8,128)S(1)}, u32[]{:S(2)}, u32[]{:S(2)}) collective-permute-start(f32[16,128]{1,0:T(8,128)S(1)} %shard_map.90.p0), channel_id=1, source_target_pairs={{0,1},{1,2},{2,3},{3,0},{4,5},{5,6},{6,7},{7,4},{8,9},{9,10},{10,1... | collective-permute-start | bytes 24584 | tf_op jit(solution)/shard_map/ppermute | solution.py:387
  51.5 30.9 %copy-start.1 = (f32[512]{0:T(512)S(1)}, f32[512]{0:T(512)}, u32[]{:S(2)}) copy-start(f32[512]{0:T(512)} %param.7) | copy-start | bytes 6148
  65.8 19.1 %all-to-all-start.2 = ((bf16[16,128,256]{2,1,0:T(8,128)(2,1)}), bf16[16,128,256]{2,1,0:T(8,128)(2,1)S(1)}, u32[]{:S(2)}, u32[]{:S(2)}) async-start(bf16[16,128,256]{2,1,0:T(8,128)(2,1)} %get-tuple-element.58), calls=%async_computation.2 | async-start | bytes 2097152 | tf_op jit(solution)/shard_map/all_to_all | solution.py:438
  69.4 1.5 %collective-permute-start.9 = (bf16[144,512]{1,0:T(8,128)(2,1)S(1)}, bf16[144,512]{1,0:T(8,128)(2,1)S(1)}, u32[]{:S(2)}, u32[]{:S(2)}) collective-permute-start(bf16[144,512]{1,0:T(8,128)(2,1)S(1)} %get-tuple-element.54), channel_id=1, source_target_pairs={{0,4},{4,0},{1,5},{5,1},{2,6},{6,2},{3,7},{7,3},{8,12},{12,8},{9,1... | collective-permute-start | bytes 442376 | tf_op jit(solution)/shard_map/ppermute | solution.py:437
  71.0 6.8 %collective-permute-start.12 = (bf16[144,512]{1,0:T(8,128)(2,1)S(1)}, bf16[144,512]{1,0:T(8,128)(2,1)S(1)}, u32[]{:S(2)}, u32[]{:S(2)}) collective-permute-start(bf16[144,512]{1,0:T(8,128)(2,1)S(1)} %shard_map.93.p0), channel_id=1, source_target_pairs={{0,3},{1,0},{2,1},{3,2},{4,7},{5,4},{6,5},{7,6},{8,11},{9,8},{10,9... | collective-permute-start | bytes 442376 | tf_op jit(solution)/shard_map/ppermute | solution.py:387
  72.1 8.3 %collective-permute-start.11 = (bf16[144,512]{1,0:T(8,128)(2,1)S(1)}, bf16[144,512]{1,0:T(8,128)(2,1)S(1)}, u32[]{:S(2)}, u32[]{:S(2)}) collective-permute-start(bf16[144,512]{1,0:T(8,128)(2,1)S(1)} %shard_map.93.p0), channel_id=1, source_target_pairs={{0,2},{1,3},{2,0},{3,1},{4,6},{5,7},{6,4},{7,5},{8,10},{9,11},{10,... | collective-permute-start | bytes 442376 | tf_op jit(solution)/shard_map/ppermute | solution.py:387
  73.0 9.4 %collective-permute-start.10 = (bf16[144,512]{1,0:T(8,128)(2,1)S(1)}, bf16[144,512]{1,0:T(8,128)(2,1)S(1)}, u32[]{:S(2)}, u32[]{:S(2)}) collective-permute-start(bf16[144,512]{1,0:T(8,128)(2,1)S(1)} %shard_map.93.p0), channel_id=1, source_target_pairs={{0,1},{1,2},{2,3},{3,0},{4,5},{5,6},{6,7},{7,4},{8,9},{9,10},{10,1... | collective-permute-start | bytes 442376 | tf_op jit(solution)/shard_map/ppermute | solution.py:387
  73.3 10.1 %collective-permute-start.13 = (f32[32,128]{1,0:T(8,128)S(1)}, f32[32,128]{1,0:T(8,128)S(1)}, u32[]{:S(2)}, u32[]{:S(2)}) collective-permute-start(f32[32,128]{1,0:T(8,128)S(1)} %get-tuple-element.60.own_pot), channel_id=1, source_target_pairs={{0,4},{4,0},{1,5},{5,1},{2,6},{6,2},{3,7},{7,3},{8,12},{12,8},{9,1... | collective-permute-start | bytes 49160 | tf_op jit(solution)/shard_map/ppermute | solution.py:439

commit v3 on v2

--- a/solution.py
+++ b/solution.py
@@ -70,13 +70,14 @@
     return (raw / norm).astype(BF16)
 
 
-def prep_kernel(place, desc_b, g_all, lb_all, desc_a, a_out, b_out, bt_out, at_out, rows_out, shift_out, lb_out,
+def prep_kernel(desc_b, g_all, lb_all, desc_a, la_all, bt_out, at_out, rows_out, shift_out, lb_out, la_out,
                 b_raw, a_raw, g_raw, lb_raw, vec, rows, sems):
-    core = place[0]
+    core = lax.axis_index("core")
     copies = [
         pltpu.make_async_copy(g_all, g_raw, sems.at[NK]),
         pltpu.make_async_copy(desc_a, a_raw, sems.at[NK + 1]),
         pltpu.make_async_copy(lb_all, lb_raw, sems.at[NK + 2]),
+        pltpu.make_async_copy(la_all, la_out, sems.at[NK + 3]),
     ]
     loads = [pltpu.make_async_copy(desc_b.at[k, core], b_raw.at[k], sems.at[k]) for k in range(NK)]
     for copy in copies + loads:
@@ -93,38 +94,33 @@
     rows_out[...] = rows[...].astype(BF16)
     for m in range(2):
         span = slice(m * 256, (m + 1) * 256)
-        unit = unit_t(a_raw[span, :].T.astype(F32))
-        at_out[:, span] = unit
-        a_out[span, :] = unit.T
+        at_out[:, span] = unit_t(a_raw[span, :].T.astype(F32))
     for k in range(NK):
         loads[k].wait()
-        span = slice(k * CH, (k + 1) * CH)
-        unit = unit_t(b_raw[k].T.astype(F32))
-        bt_out[:, span] = unit
-        b_out[span, :] = unit.T
-
-
-def first_kernel(place, at_own, other_a, la_own, b_unit, rows, shift, kt_out, at_out, a_out, msg):
-    core = place[0]
+        bt_out[:, k * CH : (k + 1) * CH] = unit_t(b_raw[k].T.astype(F32))
+
+
+def tn(left, right):
+    return lax.dot_general(left, right, (((0,), (0,)), ((), ())), preferred_element_type=F32)
+
+
+def fill_exponentials(left_t, right_t, out):
+    for q in range(left_t.shape[1] // 512):
+        left = left_t[:, q * 512 : (q + 1) * 512]
+        for m in range(right_t.shape[1] // 256):
+            span = slice(m * 256, (m + 1) * 256)
+            out[q * 512 : (q + 1) * 512, span] = jnp.exp2(tn(left, right_t[:, span]) * (2.0 * C2)).astype(BF16)
+
+
+def first_kernel(at_own, other_a, la_own, b_t, rows, shift, kt_out, at_out, msg):
+    core = lax.axis_index("core")
     for m in range(2):
         span = slice(m * 256, (m + 1) * 256)
         for half, unit in ((core, at_own[:, span]), (1 - core, unit_t(other_a[span, :].T.astype(F32)))):
-            at = pl.multiple_of(half * 512 + m * 256, 256)
-            at_out[:, pl.ds(at, 256)] = unit
-            a_out[pl.ds(at, 256), :] = unit.T
+            at_out[:, pl.ds(pl.multiple_of(half * 512 + m * 256, 256), 256)] = unit
     msg[16:20, :] = la_own[...]
     msg[20:24, :] = la_own[...]
-
-    def block(j, carry):
-        at = pl.multiple_of(j * 2048, 2048)
-        for q in range(4):
-            left = b_unit[pl.ds(at + q * 512, 512), :]
-            for m in range(NR // 256):
-                span = slice(m * 256, (m + 1) * 256)
-                kt_out[pl.ds(at + q * 512, 512), span] = jnp.exp2(nn(left, at_out[:, span]) * (2.0 * C2)).astype(BF16)
-        return carry
-
-    lax.fori_loop(0, NC // 2048, block, 0)
+    fill_exponentials(b_t, at_out, kt_out)
     put_rows(msg, nn(rows[...], kt_out[...]), shift[0:1, :])
 
 
@@ -145,11 +141,12 @@
     return pair_sum(terms), top
 
 
-def first_pair_kernel(place, own, received, out, la_out):
+def first_pair_kernel(own, received, out, la_out):
+    core = lax.axis_index("core")
     pair_kernel(own, received, out)
     mine, theirs = own[16:20, :], received[16:20, :]
-    la_out[0:4, :] = jnp.where(place[0] == 0, mine, theirs)
-    la_out[4:8, :] = jnp.where(place[0] == 0, theirs, mine)
+    la_out[0:4, :] = jnp.where(core == 0, mine, theirs)
+    la_out[4:8, :] = jnp.where(core == 0, theirs, mine)
 
 
 def pair_kernel(own, received, out):
@@ -158,16 +155,8 @@
     out[8:16, :] = top
 
 
-def kernel_matrix(a_unit, b_t, k_out):
-    def block(j, carry):
-        at = pl.multiple_of(j * 512, 512)
-        left = a_unit[pl.ds(at, 512), :]
-        for m in range(NK):
-            span = slice(m * CH, (m + 1) * CH)
-            k_out[pl.ds(at, 512), span] = jnp.exp2(nn(left, b_t[:, span]) * (2.0 * C2)).astype(BF16)
-        return carry
-
-    lax.fori_loop(0, NR // 512, block, 0)
+def kernel_matrix(a_t, b_t, k_out):
+    fill_exponentials(a_t, b_t, k_out)
 
 
 def row_scales(parts, la, rows):
@@ -241,9 +230,9 @@
     out_ref[128:144, :] = tail.astype(BF16)
 
 
-def row_flow_kernel(place, parts, lb, kt_mat, base, b_t, held, own_out, other_out, pot_out, total_out, base_out, held_out,
+def row_flow_kernel(parts, lb, kt_mat, base, b_t, held, own_out, other_out, pot_out, total_out, base_out, held_out,
                     rows, lhs, acc):
-    core = place[0]
+    core = lax.axis_index("core")
     level, total, shift, top = col_scales(parts, lb, rows)
     level_base = base[...] - top
     base_out[...] = level_base
@@ -275,19 +264,19 @@
     pack_rows(out, flow, total, top)
 
 
-def final_a_kernel(p0, p1, p2, p3, a_own, la, base, flow_out, pot_out):
+def final_a_kernel(p0, p1, p2, p3, at_own, la, base, flow_out, pot_out):
     flow, total, top = merge([p0, p2, p1, p3])
     flow_t = flow / total
     level = jnp.log2(total) + (top - TOP - 2.0 * C2)
     for r in range(4):
         here = slice(r * 128, (r + 1) * 128)
-        flow_out[here, :] = flow_t[:, here].T - a_own[here, :].astype(F32)
+        flow_out[here, :] = (flow_t[:, here] - at_own[:, here].astype(F32)).T
         pot_out[r : r + 1, :] = (la[r : r + 1, :] * LOG2E - level[:, here] - base[0:1, :]) * (1.0 / C2)
 
 
-def final_b_kernel(place, sums, parts, total, b_t, own_pot, other_pot, flow_out, pot_out):
-    core = place[0]
-    chunk = place[1]
+def final_b_kernel(sums, parts, total, b_t, own_pot, other_pot, flow_out, pot_out):
+    core = lax.axis_index("core")
+    chunk = lax.axis_index("zy")
     shifts = [parts[d, 32:40, :] for d in range(NZY)]
     top = functools.reduce(jnp.maximum, shifts)
     acc = 0.0
@@ -312,7 +301,6 @@
 
 
 VM = pl.BlockSpec(memory_space=pltpu.VMEM)
-SM = pl.BlockSpec(memory_space=pltpu.SMEM)
 HB = pl.BlockSpec(memory_space=pltpu.HBM)
 ANY = pl.BlockSpec(memory_space=pl.ANY)
 
@@ -334,26 +322,22 @@
 
 
 def on_device(desc_a, desc_b, logmass_a, logmass_b, g_start):
-    core = lax.axis_index("core")
-    place = jnp.stack([core, lax.axis_index("zy")]).astype(jnp.int32)
     swap = [(0, 1), (1, 0)]
     ring = [[(i, (i + s) % 4) for i in range(4)] for s in range(4)]
     keep = lambda x: pltpu.with_memory_space_constraint(x, pltpu.VMEM)
     stay = lambda x: pltpu.with_memory_space_constraint(x, pltpu.HBM)
-    la_own = logmass_a.reshape(4, 128)
     other_a = lax.ppermute(desc_a, "core", swap)
 
-    a_own, b_unit, b_t, at_own, rows, shift, lb = call(
+    b_t, at_own, rows, shift, lb, la_own = call(
         prep_kernel,
-        [SM, HB, HB, HB, HB],
+        [HB] * 5,
         [
-            sds(512, DIM, dtype=BF16),
-            sds(NC, DIM, dtype=BF16),
             sds(DIM, NC, dtype=BF16),
             sds(DIM, 512, dtype=BF16),
             sds(16, NC, dtype=BF16),
             sds(8, 128),
             sds(32, 128),
+            sds(4, 128),
         ],
         [
             pltpu.VMEM((NK, CH, DIM), BF16),
@@ -362,36 +346,33 @@
             pltpu.VMEM((64, 128), F32),
             pltpu.VMEM((32, 128), F32),
             pltpu.VMEM((16, NC), F32),
-            pltpu.SemaphoreType.DMA((NK + 3,)),
+            pltpu.SemaphoreType.DMA((NK + 4,)),
         ],
         flops=8 * NC * DIM,
         bytes_accessed=2 * NC * DIM,
     )(
-        place,
         stay(desc_b.reshape(NK, 2, CH, DIM)),
         stay(g_start.reshape(64, 128)),
         stay(logmass_b.reshape(64, 128)),
         stay(desc_a),
+        stay(logmass_a.reshape(4, 128)),
     )
 
-
-    kt_mat, a_t, a_unit, msg = call(
+    kt_mat, a_t, msg = call(
         first_kernel,
-        [SM] + [VM] * 6,
-        [pltpu.VMEM((NC, NR), BF16), sds(DIM, NR, dtype=BF16), sds(NR, DIM, dtype=BF16), sds(24, 128)],
+        [VM] * 6,
+        [pltpu.VMEM((NC, NR), BF16), sds(DIM, NR, dtype=BF16), sds(24, 128)],
         flops=2 * PASS * DIM,
         trans=PASS,
-    )(place, at_own, other_a, la_own, b_unit, rows, shift)
+    )(at_own, other_a, la_own, b_t, rows, shift)
 
     def over_x(pair):
         return [pair] + [lax.ppermute(pair, "x", ring[s]) for s in (1, 2, 3)]
 
-    pair, la = call(first_pair_kernel, [SM] + [VM] * 2, [sds(16, 128), sds(8, 128)])(
-        place, msg, lax.ppermute(msg, "core", swap)
-    )
+    pair, la = call(first_pair_kernel, [VM] * 2, [sds(16, 128), sds(8, 128)])(msg, lax.ppermute(msg, "core", swap))
     k_mat = call(
         kernel_matrix, [VM] * 2, [pltpu.VMEM((NR, NC), BF16)], flops=2 * PASS * DIM, trans=PASS
-    )(a_unit, b_t)[0]
+    )(a_t, b_t)[0]
     msg, base = call(
         col_kernel,
         [VM] * 6,
@@ -420,7 +401,7 @@
     parts = lax.all_to_all(msg, "zy", 0, 0)
     own, other, own_pot, total, base, sums = call(
         row_flow_kernel,
-        [SM] + [VM] * 5 + [ANY],
+        [VM] * 5 + [ANY],
         [
             sds(144, 512, dtype=BF16),
             sds(144, 512, dtype=BF16),
@@ -431,8 +412,8 @@
         ],
         [pltpu.VMEM((16, NC), F32), pltpu.VMEM((144, NC), BF16), pltpu.VMEM((144, NR), F32)],
         flops=2 * PASS * 144,
-        passes={6: 5},
-    )(place, parts, lb, keep(kt_mat), base, b_t, sums)
+        passes={5: 5},
+    )(parts, lb, keep(kt_mat), base, b_t, sums)
 
     received = lax.ppermute(other, "core", swap)
     sums = lax.all_to_all(sums, "zy", 0, 0)
@@ -441,10 +422,10 @@
     others = over_x(mine)[1:]
     flow_a, pot_a = call(
         final_a_kernel, [VM] * 7, [sds(512, DIM), sds(4, 128)]
-    )(mine, *others, a_own, la_own, base)
+    )(mine, *others, at_own, la_own, base)
     flow_b, pot_b = call(
-        final_b_kernel, [SM] + [VM] * 6, [sds(CH, DIM), sds(64, 128)]
-    )(place, sums, parts, total, b_t, own_pot, other_pot)
+        final_b_kernel, [VM] * 6, [sds(CH, DIM), sds(64, 128)]
+    )(sums, parts, total, b_t, own_pot, other_pot)
     return (pot_a.reshape(512), pot_b.reshape(8192), flow_a, flow_b)
 
 

time: 86.8 us -> 81.8 us (0.942)
  Pallas kernels: 22 us -> 17.9 us
    pallas_call x5, Pallas kernels: 13.3 us -> 9.35 us  [the longest x1 3.61 us: on_device(): call(first_kernel, [VM] * 6, [pltpu.VMEM((NC, NR), BF16), sds(DIM, NR, dt...]
  transfers between devices with their start and end apart: 15 -> 15, of which waited for: 12 -> 12; matrix products, arithmetic and copies ran while one was open for 0% -> 0% of each run, Pallas kernels for 9% -> 8%
where the time goes in v3:
time: 81.8 us; the launch traced here: 81.5 us
  blocking collectives  28.8 us (35%)
  waiting for transfers between devices  19.8 us (24%)
  Pallas kernels  17.9 us (22%)
  starting transfers between devices  14.2 us (17%)
    all_to_all x2, blocking collectives, on_device(): parts = lax.all_to_all(msg, 'zy', 0, 0)  28.8 us
    ppermute x9, waiting for transfers between devices, over_x(): return [pair] + [lax.ppermute(pair, 'x', ring[s]) for s in (1, 2, 3)]  15.1 us
    ppermute x9, starting transfers between devices, over_x(): return [pair] + [lax.ppermute(pair, 'x', ring[s]) for s in (1, 2, 3)]  9.89 us
    all_to_all x1, starting transfers between devices, on_device(): sums = lax.all_to_all(sums, 'zy', 0, 0)  3.66 us
    pallas_call x1, Pallas kernels, on_device(): call(first_kernel, [VM] * 6, [pltpu.VMEM((NC, NR), BF16), sds(DIM, NR, dt...  3.61 us
    pallas_call x1, Pallas kernels, on_device(): call(prep_kernel, [HB] * 5, [sds(DIM, NC, dtype=BF16), sds(DIM, 512, dtyp...  2.99 us
    pallas_call x1, Pallas kernels, on_device(): call(last_col_kernel, [VM] * 8, [sds(NZY, 40, 128), sds(NZY, DIM, CH, dty...  2.52 us
    pallas_call x1, Pallas kernels, on_device(): call(kernel_matrix, [VM] * 2, [pltpu.VMEM((NR, NC), BF16)], flops=2 * PAS...  2.36 us
  transfers between devices with their start and end apart: 15, of which 12 were waited for; matrix products, arithmetic and copies ran while one was open for 0% of the time, Pallas kernels for 8%

profile of v3, /device:TPU:0, one launch (start us, length us, event | category | flops | bytes accessed | tf_op | source)
XLA Modules:
  0.0 81.5 jit_solution(11479479646208080326)
XLA Ops:
  0.6 0.1 collective-permute-start
  0.7 3.0 %shard_map.84 = (bf16[128,4096]{1,0:T(8,128)(2,1)S(1)}, bf16[128,512]{1,0:T(8,128)(2,1)S(1)}, bf16[16,4096]{1,0:T(8,128)(2,1)S(1)}, f32[8,128]{1,0:T(8,128)S(1)}...) custom-call(bf16[16,2,256,128]{3,2,1,0:T(8,128)(2,1)} %bitcast.6, f32[64,128]{1,0:T(8,128)} %bitcast.7, f32[64,128]{1,0:T(8,128)} %bitcast.8, ...), custom_call_target="tpu_custom_call" | custom-call | flops 4194304 | bytes 1048576 | tf_op jit(solution)/shard_map/pallas_call | solution.py:331
  3.7 0.0 collective-permute-done.other_a
  3.7 3.6 %shard_map.85 = (bf16[4096,1024]{1,0:T(8,128)(2,1)S(1)}, bf16[128,1024]{1,0:T(8,128)(2,1)S(1)}, f32[24,128]{1,0:T(8,128)S(1)}) custom-call(bf16[128,512]{1,0:T(8,128)(2,1)S(1)} %get-tuple-element.32.at_own, bf16[512,128]{1,0:T(8,128)(2,1)S(1)} %collective-permute-done.other_a, f32[4,128]{1,0:T(4,128)S(1)} %get-tuple-element.33.la_own.la, ...), custom_call_target="tpu_custom_call" | custom-call | flops 1073741824 | tf_op jit(solution)/shard_map/pallas_call | solution.py:361
  7.3 0.5 collective-permute-start.1
  7.9 0.8 %collective-permute-done.1.received = f32[24,128]{1,0:T(8,128)S(1)} collective-permute-done((f32[24,128]{1,0:T(8,128)S(1)}, f32[24,128]{1,0:T(8,128)S(1)}, u32[]{:S(2)}, u32[]{:S(2)}) %collective-permute-start.1) | collective-permute-done | bytes 12320 | tf_op jit(solution)/shard_map/ppermute | solution.py:372
  8.7 2.9 %collective-permute-start.4 = (f32[16,128]{1,0:T(8,128)S(1)}, f32[16,128]{1,0:T(8,128)S(1)}, u32[]{:S(2)}, u32[]{:S(2)}) collective-permute-start(f32[16,128]{1,0:T(8,128)S(1)} %get-tuple-element.38.p0), channel_id=1, source_target_pairs={{0,3},{1,0},{2,1},{3,2},{4,7},{5,4},{6,5},{7,6},{8,11},{9,8},{10,9... | collective-permute-start | bytes 24584 | tf_op jit(solution)/shard_map/ppermute | solution.py:370
  11.6 0.8 collective-permute-start.3
  12.4 0.9 %collective-permute-start.2 = (f32[16,128]{1,0:T(8,128)S(1)}, f32[16,128]{1,0:T(8,128)S(1)}, u32[]{:S(2)}, u32[]{:S(2)}) collective-permute-start(f32[16,128]{1,0:T(8,128)S(1)} %get-tuple-element.38.p0), channel_id=1, source_target_pairs={{0,1},{1,2},{2,3},{3,0},{4,5},{5,6},{6,7},{7,4},{8,9},{9,10},{10,1... | collective-permute-start | bytes 24584 | tf_op jit(solution)/shard_map/ppermute | solution.py:370
  13.3 2.4 %shard_map.87.k_mat = bf16[1024,4096]{1,0:T(8,128)(2,1)S(1)} custom-call(bf16[128,1024]{1,0:T(8,128)(2,1)S(1)} %get-tuple-element.40.a_t, bf16[128,4096]{1,0:T(8,128)(2,1)S(1)} %get-tuple-element.34.b_t), custom_call_target="tpu_custom_call" | custom-call | flops 1073741824 | tf_op jit(solution)/shard_map/pallas_call | solution.py:373
  15.7 0.0 collective-permute-done.4.p3
  15.7 1.1 %collective-permute-done.3.p2 = f32[16,128]{1,0:T(8,128)S(1)} collective-permute-done((f32[16,128]{1,0:T(8,128)S(1)}, f32[16,128]{1,0:T(8,128)S(1)}, u32[]{:S(2)}, u32[]{:S(2)}) %collective-permute-start.3) | collective-permute-done | bytes 8224 | tf_op jit(solution)/shard_map/ppermute | solution.py:370
  16.8 0.5 collective-permute-done.2.p1
  17.3 1.3 %shard_map.88 = (f32[16,40,128]{2,1,0:T(8,128)S(1)}, f32[8,128]{1,0:T(8,128)S(1)}) custom-call(f32[16,128]{1,0:T(8,128)S(1)} %get-tuple-element.38.p0, f32[16,128]{1,0:T(8,128)S(1)} %collective-permute-done.2.p1, f32[16,128]{1,0:T(8,128)S(1)} %collective-permute-done.3.p2, f32[16,128]{1,0:T(8,128)S(1)} %collective-permute-done.4.p3, ...), custom_call_target="tpu_custom_call" | custom-call | flops 134217728 | tf_op jit(solution)/shard_map/pallas_call | solution.py:376
  18.6 16.9 %all_to_all.15.parts = f32[16,40,128]{2,1,0:T(8,128)S(1)} all-to-all(f32[16,40,128]{2,1,0:T(8,128)S(1)} %get-tuple-element.41), channel_id=1, replica_groups=mesh['zy'=16,'core'=2,'x'=4] {'zy'}, dimensions={0} | all-to-all | bytes 655360 | tf_op jit(solution)/shard_map/all_to_all | solution.py:384
  35.5 1.3 %shard_map.89 = (f32[16,128]{1,0:T(8,128)S(1)}, f32[8,128]{1,0:T(8,128)S(1)}) custom-call(f32[16,40,128]{2,1,0:T(8,128)S(1)} %all_to_all.15.parts, f32[32,128]{1,0:T(8,128)S(1)} %get-tuple-element.42.lb, bf16[4096,1024]{1,0:T(8,128)(2,1)S(1)} %get-tuple-element.43.kt_mat, f32[8,128]{1,0:T(8,128)S(1)} %get-tuple-element.44.base), custom_call_target="tpu_custom_call" | custom-call | flops 134217728 | tf_op jit(solution)/shard_map/pallas_call | solution.py:385
  36.8 0.0 collective-permute-start.5
  36.8 1.2 %collective-permute-done.5.received = f32[16,128]{1,0:T(8,128)S(1)} collective-permute-done((f32[16,128]{1,0:T(8,128)S(1)}, f32[16,128]{1,0:T(8,128)S(1)}, u32[]{:S(2)}, u32[]{:S(2)}) %collective-permute-start.5) | collective-permute-done | bytes 8224 | tf_op jit(solution)/shard_map/ppermute | solution.py:393
  38.0 0.9 %collective-permute-start.8 = (f32[16,128]{1,0:T(8,128)S(1)}, f32[16,128]{1,0:T(8,128)S(1)}, u32[]{:S(2)}, u32[]{:S(2)}) collective-permute-start(f32[16,128]{1,0:T(8,128)S(1)} %shard_map.90.p0), channel_id=1, source_target_pairs={{0,3},{1,0},{2,1},{3,2},{4,7},{5,4},{6,5},{7,6},{8,11},{9,8},{10,9... | collective-permute-start | bytes 24584 | tf_op jit(solution)/shard_map/ppermute | solution.py:370
  38.9 1.5 %collective-permute-start.7 = (f32[16,128]{1,0:T(8,128)S(1)}, f32[16,128]{1,0:T(8,128)S(1)}, u32[]{:S(2)}, u32[]{:S(2)}) collective-permute-start(f32[16,128]{1,0:T(8,128)S(1)} %shard_map.90.p0), channel_id=1, source_target_pairs={{0,2},{1,3},{2,0},{3,1},{4,6},{5,7},{6,4},{7,5},{8,10},{9,11},{10,... | collective-permute-start | bytes 24584 | tf_op jit(solution)/shard_map/ppermute | solution.py:370
  40.4 0.6 collective-permute-start.6
  41.0 0.7 collective-permute-done.8.p3
  41.7 2.3 %collective-permute-done.7.p2 = f32[16,128]{1,0:T(8,128)S(1)} collective-permute-done((f32[16,128]{1,0:T(8,128)S(1)}, f32[16,128]{1,0:T(8,128)S(1)}, u32[]{:S(2)}, u32[]{:S(2)}) %collective-permute-start.7) | collective-permute-done | bytes 8224 | tf_op jit(solution)/shard_map/ppermute | solution.py:370
  44.0 1.2 %collective-permute-done.6.p1 = f32[16,128]{1,0:T(8,128)S(1)} collective-permute-done((f32[16,128]{1,0:T(8,128)S(1)}, f32[16,128]{1,0:T(8,128)S(1)}, u32[]{:S(2)}, u32[]{:S(2)}) %collective-permute-start.6) | collective-permute-done | bytes 8224 | tf_op jit(solution)/shard_map/ppermute | solution.py:370
  45.2 2.5 %shard_map.91 = (f32[16,40,128]{2,1,0:T(8,128)S(1)}, bf16[16,128,256]{2,1,0:T(8,128)(2,1)}, f32[8,128]{1,0:T(8,128)S(1)}) custom-call(f32[16,128]{1,0:T(8,128)S(1)} %shard_map.90.p0, f32[16,128]{1,0:T(8,128)S(1)} %collective-permute-done.6.p1, f32[16,128]{1,0:T(8,128)S(1)} %collective-permute-done.7.p2, f32[16,128]{1,0:T(8,128)S(1)} %collective-permute-done.8.p3, ...), custom_call_target="tpu_custom_call" | custom-call | flops 1207959552 | tf_op jit(solution)/shard_map/pallas_call | solution.py:394
  47.8 11.9 %all_to_all.16.parts = f32[16,40,128]{2,1,0:T(8,128)S(1)} all-to-all(f32[16,40,128]{2,1,0:T(8,128)S(1)} %get-tuple-element.47), channel_id=1, replica_groups=mesh['zy'=16,'core'=2,'x'=4] {'zy'}, dimensions={0} | all-to-all | bytes 655360 | tf_op jit(solution)/shard_map/all_to_all | solution.py:401
  59.7 1.7 %shard_map.92 = (bf16[144,512]{1,0:T(8,128)(2,1)S(1)}, bf16[144,512]{1,0:T(8,128)(2,1)S(1)}, f32[32,128]{1,0:T(8,128)S(1)}, f32[32,128]{1,0:T(8,128)S(1)}, f32[8...) custom-call(f32[16,40,128]{2,1,0:T(8,128)S(1)} %all_to_all.16.parts, ...), custom_call_target="tpu_custom_call", output_to_operand_aliasing={{5}: (5, {})} | custom-call | flops 1207959552 | tf_op jit(solution)/shard_map/pallas_call | solution.py:402
  61.3 3.7 %all-to-all-start.2 = ((bf16[16,128,256]{2,1,0:T(8,128)(2,1)}), bf16[16,128,256]{2,1,0:T(8,128)(2,1)S(1)}, u32[]{:S(2)}, u32[]{:S(2)}) async-start(bf16[16,128,256]{2,1,0:T(8,128)(2,1)} %get-tuple-element.54), calls=%async_computation.2 | async-start | bytes 2097152 | tf_op jit(solution)/shard_map/all_to_all | solution.py:419
  65.0 0.1 collective-permute-start.9
  65.1 1.4 %collective-permute-done.9.received = bf16[144,512]{1,0:T(8,128)(2,1)S(1)} collective-permute-done((bf16[144,512]{1,0:T(8,128)(2,1)S(1)}, bf16[144,512]{1,0:T(8,128)(2,1)S(1)}, u32[]{:S(2)}, u32[]{:S(2)}) %collective-permute-start.9) | collective-permute-done | bytes 147488 | tf_op jit(solution)/shard_map/ppermute | solution.py:418
  66.5 0.1 shard_map.93.p0
  66.5 1.2 %collective-permute-start.12 = (bf16[144,512]{1,0:T(8,128)(2,1)S(1)}, bf16[144,512]{1,0:T(8,128)(2,1)S(1)}, u32[]{:S(2)}, u32[]{:S(2)}) collective-permute-start(bf16[144,512]{1,0:T(8,128)(2,1)S(1)} %shard_map.93.p0), channel_id=1, source_target_pairs={{0,3},{1,0},{2,1},{3,2},{4,7},{5,4},{6,5},{7,6},{8,11},{9,8},{10,9... | collective-permute-start | bytes 442376 | tf_op jit(solution)/shard_map/ppermute | solution.py:370
  67.8 0.9 %collective-permute-start.11 = (bf16[144,512]{1,0:T(8,128)(2,1)S(1)}, bf16[144,512]{1,0:T(8,128)(2,1)S(1)}, u32[]{:S(2)}, u32[]{:S(2)}) collective-permute-start(bf16[144,512]{1,0:T(8,128)(2,1)S(1)} %shard_map.93.p0), channel_id=1, source_target_pairs={{0,2},{1,3},{2,0},{3,1},{4,6},{5,7},{6,4},{7,5},{8,10},{9,11},{10,... | collective-permute-start | bytes 442376 | tf_op jit(solution)/shard_map/ppermute | solution.py:370
  68.7 0.1 collective-permute-start.10
  68.8 0.0 collective-permute-start.13
  68.8 4.5 %collective-permute-done.12.p3 = bf16[144,512]{1,0:T(8,128)(2,1)S(1)} collective-permute-done((bf16[144,512]{1,0:T(8,128)(2,1)S(1)}, bf16[144,512]{1,0:T(8,128)(2,1)S(1)}, u32[]{:S(2)}, u32[]{:S(2)}) %collective-permute-start.12) | collective-permute-done | bytes 147488 | tf_op jit(solution)/shard_map/ppermute | solution.py:370
  73.3 2.7 %collective-permute-done.11.p2 = bf16[144,512]{1,0:T(8,128)(2,1)S(1)} collective-permute-done((bf16[144,512]{1,0:T(8,128)(2,1)S(1)}, bf16[144,512]{1,0:T(8,128)(2,1)S(1)}, u32[]{:S(2)}, u32[]{:S(2)}) %collective-permute-start.11) | collective-permute-done | bytes 147488 | tf_op jit(solution)/shard_map/ppermute | solution.py:370
  76.1 2.0 %collective-permute-done.10.p1 = bf16[144,512]{1,0:T(8,128)(2,1)S(1)} collective-permute-done((bf16[144,512]{1,0:T(8,128)(2,1)S(1)}, bf16[144,512]{1,0:T(8,128)(2,1)S(1)}, u32[]{:S(2)}, u32[]{:S(2)}) %collective-permute-start.10) | collective-permute-done | bytes 147488 | tf_op jit(solution)/shard_map/ppermute | solution.py:370
  78.1 1.0 %shard_map.94 = (f32[512,128]{1,0:T(8,128)}, f32[4,128]{1,0:T(4,128)}) custom-call(bf16[144,512]{1,0:T(8,128)(2,1)S(1)} %shard_map.93.p0, bf16[144,512]{1,0:T(8,128)(2,1)S(1)} %collective-permute-done.10.p1, bf16[144,512]{1,0:T(8,128)(2,1)S(1)} %collective-permute-done.11.p2, bf16[144,512]{1,0:T(8,128)(2,1)S(1)} %collective-permute-done.12.p3, ...), custom_call_target="tpu_custom_call" | custom-call | tf_op jit(solution)/shard_map/pallas_call | solution.py:423
  79.0 0.0 collective-permute-done.13.other_pot
  79.0 1.4 %all-to-all-done.2.sums = bf16[16,128,256]{2,1,0:T(8,128)(2,1)S(1)} async-done(((bf16[16,128,256]{2,1,0:T(8,128)(2,1)}), bf16[16,128,256]{2,1,0:T(8,128)(2,1)S(1)}, u32[]{:S(2)}, u32[]{:S(2)}) %all-to-all-start.2) | async-done | bytes 1048608 | tf_op jit(solution)/shard_map/all_to_all | solution.py:419
  80.5 1.1 %shard_map.95 = (f32[256,128]{1,0:T(8,128)}, f32[64,128]{1,0:T(8,128)}) custom-call(bf16[16,128,256]{2,1,0:T(8,128)(2,1)S(1)} %all-to-all-done.2.sums, f32[16,40,128]{2,1,0:T(8,128)S(1)} %all_to_all.16.parts, f32[32,128]{1,0:T(8,128)S(1)} %get-tuple-element.55.total, bf16[128,4096]{1,0:T(8,128)(2,1)S(1)} %get-tuple-element.34.b_t, ...), custom_call_target="tpu_custom_call" | custom-call | tf_op jit(solution)/shard_map/pallas_call | solution.py:426
  (2 shorter events, 0.0 us)
Async XLA Ops:
  0.6 3.1 %collective-permute-start = (bf16[512,128]{1,0:T(8,128)(2,1)}, bf16[512,128]{1,0:T(8,128)(2,1)S(1)}, u32[]{:S(2)}, u32[]{:S(2)}) collective-permute-start(bf16[512,128]{1,0:T(8,128)(2,1)} %desc_a.1), channel_id=1, source_target_pairs={{0,4},{4,0},{1,5},{5,1},{2,6},{6,2},{3,7},{7,3},{8,12},{12,8},{9,1... | collective-permute-start | bytes 393224 | tf_op jit(solution)/shard_map/ppermute | solution.py:329
  7.3 1.3 %collective-permute-start.1 = (f32[24,128]{1,0:T(8,128)S(1)}, f32[24,128]{1,0:T(8,128)S(1)}, u32[]{:S(2)}, u32[]{:S(2)}) collective-permute-start(f32[24,128]{1,0:T(8,128)S(1)} %get-tuple-element.37.own), channel_id=1, source_target_pairs={{0,4},{4,0},{1,5},{5,1},{2,6},{6,2},{3,7},{7,3},{8,12},{12,8},{9,1... | collective-permute-start | bytes 36872 | tf_op jit(solution)/shard_map/ppermute | solution.py:372
  8.7 7.0 %collective-permute-start.4 = (f32[16,128]{1,0:T(8,128)S(1)}, f32[16,128]{1,0:T(8,128)S(1)}, u32[]{:S(2)}, u32[]{:S(2)}) collective-permute-start(f32[16,128]{1,0:T(8,128)S(1)} %get-tuple-element.38.p0), channel_id=1, source_target_pairs={{0,3},{1,0},{2,1},{3,2},{4,7},{5,4},{6,5},{7,6},{8,11},{9,8},{10,9... | collective-permute-start | bytes 24584 | tf_op jit(solution)/shard_map/ppermute | solution.py:370
  11.6 5.2 %collective-permute-start.3 = (f32[16,128]{1,0:T(8,128)S(1)}, f32[16,128]{1,0:T(8,128)S(1)}, u32[]{:S(2)}, u32[]{:S(2)}) collective-permute-start(f32[16,128]{1,0:T(8,128)S(1)} %get-tuple-element.38.p0), channel_id=1, source_target_pairs={{0,2},{1,3},{2,0},{3,1},{4,6},{5,7},{6,4},{7,5},{8,10},{9,11},{10,... | collective-permute-start | bytes 24584 | tf_op jit(solution)/shard_map/ppermute | solution.py:370
  12.4 4.9 %collective-permute-start.2 = (f32[16,128]{1,0:T(8,128)S(1)}, f32[16,128]{1,0:T(8,128)S(1)}, u32[]{:S(2)}, u32[]{:S(2)}) collective-permute-start(f32[16,128]{1,0:T(8,128)S(1)} %get-tuple-element.38.p0), channel_id=1, source_target_pairs={{0,1},{1,2},{2,3},{3,0},{4,5},{5,6},{6,7},{7,4},{8,9},{9,10},{10,1... | collective-permute-start | bytes 24584 | tf_op jit(solution)/shard_map/ppermute | solution.py:370
  36.8 1.2 %collective-permute-start.5 = (f32[16,128]{1,0:T(8,128)S(1)}, f32[16,128]{1,0:T(8,128)S(1)}, u32[]{:S(2)}, u32[]{:S(2)}) collective-permute-start(f32[16,128]{1,0:T(8,128)S(1)} %get-tuple-element.45.own), channel_id=1, source_target_pairs={{0,4},{4,0},{1,5},{5,1},{2,6},{6,2},{3,7},{7,3},{8,12},{12,8},{9,1... | collective-permute-start | bytes 24584 | tf_op jit(solution)/shard_map/ppermute | solution.py:393
  38.0 3.7 %collective-permute-start.8 = (f32[16,128]{1,0:T(8,128)S(1)}, f32[16,128]{1,0:T(8,128)S(1)}, u32[]{:S(2)}, u32[]{:S(2)}) collective-permute-start(f32[16,128]{1,0:T(8,128)S(1)} %shard_map.90.p0), channel_id=1, source_target_pairs={{0,3},{1,0},{2,1},{3,2},{4,7},{5,4},{6,5},{7,6},{8,11},{9,8},{10,9... | collective-permute-start | bytes 24584 | tf_op jit(solution)/shard_map/ppermute | solution.py:370
  38.9 5.2 %collective-permute-start.7 = (f32[16,128]{1,0:T(8,128)S(1)}, f32[16,128]{1,0:T(8,128)S(1)}, u32[]{:S(2)}, u32[]{:S(2)}) collective-permute-start(f32[16,128]{1,0:T(8,128)S(1)} %shard_map.90.p0), channel_id=1, source_target_pairs={{0,2},{1,3},{2,0},{3,1},{4,6},{5,7},{6,4},{7,5},{8,10},{9,11},{10,... | collective-permute-start | bytes 24584 | tf_op jit(solution)/shard_map/ppermute | solution.py:370
  40.4 4.9 %collective-permute-start.6 = (f32[16,128]{1,0:T(8,128)S(1)}, f32[16,128]{1,0:T(8,128)S(1)}, u32[]{:S(2)}, u32[]{:S(2)}) collective-permute-start(f32[16,128]{1,0:T(8,128)S(1)} %shard_map.90.p0), channel_id=1, source_target_pairs={{0,1},{1,2},{2,3},{3,0},{4,5},{5,6},{6,7},{7,4},{8,9},{9,10},{10,1... | collective-permute-start | bytes 24584 | tf_op jit(solution)/shard_map/ppermute | solution.py:370
  61.3 19.1 %all-to-all-start.2 = ((bf16[16,128,256]{2,1,0:T(8,128)(2,1)}), bf16[16,128,256]{2,1,0:T(8,128)(2,1)S(1)}, u32[]{:S(2)}, u32[]{:S(2)}) async-start(bf16[16,128,256]{2,1,0:T(8,128)(2,1)} %get-tuple-element.54), calls=%async_computation.2 | async-start | bytes 2097152 | tf_op jit(solution)/shard_map/all_to_all | solution.py:419
  65.0 1.5 %collective-permute-start.9 = (bf16[144,512]{1,0:T(8,128)(2,1)S(1)}, bf16[144,512]{1,0:T(8,128)(2,1)S(1)}, u32[]{:S(2)}, u32[]{:S(2)}) collective-permute-start(bf16[144,512]{1,0:T(8,128)(2,1)S(1)} %get-tuple-element.51), channel_id=1, source_target_pairs={{0,4},{4,0},{1,5},{5,1},{2,6},{6,2},{3,7},{7,3},{8,12},{12,8},{9,1... | collective-permute-start | bytes 442376 | tf_op jit(solution)/shard_map/ppermute | solution.py:418
  66.5 6.8 %collective-permute-start.12 = (bf16[144,512]{1,0:T(8,128)(2,1)S(1)}, bf16[144,512]{1,0:T(8,128)(2,1)S(1)}, u32[]{:S(2)}, u32[]{:S(2)}) collective-permute-start(bf16[144,512]{1,0:T(8,128)(2,1)S(1)} %shard_map.93.p0), channel_id=1, source_target_pairs={{0,3},{1,0},{2,1},{3,2},{4,7},{5,4},{6,5},{7,6},{8,11},{9,8},{10,9... | collective-permute-start | bytes 442376 | tf_op jit(solution)/shard_map/ppermute | solution.py:370
  67.8 8.3 %collective-permute-start.11 = (bf16[144,512]{1,0:T(8,128)(2,1)S(1)}, bf16[144,512]{1,0:T(8,128)(2,1)S(1)}, u32[]{:S(2)}, u32[]{:S(2)}) collective-permute-start(bf16[144,512]{1,0:T(8,128)(2,1)S(1)} %shard_map.93.p0), channel_id=1, source_target_pairs={{0,2},{1,3},{2,0},{3,1},{4,6},{5,7},{6,4},{7,5},{8,10},{9,11},{10,... | collective-permute-start | bytes 442376 | tf_op jit(solution)/shard_map/ppermute | solution.py:370
  68.7 9.4 %collective-permute-start.10 = (bf16[144,512]{1,0:T(8,128)(2,1)S(1)}, bf16[144,512]{1,0:T(8,128)(2,1)S(1)}, u32[]{:S(2)}, u32[]{:S(2)}) collective-permute-start(bf16[144,512]{1,0:T(8,128)(2,1)S(1)} %shard_map.93.p0), channel_id=1, source_target_pairs={{0,1},{1,2},{2,3},{3,0},{4,5},{5,6},{6,7},{7,4},{8,9},{9,10},{10,1... | collective-permute-start | bytes 442376 | tf_op jit(solution)/shard_map/ppermute | solution.py:370
  68.8 10.2 %collective-permute-start.13 = (f32[32,128]{1,0:T(8,128)S(1)}, f32[32,128]{1,0:T(8,128)S(1)}, u32[]{:S(2)}, u32[]{:S(2)}) collective-permute-start(f32[32,128]{1,0:T(8,128)S(1)} %get-tuple-element.56.own_pot), channel_id=1, source_target_pairs={{0,4},{4,0},{1,5},{5,1},{2,6},{6,2},{3,7},{7,3},{8,12},{12,8},{9,1... | collective-permute-start | bytes 49160 | tf_op jit(solution)/shard_map/ppermute | solution.py:420

commit v4 on v3

--- a/solution.py
+++ b/solution.py
@@ -70,34 +70,39 @@
     return (raw / norm).astype(BF16)
 
 
-def prep_kernel(desc_b, g_all, lb_all, desc_a, la_all, bt_out, at_out, rows_out, shift_out, lb_out, la_out,
-                b_raw, a_raw, g_raw, lb_raw, vec, rows, sems):
+def prep_kernel(desc_b, g_all, lb_all, desc_a, la_all, bt_out, at_out, scale_out, shift_out, lb_out, la_out,
+                b_raw, a_raw, g_raw, lb_raw, vec, sems):
     core = lax.axis_index("core")
-    copies = [
-        pltpu.make_async_copy(g_all, g_raw, sems.at[NK]),
-        pltpu.make_async_copy(desc_a, a_raw, sems.at[NK + 1]),
-        pltpu.make_async_copy(lb_all, lb_raw, sems.at[NK + 2]),
-        pltpu.make_async_copy(la_all, la_out, sems.at[NK + 3]),
+    half = NK // 2
+    load_g = pltpu.make_async_copy(g_all, g_raw, sems.at[0])
+    load_a = pltpu.make_async_copy(desc_a, a_raw, sems.at[1])
+    load_lb = pltpu.make_async_copy(lb_all, lb_raw, sems.at[2])
+    load_la = pltpu.make_async_copy(la_all, la_out, sems.at[3])
+    loads = [
+        pltpu.make_async_copy(desc_b.at[pl.ds(q * half, half), core], b_raw.at[pl.ds(q * half, half)], sems.at[4 + q])
+        for q in range(2)
     ]
-    loads = [pltpu.make_async_copy(desc_b.at[k, core], b_raw.at[k], sems.at[k]) for k in range(NK)]
-    for copy in copies + loads:
+    for copy in (load_g, loads[0], load_a, loads[1], load_lb, load_la):
         copy.start()
-    rows[...] = jnp.zeros_like(rows)
-    for copy in copies:
-        copy.wait()
-    pick_cols(lb_raw, core, lb_out)
+    load_g.wait()
     pick_cols(g_raw, core, vec)
     pot = vec[...] * C2
     shift = jnp.max(jnp.max(pot, axis=0, keepdims=True), axis=1, keepdims=True)
     shift_out[...] = jnp.broadcast_to(shift, (8, 128))
-    split_rows(jnp.exp2(pot - shift + TOP), rows)
-    rows_out[...] = rows[...].astype(BF16)
+    scale = jnp.exp2(pot - shift + TOP)
+    for r in range(32):
+        scale_out[r * 128 : (r + 1) * 128, :] = jnp.broadcast_to(scale[r : r + 1, :], (128, 128)).T
+    load_a.wait()
     for m in range(2):
         span = slice(m * 256, (m + 1) * 256)
         at_out[:, span] = unit_t(a_raw[span, :].T.astype(F32))
-    for k in range(NK):
-        loads[k].wait()
-        bt_out[:, k * CH : (k + 1) * CH] = unit_t(b_raw[k].T.astype(F32))
+    for q in range(2):
+        loads[q].wait()
+        for k in range(q * half, (q + 1) * half):
+            bt_out[:, k * CH : (k + 1) * CH] = unit_t(b_raw[k].T.astype(F32))
+    load_lb.wait()
+    load_la.wait()
+    pick_cols(lb_raw, core, lb_out)
 
 
 def tn(left, right):
@@ -112,16 +117,29 @@
             out[q * 512 : (q + 1) * 512, span] = jnp.exp2(tn(left, right_t[:, span]) * (2.0 * C2)).astype(BF16)
 
 
-def first_kernel(at_own, other_a, la_own, b_t, rows, shift, kt_out, at_out, msg):
+def first_kernel(at_own, other_a, la_own, b_t, scales, shift, kt_out, at_out, msg):
     core = lax.axis_index("core")
     for m in range(2):
         span = slice(m * 256, (m + 1) * 256)
         for half, unit in ((core, at_own[:, span]), (1 - core, unit_t(other_a[span, :].T.astype(F32)))):
             at_out[:, pl.ds(pl.multiple_of(half * 512 + m * 256, 256), 256)] = unit
+    sums = [jnp.zeros((8, 256), F32)] * 4
+    for q in range(NC // 512):
+        here = slice(q * 512, (q + 1) * 512)
+        left = b_t[:, here]
+        scale = jnp.concatenate([scales[here, :], scales[here, :]], axis=1)
+        for m in range(4):
+            span = slice(m * 256, (m + 1) * 256)
+            part = jnp.exp2(tn(left, at_out[:, span]) * (2.0 * C2))
+            kt_out[here, span] = part.astype(BF16)
+            sums[m] = sums[m] + jnp.sum((part * scale).reshape(64, 8, 256), axis=0)
+    for m in range(4):
+        total = jnp.sum(sums[m], axis=0, keepdims=True)
+        msg[2 * m : 2 * m + 1, :] = total[:, 0:128]
+        msg[2 * m + 1 : 2 * m + 2, :] = total[:, 128:256]
+    msg[8:16, :] = shift[...]
     msg[16:20, :] = la_own[...]
     msg[20:24, :] = la_own[...]
-    fill_exponentials(b_t, at_out, kt_out)
-    put_rows(msg, nn(rows[...], kt_out[...]), shift[0:1, :])
 
 
 def put_rows(msg, part, shift):
@@ -231,7 +249,9 @@
 
 
 def row_flow_kernel(parts, lb, kt_mat, base, b_t, held, own_out, other_out, pot_out, total_out, base_out, held_out,
-                    rows, lhs, acc):
+                    rows, lhs, acc, sem):
+    copy = pltpu.make_async_copy(held, held_out, sem)
+    copy.start()
     core = lax.axis_index("core")
     level, total, shift, top = col_scales(parts, lb, rows)
     level_base = base[...] - top
@@ -245,6 +265,7 @@
     for half, out in ((core, own_out), (1 - core, other_out)):
         part = acc[:, pl.ds(pl.multiple_of(half * 512, 512), 512)]
         pack_rows(out, part[0:128, :], part[128:129, :] + part[129:130, :], shift)
+    copy.wait()
 
 
 def merge(parts):
@@ -264,7 +285,7 @@
     pack_rows(out, flow, total, top)
 
 
-def final_a_kernel(p0, p1, p2, p3, at_own, la, base, flow_out, pot_out):
+def final_a(p0, p1, p2, p3, at_own, la, base, flow_out, pot_out):
     flow, total, top = merge([p0, p2, p1, p3])
     flow_t = flow / total
     level = jnp.log2(total) + (top - TOP - 2.0 * C2)
@@ -274,7 +295,13 @@
         pot_out[r : r + 1, :] = (la[r : r + 1, :] * LOG2E - level[:, here] - base[0:1, :]) * (1.0 / C2)
 
 
-def final_b_kernel(sums, parts, total, b_t, own_pot, other_pot, flow_out, pot_out):
+def final_kernel(p0, p1, p2, p3, at_own, la, base, sums, parts, total, b_t, own_pot, other_pot,
+                 flow_a, pot_a, flow_b, pot_b):
+    final_a(p0, p1, p2, p3, at_own, la, base, flow_a, pot_a)
+    final_b(sums, parts, total, b_t, own_pot, other_pot, flow_b, pot_b)
+
+
+def final_b(sums, parts, total, b_t, own_pot, other_pot, flow_out, pot_out):
     core = lax.axis_index("core")
     chunk = lax.axis_index("zy")
     shifts = [parts[d, 32:40, :] for d in range(NZY)]
@@ -302,15 +329,13 @@
 
 VM = pl.BlockSpec(memory_space=pltpu.VMEM)
 HB = pl.BlockSpec(memory_space=pltpu.HBM)
-ANY = pl.BlockSpec(memory_space=pl.ANY)
-
-
-def call(kernel, ins, outs, scratch=(), flops=0, bytes_accessed=0, trans=0, passes=None):
+
+
+def call(kernel, ins, outs, scratch=(), flops=0, bytes_accessed=0, trans=0, outside=()):
     return pl.pallas_call(
         kernel,
         in_specs=ins,
-        out_specs=[ANY if i in (passes or {}).values() else VM for i in range(len(outs))],
-        input_output_aliases=passes or {},
+        out_specs=[HB if i in outside else VM for i in range(len(outs))],
         out_shape=outs,
         scratch_shapes=list(scratch),
         compiler_params=pltpu.CompilerParams(vmem_limit_bytes=16 * 1024 * 1024),
@@ -328,13 +353,13 @@
     stay = lambda x: pltpu.with_memory_space_constraint(x, pltpu.HBM)
     other_a = lax.ppermute(desc_a, "core", swap)
 
-    b_t, at_own, rows, shift, lb, la_own = call(
+    b_t, at_own, scales, shift, lb, la_own = call(
         prep_kernel,
         [HB] * 5,
         [
             sds(DIM, NC, dtype=BF16),
             sds(DIM, 512, dtype=BF16),
-            sds(16, NC, dtype=BF16),
+            sds(NC, 128),
             sds(8, 128),
             sds(32, 128),
             sds(4, 128),
@@ -345,8 +370,7 @@
             pltpu.VMEM((64, 128), F32),
             pltpu.VMEM((64, 128), F32),
             pltpu.VMEM((32, 128), F32),
-            pltpu.VMEM((16, NC), F32),
-            pltpu.SemaphoreType.DMA((NK + 4,)),
+            pltpu.SemaphoreType.DMA((6,)),
         ],
         flops=8 * NC * DIM,
         bytes_accessed=2 * NC * DIM,
@@ -364,7 +388,7 @@
         [pltpu.VMEM((NC, NR), BF16), sds(DIM, NR, dtype=BF16), sds(24, 128)],
         flops=2 * PASS * DIM,
         trans=PASS,
-    )(at_own, other_a, la_own, b_t, rows, shift)
+    )(at_own, other_a, la_own, b_t, scales, shift)
 
     def over_x(pair):
         return [pair] + [lax.ppermute(pair, "x", ring[s]) for s in (1, 2, 3)]
@@ -394,38 +418,35 @@
     msg, sums, base = call(
         last_col_kernel,
         [VM] * 8,
-        [sds(NZY, 40, 128), sds(NZY, DIM, CH, dtype=BF16), sds(8, 128)],
+        [sds(NZY, 40, 128), pltpu.VMEM((NZY, DIM, CH), BF16), sds(8, 128)],
         [pltpu.VMEM((16, NR), F32), pltpu.VMEM((144, NR), BF16)],
         flops=2 * PASS * 144,
     )(*over_x(pair), la, keep(k_mat), base, a_t)
     parts = lax.all_to_all(msg, "zy", 0, 0)
     own, other, own_pot, total, base, sums = call(
         row_flow_kernel,
-        [VM] * 5 + [ANY],
+        [VM] * 6,
         [
             sds(144, 512, dtype=BF16),
             sds(144, 512, dtype=BF16),
             sds(32, 128),
             sds(32, 128),
             sds(8, 128),
-            sds(NZY, DIM, CH, dtype=BF16),
+            pltpu.HBM((NZY, DIM, CH), BF16),
         ],
-        [pltpu.VMEM((16, NC), F32), pltpu.VMEM((144, NC), BF16), pltpu.VMEM((144, NR), F32)],
+        [pltpu.VMEM((16, NC), F32), pltpu.VMEM((144, NC), BF16), pltpu.VMEM((144, NR), F32), pltpu.SemaphoreType.DMA],
         flops=2 * PASS * 144,
-        passes={5: 5},
-    )(parts, lb, keep(kt_mat), base, b_t, sums)
+        outside=(5,),
+    )(parts, lb, keep(kt_mat), base, b_t, keep(sums))
 
     received = lax.ppermute(other, "core", swap)
     sums = lax.all_to_all(sums, "zy", 0, 0)
     other_pot = lax.ppermute(own_pot, "core", swap)
     mine = call(merge_kernel, [VM] * 2, [sds(144, 512, dtype=BF16)])(own, received)[0]
     others = over_x(mine)[1:]
-    flow_a, pot_a = call(
-        final_a_kernel, [VM] * 7, [sds(512, DIM), sds(4, 128)]
-    )(mine, *others, at_own, la_own, base)
-    flow_b, pot_b = call(
-        final_b_kernel, [VM] * 6, [sds(CH, DIM), sds(64, 128)]
-    )(sums, parts, total, b_t, own_pot, other_pot)
+    flow_a, pot_a, flow_b, pot_b = call(
+        final_kernel, [VM] * 13, [sds(512, DIM), sds(4, 128), sds(CH, DIM), sds(64, 128)]
+    )(mine, *others, at_own, la_own, base, sums, parts, total, b_t, own_pot, other_pot)
     return (pot_a.reshape(512), pot_b.reshape(8192), flow_a, flow_b)
 
 

time: 81.8 us -> 80 us (0.978)
  Pallas kernels: 17.9 us -> 15.1 us
  waiting for transfers between devices: 19.8 us -> 20.8 us
    pallas_call x4 -> x3, Pallas kernels: 6.22 us -> 4.45 us  [the longest x1 1.68 us: on_device(): call(row_flow_kernel, [VM] * 6, [sds(144, 512, dtype=BF16), sds(144, 512,...]
    ppermute x9, waiting for transfers between devices: 15.1 us -> 13.9 us  [over_x(): return [pair] + [lax.ppermute(pair, 'x', ring[s]) for s in (1, 2, 3)]]
    ppermute x1, waiting for transfers between devices: 0.01 us -> 1.18 us  [on_device(): other_pot = lax.ppermute(own_pot, 'core', swap)]
    all_to_all x1, waiting for transfers between devices: 1.4 us -> 2.35 us  [on_device(): sums = lax.all_to_all(sums, 'zy', 0, 0)]
  transfers between devices with their start and end apart: 15 -> 15, of which waited for: 12 -> 13; matrix products, arithmetic and copies ran while one was open for 0% -> 0% of each run, Pallas kernels for 8% -> 6%
where the time goes in v4:
time: 80 us; the launch traced here: 79.7 us
  blocking collectives  28.8 us (36%)
  waiting for transfers between devices  20.8 us (26%)
  Pallas kernels  15.1 us (19%)
  starting transfers between devices  14.3 us (18%)
    all_to_all x2, blocking collectives, on_device(): parts = lax.all_to_all(msg, 'zy', 0, 0)  28.8 us
    ppermute x9, waiting for transfers between devices, over_x(): return [pair] + [lax.ppermute(pair, 'x', ring[s]) for s in (1, 2, 3)]  13.9 us
    ppermute x9, starting transfers between devices, over_x(): return [pair] + [lax.ppermute(pair, 'x', ring[s]) for s in (1, 2, 3)]  9.91 us
    all_to_all x1, starting transfers between devices, on_device(): sums = lax.all_to_all(sums, 'zy', 0, 0)  3.66 us
    pallas_call x1, Pallas kernels, on_device(): call(first_kernel, [VM] * 6, [pltpu.VMEM((NC, NR), BF16), sds(DIM, NR, dt...  3.31 us
    pallas_call x1, Pallas kernels, on_device(): call(kernel_matrix, [VM] * 2, [pltpu.VMEM((NR, NC), BF16)], flops=2 * PAS...  2.37 us
    all_to_all x1, waiting for transfers between devices, on_device(): sums = lax.all_to_all(sums, 'zy', 0, 0)  2.35 us
    pallas_call x1, Pallas kernels, on_device(): call(prep_kernel, [HB] * 5, [sds(DIM, NC, dtype=BF16), sds(DIM, 512, dtyp...  2.25 us
  transfers between devices with their start and end apart: 15, of which 13 were waited for; matrix products, arithmetic and copies ran while one was open for 0% of the time, Pallas kernels for 6%

profile of v4, /device:TPU:0, one launch (start us, length us, event | category | flops | bytes accessed | tf_op | source)
XLA Modules:
  0.0 79.7 jit_solution(5067528754410022593)
XLA Ops:
  0.6 0.1 collective-permute-start
  0.7 2.3 %shard_map.84 = (bf16[128,4096]{1,0:T(8,128)(2,1)S(1)}, bf16[128,512]{1,0:T(8,128)(2,1)S(1)}, f32[4096,128]{1,0:T(8,128)S(1)}, f32[8,128]{1,0:T(8,128)S(1)}, f32...) custom-call(bf16[16,2,256,128]{3,2,1,0:T(8,128)(2,1)} %bitcast.6, f32[64,128]{1,0:T(8,128)} %bitcast.7, f32[64,128]{1,0:T(8,128)} %bitcast.8, ...), custom_call_target="tpu_custom_call" | custom-call | flops 4194304 | bytes 1048576 | tf_op jit(solution)/shard_map/pallas_call | solution.py:356
  3.0 0.0 collective-permute-done.other_a
  3.0 3.3 %shard_map.85 = (bf16[4096,1024]{1,0:T(8,128)(2,1)S(1)}, bf16[128,1024]{1,0:T(8,128)(2,1)S(1)}, f32[24,128]{1,0:T(8,128)S(1)}) custom-call(bf16[128,512]{1,0:T(8,128)(2,1)S(1)} %get-tuple-element.32.at_own, bf16[512,128]{1,0:T(8,128)(2,1)S(1)} %collective-permute-done.other_a, f32[4,128]{1,0:T(4,128)S(1)} %get-tuple-element.33.la_own.la, ...), custom_call_target="tpu_custom_call" | custom-call | flops 1073741824 | tf_op jit(solution)/shard_map/pallas_call | solution.py:385
  6.3 0.5 collective-permute-start.1
  6.9 0.8 %collective-permute-done.1.received = f32[24,128]{1,0:T(8,128)S(1)} collective-permute-done((f32[24,128]{1,0:T(8,128)S(1)}, f32[24,128]{1,0:T(8,128)S(1)}, u32[]{:S(2)}, u32[]{:S(2)}) %collective-permute-start.1) | collective-permute-done | bytes 12320 | tf_op jit(solution)/shard_map/ppermute | solution.py:396
  7.7 2.9 %collective-permute-start.4 = (f32[16,128]{1,0:T(8,128)S(1)}, f32[16,128]{1,0:T(8,128)S(1)}, u32[]{:S(2)}, u32[]{:S(2)}) collective-permute-start(f32[16,128]{1,0:T(8,128)S(1)} %get-tuple-element.38.p0), channel_id=1, source_target_pairs={{0,3},{1,0},{2,1},{3,2},{4,7},{5,4},{6,5},{7,6},{8,11},{9,8},{10,9... | collective-permute-start | bytes 24584 | tf_op jit(solution)/shard_map/ppermute | solution.py:394
  10.6 0.8 %collective-permute-start.3 = (f32[16,128]{1,0:T(8,128)S(1)}, f32[16,128]{1,0:T(8,128)S(1)}, u32[]{:S(2)}, u32[]{:S(2)}) collective-permute-start(f32[16,128]{1,0:T(8,128)S(1)} %get-tuple-element.38.p0), channel_id=1, source_target_pairs={{0,2},{1,3},{2,0},{3,1},{4,6},{5,7},{6,4},{7,5},{8,10},{9,11},{10,... | collective-permute-start | bytes 24584 | tf_op jit(solution)/shard_map/ppermute | solution.py:394
  11.4 0.9 %collective-permute-start.2 = (f32[16,128]{1,0:T(8,128)S(1)}, f32[16,128]{1,0:T(8,128)S(1)}, u32[]{:S(2)}, u32[]{:S(2)}) collective-permute-start(f32[16,128]{1,0:T(8,128)S(1)} %get-tuple-element.38.p0), channel_id=1, source_target_pairs={{0,1},{1,2},{2,3},{3,0},{4,5},{5,6},{6,7},{7,4},{8,9},{9,10},{10,1... | collective-permute-start | bytes 24584 | tf_op jit(solution)/shard_map/ppermute | solution.py:394
  12.3 2.4 %shard_map.87.k_mat = bf16[1024,4096]{1,0:T(8,128)(2,1)S(1)} custom-call(bf16[128,1024]{1,0:T(8,128)(2,1)S(1)} %get-tuple-element.40.a_t, bf16[128,4096]{1,0:T(8,128)(2,1)S(1)} %get-tuple-element.34.b_t), custom_call_target="tpu_custom_call" | custom-call | flops 1073741824 | tf_op jit(solution)/shard_map/pallas_call | solution.py:397
  14.7 0.0 collective-permute-done.4.p3
  14.7 1.1 %collective-permute-done.3.p2 = f32[16,128]{1,0:T(8,128)S(1)} collective-permute-done((f32[16,128]{1,0:T(8,128)S(1)}, f32[16,128]{1,0:T(8,128)S(1)}, u32[]{:S(2)}, u32[]{:S(2)}) %collective-permute-start.3) | collective-permute-done | bytes 8224 | tf_op jit(solution)/shard_map/ppermute | solution.py:394
  15.8 0.5 collective-permute-done.2.p1
  16.3 1.3 %shard_map.88 = (f32[16,40,128]{2,1,0:T(8,128)S(1)}, f32[8,128]{1,0:T(8,128)S(1)}) custom-call(f32[16,128]{1,0:T(8,128)S(1)} %get-tuple-element.38.p0, f32[16,128]{1,0:T(8,128)S(1)} %collective-permute-done.2.p1, f32[16,128]{1,0:T(8,128)S(1)} %collective-permute-done.3.p2, f32[16,128]{1,0:T(8,128)S(1)} %collective-permute-done.4.p3, ...), custom_call_target="tpu_custom_call" | custom-call | flops 134217728 | tf_op jit(solution)/shard_map/pallas_call | solution.py:400
  17.6 16.9 %all_to_all.15.parts = f32[16,40,128]{2,1,0:T(8,128)S(1)} all-to-all(f32[16,40,128]{2,1,0:T(8,128)S(1)} %get-tuple-element.41), channel_id=1, replica_groups=mesh['zy'=16,'core'=2,'x'=4] {'zy'}, dimensions={0} | all-to-all | bytes 655360 | tf_op jit(solution)/shard_map/all_to_all | solution.py:408
  34.5 1.3 %shard_map.89 = (f32[16,128]{1,0:T(8,128)S(1)}, f32[8,128]{1,0:T(8,128)S(1)}) custom-call(f32[16,40,128]{2,1,0:T(8,128)S(1)} %all_to_all.15.parts, f32[32,128]{1,0:T(8,128)S(1)} %get-tuple-element.42.lb, bf16[4096,1024]{1,0:T(8,128)(2,1)S(1)} %get-tuple-element.43.kt_mat, f32[8,128]{1,0:T(8,128)S(1)} %get-tuple-element.44.base), custom_call_target="tpu_custom_call" | custom-call | flops 134217728 | tf_op jit(solution)/shard_map/pallas_call | solution.py:409
  35.8 0.0 collective-permute-start.5
  35.8 1.2 %collective-permute-done.5.received = f32[16,128]{1,0:T(8,128)S(1)} collective-permute-done((f32[16,128]{1,0:T(8,128)S(1)}, f32[16,128]{1,0:T(8,128)S(1)}, u32[]{:S(2)}, u32[]{:S(2)}) %collective-permute-start.5) | collective-permute-done | bytes 8224 | tf_op jit(solution)/shard_map/ppermute | solution.py:417
  37.0 0.9 %collective-permute-start.8 = (f32[16,128]{1,0:T(8,128)S(1)}, f32[16,128]{1,0:T(8,128)S(1)}, u32[]{:S(2)}, u32[]{:S(2)}) collective-permute-start(f32[16,128]{1,0:T(8,128)S(1)} %shard_map.90.p0), channel_id=1, source_target_pairs={{0,3},{1,0},{2,1},{3,2},{4,7},{5,4},{6,5},{7,6},{8,11},{9,8},{10,9... | collective-permute-start | bytes 24584 | tf_op jit(solution)/shard_map/ppermute | solution.py:394
  37.9 1.5 %collective-permute-start.7 = (f32[16,128]{1,0:T(8,128)S(1)}, f32[16,128]{1,0:T(8,128)S(1)}, u32[]{:S(2)}, u32[]{:S(2)}) collective-permute-start(f32[16,128]{1,0:T(8,128)S(1)} %shard_map.90.p0), channel_id=1, source_target_pairs={{0,2},{1,3},{2,0},{3,1},{4,6},{5,7},{6,4},{7,5},{8,10},{9,11},{10,... | collective-permute-start | bytes 24584 | tf_op jit(solution)/shard_map/ppermute | solution.py:394
  39.4 0.6 collective-permute-start.6
  40.0 0.7 collective-permute-done.8.p3
  40.7 2.3 %collective-permute-done.7.p2 = f32[16,128]{1,0:T(8,128)S(1)} collective-permute-done((f32[16,128]{1,0:T(8,128)S(1)}, f32[16,128]{1,0:T(8,128)S(1)}, u32[]{:S(2)}, u32[]{:S(2)}) %collective-permute-start.7) | collective-permute-done | bytes 8224 | tf_op jit(solution)/shard_map/ppermute | solution.py:394
  43.0 1.2 %collective-permute-done.6.p1 = f32[16,128]{1,0:T(8,128)S(1)} collective-permute-done((f32[16,128]{1,0:T(8,128)S(1)}, f32[16,128]{1,0:T(8,128)S(1)}, u32[]{:S(2)}, u32[]{:S(2)}) %collective-permute-start.6) | collective-permute-done | bytes 8224 | tf_op jit(solution)/shard_map/ppermute | solution.py:394
  44.2 1.5 %shard_map.91 = (f32[16,40,128]{2,1,0:T(8,128)S(1)}, bf16[16,128,256]{2,1,0:T(8,128)(2,1)S(1)}, f32[8,128]{1,0:T(8,128)S(1)}) custom-call(f32[16,128]{1,0:T(8,128)S(1)} %shard_map.90.p0, f32[16,128]{1,0:T(8,128)S(1)} %collective-permute-done.6.p1, f32[16,128]{1,0:T(8,128)S(1)} %collective-permute-done.7.p2, f32[16,128]{1,0:T(8,128)S(1)} %collective-permute-done.8.p3, ...), custom_call_target="tpu_custom_call" | custom-call | flops 1207959552 | tf_op jit(solution)/shard_map/pallas_call | solution.py:418
  45.8 11.9 %all_to_all.16.parts = f32[16,40,128]{2,1,0:T(8,128)S(1)} all-to-all(f32[16,40,128]{2,1,0:T(8,128)S(1)} %get-tuple-element.47), channel_id=1, replica_groups=mesh['zy'=16,'core'=2,'x'=4] {'zy'}, dimensions={0} | all-to-all | bytes 655360 | tf_op jit(solution)/shard_map/all_to_all | solution.py:425
  57.7 1.7 %shard_map.92 = (bf16[144,512]{1,0:T(8,128)(2,1)S(1)}, bf16[144,512]{1,0:T(8,128)(2,1)S(1)}, f32[32,128]{1,0:T(8,128)S(1)}, f32[32,128]{1,0:T(8,128)S(1)}, f32[8...) custom-call(f32[16,40,128]{2,1,0:T(8,128)S(1)} %all_to_all.16.parts, f32[32,128]{1,0:T(8,128)S(1)} %get-tuple-element.42.lb, ...), custom_call_target="tpu_custom_call" | custom-call | flops 1207959552 | tf_op jit(solution)/shard_map/pallas_call | solution.py:426
  59.4 3.7 %all-to-all-start.2 = ((bf16[16,128,256]{2,1,0:T(8,128)(2,1)}), bf16[16,128,256]{2,1,0:T(8,128)(2,1)S(1)}, u32[]{:S(2)}, u32[]{:S(2)}) async-start(bf16[16,128,256]{2,1,0:T(8,128)(2,1)} %get-tuple-element.53), calls=%async_computation.2 | async-start | bytes 2097152 | tf_op jit(solution)/shard_map/all_to_all | solution.py:443
  63.1 0.1 collective-permute-start.9
  63.1 1.4 %collective-permute-done.9.received = bf16[144,512]{1,0:T(8,128)(2,1)S(1)} collective-permute-done((bf16[144,512]{1,0:T(8,128)(2,1)S(1)}, bf16[144,512]{1,0:T(8,128)(2,1)S(1)}, u32[]{:S(2)}, u32[]{:S(2)}) %collective-permute-start.9) | collective-permute-done | bytes 147488 | tf_op jit(solution)/shard_map/ppermute | solution.py:442
  64.5 0.1 shard_map.93.p0
  64.6 1.3 %collective-permute-start.12 = (bf16[144,512]{1,0:T(8,128)(2,1)S(1)}, bf16[144,512]{1,0:T(8,128)(2,1)S(1)}, u32[]{:S(2)}, u32[]{:S(2)}) collective-permute-start(bf16[144,512]{1,0:T(8,128)(2,1)S(1)} %shard_map.93.p0), channel_id=1, source_target_pairs={{0,3},{1,0},{2,1},{3,2},{4,7},{5,4},{6,5},{7,6},{8,11},{9,8},{10,9... | collective-permute-start | bytes 442376 | tf_op jit(solution)/shard_map/ppermute | solution.py:394
  65.9 0.9 %collective-permute-start.11 = (bf16[144,512]{1,0:T(8,128)(2,1)S(1)}, bf16[144,512]{1,0:T(8,128)(2,1)S(1)}, u32[]{:S(2)}, u32[]{:S(2)}) collective-permute-start(bf16[144,512]{1,0:T(8,128)(2,1)S(1)} %shard_map.93.p0), channel_id=1, source_target_pairs={{0,2},{1,3},{2,0},{3,1},{4,6},{5,7},{6,4},{7,5},{8,10},{9,11},{10,... | collective-permute-start | bytes 442376 | tf_op jit(solution)/shard_map/ppermute | solution.py:394
  66.8 0.1 collective-permute-start.10
  66.9 0.0 collective-permute-start.13
  66.9 1.2 %collective-permute-done.13.other_pot = f32[32,128]{1,0:T(8,128)S(1)} collective-permute-done((f32[32,128]{1,0:T(8,128)S(1)}, f32[32,128]{1,0:T(8,128)S(1)}, u32[]{:S(2)}, u32[]{:S(2)}) %collective-permute-start.13) | collective-permute-done | bytes 16416 | tf_op jit(solution)/shard_map/ppermute | solution.py:444
  68.1 3.3 %collective-permute-done.12.p3 = bf16[144,512]{1,0:T(8,128)(2,1)S(1)} collective-permute-done((bf16[144,512]{1,0:T(8,128)(2,1)S(1)}, bf16[144,512]{1,0:T(8,128)(2,1)S(1)}, u32[]{:S(2)}, u32[]{:S(2)}) %collective-permute-start.12) | collective-permute-done | bytes 147488 | tf_op jit(solution)/shard_map/ppermute | solution.py:394
  71.4 2.8 %collective-permute-done.11.p2 = bf16[144,512]{1,0:T(8,128)(2,1)S(1)} collective-permute-done((bf16[144,512]{1,0:T(8,128)(2,1)S(1)}, bf16[144,512]{1,0:T(8,128)(2,1)S(1)}, u32[]{:S(2)}, u32[]{:S(2)}) %collective-permute-start.11) | collective-permute-done | bytes 147488 | tf_op jit(solution)/shard_map/ppermute | solution.py:394
  74.1 2.0 %collective-permute-done.10.p1 = bf16[144,512]{1,0:T(8,128)(2,1)S(1)} collective-permute-done((bf16[144,512]{1,0:T(8,128)(2,1)S(1)}, bf16[144,512]{1,0:T(8,128)(2,1)S(1)}, u32[]{:S(2)}, u32[]{:S(2)}) %collective-permute-start.10) | collective-permute-done | bytes 147488 | tf_op jit(solution)/shard_map/ppermute | solution.py:394
  76.1 2.4 %all-to-all-done.2.sums = bf16[16,128,256]{2,1,0:T(8,128)(2,1)S(1)} async-done(((bf16[16,128,256]{2,1,0:T(8,128)(2,1)}), bf16[16,128,256]{2,1,0:T(8,128)(2,1)S(1)}, u32[]{:S(2)}, u32[]{:S(2)}) %all-to-all-start.2) | async-done | bytes 1048608 | tf_op jit(solution)/shard_map/all_to_all | solution.py:443
  78.5 1.2 %shard_map.94 = (f32[512,128]{1,0:T(8,128)}, f32[4,128]{1,0:T(4,128)}, f32[256,128]{1,0:T(8,128)}, f32[64,128]{1,0:T(8,128)}) custom-call(bf16[144,512]{1,0:T(8,128)(2,1)S(1)} %shard_map.93.p0, bf16[144,512]{1,0:T(8,128)(2,1)S(1)} %collective-permute-done.10.p1, bf16[144,512]{1,0:T(8,128)(2,1)S(1)} %collective-permute-done.11.p2, ...), custom_call_target="tpu_custom_call" | custom-call | tf_op jit(solution)/shard_map/pallas_call | solution.py:447
  (2 shorter events, 0.0 us)
Async XLA Ops:
  0.6 2.4 %collective-permute-start = (bf16[512,128]{1,0:T(8,128)(2,1)}, bf16[512,128]{1,0:T(8,128)(2,1)S(1)}, u32[]{:S(2)}, u32[]{:S(2)}) collective-permute-start(bf16[512,128]{1,0:T(8,128)(2,1)} %desc_a.1), channel_id=1, source_target_pairs={{0,4},{4,0},{1,5},{5,1},{2,6},{6,2},{3,7},{7,3},{8,12},{12,8},{9,1... | collective-permute-start | bytes 393224 | tf_op jit(solution)/shard_map/ppermute | solution.py:354
  6.3 1.4 %collective-permute-start.1 = (f32[24,128]{1,0:T(8,128)S(1)}, f32[24,128]{1,0:T(8,128)S(1)}, u32[]{:S(2)}, u32[]{:S(2)}) collective-permute-start(f32[24,128]{1,0:T(8,128)S(1)} %get-tuple-element.37.own), channel_id=1, source_target_pairs={{0,4},{4,0},{1,5},{5,1},{2,6},{6,2},{3,7},{7,3},{8,12},{12,8},{9,1... | collective-permute-start | bytes 36872 | tf_op jit(solution)/shard_map/ppermute | solution.py:396
  7.7 7.0 %collective-permute-start.4 = (f32[16,128]{1,0:T(8,128)S(1)}, f32[16,128]{1,0:T(8,128)S(1)}, u32[]{:S(2)}, u32[]{:S(2)}) collective-permute-start(f32[16,128]{1,0:T(8,128)S(1)} %get-tuple-element.38.p0), channel_id=1, source_target_pairs={{0,3},{1,0},{2,1},{3,2},{4,7},{5,4},{6,5},{7,6},{8,11},{9,8},{10,9... | collective-permute-start | bytes 24584 | tf_op jit(solution)/shard_map/ppermute | solution.py:394
  10.6 5.2 %collective-permute-start.3 = (f32[16,128]{1,0:T(8,128)S(1)}, f32[16,128]{1,0:T(8,128)S(1)}, u32[]{:S(2)}, u32[]{:S(2)}) collective-permute-start(f32[16,128]{1,0:T(8,128)S(1)} %get-tuple-element.38.p0), channel_id=1, source_target_pairs={{0,2},{1,3},{2,0},{3,1},{4,6},{5,7},{6,4},{7,5},{8,10},{9,11},{10,... | collective-permute-start | bytes 24584 | tf_op jit(solution)/shard_map/ppermute | solution.py:394
  11.4 4.9 %collective-permute-start.2 = (f32[16,128]{1,0:T(8,128)S(1)}, f32[16,128]{1,0:T(8,128)S(1)}, u32[]{:S(2)}, u32[]{:S(2)}) collective-permute-start(f32[16,128]{1,0:T(8,128)S(1)} %get-tuple-element.38.p0), channel_id=1, source_target_pairs={{0,1},{1,2},{2,3},{3,0},{4,5},{5,6},{6,7},{7,4},{8,9},{9,10},{10,1... | collective-permute-start | bytes 24584 | tf_op jit(solution)/shard_map/ppermute | solution.py:394
  35.8 1.2 %collective-permute-start.5 = (f32[16,128]{1,0:T(8,128)S(1)}, f32[16,128]{1,0:T(8,128)S(1)}, u32[]{:S(2)}, u32[]{:S(2)}) collective-permute-start(f32[16,128]{1,0:T(8,128)S(1)} %get-tuple-element.45.own), channel_id=1, source_target_pairs={{0,4},{4,0},{1,5},{5,1},{2,6},{6,2},{3,7},{7,3},{8,12},{12,8},{9,1... | collective-permute-start | bytes 24584 | tf_op jit(solution)/shard_map/ppermute | solution.py:417
  37.0 3.7 %collective-permute-start.8 = (f32[16,128]{1,0:T(8,128)S(1)}, f32[16,128]{1,0:T(8,128)S(1)}, u32[]{:S(2)}, u32[]{:S(2)}) collective-permute-start(f32[16,128]{1,0:T(8,128)S(1)} %shard_map.90.p0), channel_id=1, source_target_pairs={{0,3},{1,0},{2,1},{3,2},{4,7},{5,4},{6,5},{7,6},{8,11},{9,8},{10,9... | collective-permute-start | bytes 24584 | tf_op jit(solution)/shard_map/ppermute | solution.py:394
  37.9 5.2 %collective-permute-start.7 = (f32[16,128]{1,0:T(8,128)S(1)}, f32[16,128]{1,0:T(8,128)S(1)}, u32[]{:S(2)}, u32[]{:S(2)}) collective-permute-start(f32[16,128]{1,0:T(8,128)S(1)} %shard_map.90.p0), channel_id=1, source_target_pairs={{0,2},{1,3},{2,0},{3,1},{4,6},{5,7},{6,4},{7,5},{8,10},{9,11},{10,... | collective-permute-start | bytes 24584 | tf_op jit(solution)/shard_map/ppermute | solution.py:394
  39.4 4.9 %collective-permute-start.6 = (f32[16,128]{1,0:T(8,128)S(1)}, f32[16,128]{1,0:T(8,128)S(1)}, u32[]{:S(2)}, u32[]{:S(2)}) collective-permute-start(f32[16,128]{1,0:T(8,128)S(1)} %shard_map.90.p0), channel_id=1, source_target_pairs={{0,1},{1,2},{2,3},{3,0},{4,5},{5,6},{6,7},{7,4},{8,9},{9,10},{10,1... | collective-permute-start | bytes 24584 | tf_op jit(solution)/shard_map/ppermute | solution.py:394
  59.4 19.1 %all-to-all-start.2 = ((bf16[16,128,256]{2,1,0:T(8,128)(2,1)}), bf16[16,128,256]{2,1,0:T(8,128)(2,1)S(1)}, u32[]{:S(2)}, u32[]{:S(2)}) async-start(bf16[16,128,256]{2,1,0:T(8,128)(2,1)} %get-tuple-element.53), calls=%async_computation.2 | async-start | bytes 2097152 | tf_op jit(solution)/shard_map/all_to_all | solution.py:443
  63.1 1.5 %collective-permute-start.9 = (bf16[144,512]{1,0:T(8,128)(2,1)S(1)}, bf16[144,512]{1,0:T(8,128)(2,1)S(1)}, u32[]{:S(2)}, u32[]{:S(2)}) collective-permute-start(bf16[144,512]{1,0:T(8,128)(2,1)S(1)} %get-tuple-element.51), channel_id=1, source_target_pairs={{0,4},{4,0},{1,5},{5,1},{2,6},{6,2},{3,7},{7,3},{8,12},{12,8},{9,1... | collective-permute-start | bytes 442376 | tf_op jit(solution)/shard_map/ppermute | solution.py:442
  64.6 6.8 %collective-permute-start.12 = (bf16[144,512]{1,0:T(8,128)(2,1)S(1)}, bf16[144,512]{1,0:T(8,128)(2,1)S(1)}, u32[]{:S(2)}, u32[]{:S(2)}) collective-permute-start(bf16[144,512]{1,0:T(8,128)(2,1)S(1)} %shard_map.93.p0), channel_id=1, source_target_pairs={{0,3},{1,0},{2,1},{3,2},{4,7},{5,4},{6,5},{7,6},{8,11},{9,8},{10,9... | collective-permute-start | bytes 442376 | tf_op jit(solution)/shard_map/ppermute | solution.py:394
  65.9 8.3 %collective-permute-start.11 = (bf16[144,512]{1,0:T(8,128)(2,1)S(1)}, bf16[144,512]{1,0:T(8,128)(2,1)S(1)}, u32[]{:S(2)}, u32[]{:S(2)}) collective-permute-start(bf16[144,512]{1,0:T(8,128)(2,1)S(1)} %shard_map.93.p0), channel_id=1, source_target_pairs={{0,2},{1,3},{2,0},{3,1},{4,6},{5,7},{6,4},{7,5},{8,10},{9,11},{10,... | collective-permute-start | bytes 442376 | tf_op jit(solution)/shard_map/ppermute | solution.py:394
  66.8 9.4 %collective-permute-start.10 = (bf16[144,512]{1,0:T(8,128)(2,1)S(1)}, bf16[144,512]{1,0:T(8,128)(2,1)S(1)}, u32[]{:S(2)}, u32[]{:S(2)}) collective-permute-start(bf16[144,512]{1,0:T(8,128)(2,1)S(1)} %shard_map.93.p0), channel_id=1, source_target_pairs={{0,1},{1,2},{2,3},{3,0},{4,5},{5,6},{6,7},{7,4},{8,9},{9,10},{10,1... | collective-permute-start | bytes 442376 | tf_op jit(solution)/shard_map/ppermute | solution.py:394
  66.9 1.2 %collective-permute-start.13 = (f32[32,128]{1,0:T(8,128)S(1)}, f32[32,128]{1,0:T(8,128)S(1)}, u32[]{:S(2)}, u32[]{:S(2)}) collective-permute-start(f32[32,128]{1,0:T(8,128)S(1)} %get-tuple-element.55.own_pot), channel_id=1, source_target_pairs={{0,4},{4,0},{1,5},{5,1},{2,6},{6,2},{3,7},{7,3},{8,12},{12,8},{9,1... | collective-permute-start | bytes 49160 | tf_op jit(solution)/shard_map/ppermute | solution.py:444

commit v5 on v4

--- a/solution.py
+++ b/solution.py
@@ -117,20 +117,24 @@
             out[q * 512 : (q + 1) * 512, span] = jnp.exp2(tn(left, right_t[:, span]) * (2.0 * C2)).astype(BF16)
 
 
-def first_kernel(at_own, other_a, la_own, b_t, scales, shift, kt_out, at_out, msg):
+def first_kernel(at_own, other_a, la_own, b_t, scales, shift, kt_out, at_out, msg, right):
     core = lax.axis_index("core")
     for m in range(2):
         span = slice(m * 256, (m + 1) * 256)
         for half, unit in ((core, at_own[:, span]), (1 - core, unit_t(other_a[span, :].T.astype(F32)))):
             at_out[:, pl.ds(pl.multiple_of(half * 512 + m * 256, 256), 256)] = unit
+    scaled = at_out[...].astype(F32) * (2.0 * C2)
+    high = scaled.astype(BF16)
+    right[0:DIM, :] = high
+    right[DIM : 2 * DIM, :] = (scaled - high.astype(F32)).astype(BF16)
     sums = [jnp.zeros((8, 256), F32)] * 4
     for q in range(NC // 512):
         here = slice(q * 512, (q + 1) * 512)
-        left = b_t[:, here]
+        left = jnp.concatenate([b_t[:, here].T] * 2, axis=1)
         scale = jnp.concatenate([scales[here, :], scales[here, :]], axis=1)
         for m in range(4):
             span = slice(m * 256, (m + 1) * 256)
-            part = jnp.exp2(tn(left, at_out[:, span]) * (2.0 * C2))
+            part = jnp.exp2(nn(left, right[:, span]))
             kt_out[here, span] = part.astype(BF16)
             sums[m] = sums[m] + jnp.sum((part * scale).reshape(64, 8, 256), axis=0)
     for m in range(4):
@@ -386,6 +390,7 @@
         first_kernel,
         [VM] * 6,
         [pltpu.VMEM((NC, NR), BF16), sds(DIM, NR, dtype=BF16), sds(24, 128)],
+        [pltpu.VMEM((2 * DIM, NR), BF16)],
         flops=2 * PASS * DIM,
         trans=PASS,
     )(at_own, other_a, la_own, b_t, scales, shift)

time: 80 us -> 79.4 us (level)
  no operation moved by 1% of the time
where the time goes in v5:
time: 79.4 us; the launch traced here: 79.1 us
  blocking collectives  28.8 us (36%)
  waiting for transfers between devices  20.8 us (26%)
  Pallas kernels  14.5 us (18%)
  starting transfers between devices  14.3 us (18%)
    all_to_all x2, blocking collectives, on_device(): parts = lax.all_to_all(msg, 'zy', 0, 0)  28.8 us
    ppermute x9, waiting for transfers between devices, over_x(): return [pair] + [lax.ppermute(pair, 'x', ring[s]) for s in (1, 2, 3)]  13.9 us
    ppermute x9, starting transfers between devices, over_x(): return [pair] + [lax.ppermute(pair, 'x', ring[s]) for s in (1, 2, 3)]  9.89 us
    all_to_all x1, starting transfers between devices, on_device(): sums = lax.all_to_all(sums, 'zy', 0, 0)  3.66 us
    pallas_call x1, Pallas kernels, on_device(): call(first_kernel, [VM] * 6, [pltpu.VMEM((NC, NR), BF16), sds(DIM, NR, dt...  2.66 us
    all_to_all x1, waiting for transfers between devices, on_device(): sums = lax.all_to_all(sums, 'zy', 0, 0)  2.37 us
    pallas_call x1, Pallas kernels, on_device(): call(kernel_matrix, [VM] * 2, [pltpu.VMEM((NR, NC), BF16)], flops=2 * PAS...  2.36 us
    pallas_call x1, Pallas kernels, on_device(): call(prep_kernel, [HB] * 5, [sds(DIM, NC, dtype=BF16), sds(DIM, 512, dtyp...  2.25 us
  transfers between devices with their start and end apart: 15, of which 13 were waited for; matrix products, arithmetic and copies ran while one was open for 0% of the time, Pallas kernels for 6%

profile of v5, /device:TPU:0, one launch (start us, length us, event | category | flops | bytes accessed | tf_op | source)
XLA Modules:
  0.0 79.1 jit_solution(17117079343081203786)
XLA Ops:
  0.6 0.1 collective-permute-start
  0.7 2.3 %shard_map.84 = (bf16[128,4096]{1,0:T(8,128)(2,1)S(1)}, bf16[128,512]{1,0:T(8,128)(2,1)S(1)}, f32[4096,128]{1,0:T(8,128)S(1)}, f32[8,128]{1,0:T(8,128)S(1)}, f32...) custom-call(bf16[16,2,256,128]{3,2,1,0:T(8,128)(2,1)} %bitcast.6, f32[64,128]{1,0:T(8,128)} %bitcast.7, f32[64,128]{1,0:T(8,128)} %bitcast.8, ...), custom_call_target="tpu_custom_call" | custom-call | flops 4194304 | bytes 1048576 | tf_op jit(solution)/shard_map/pallas_call | solution.py:360
  3.0 0.0 collective-permute-done.other_a
  3.0 2.7 %shard_map.85 = (bf16[4096,1024]{1,0:T(8,128)(2,1)S(1)}, bf16[128,1024]{1,0:T(8,128)(2,1)S(1)}, f32[24,128]{1,0:T(8,128)S(1)}) custom-call(bf16[128,512]{1,0:T(8,128)(2,1)S(1)} %get-tuple-element.32.at_own, bf16[512,128]{1,0:T(8,128)(2,1)S(1)} %collective-permute-done.other_a, f32[4,128]{1,0:T(4,128)S(1)} %get-tuple-element.33.la_own.la, ...), custom_call_target="tpu_custom_call" | custom-call | flops 1073741824 | tf_op jit(solution)/shard_map/pallas_call | solution.py:389
  5.7 0.6 collective-permute-start.1
  6.2 0.8 %collective-permute-done.1.received = f32[24,128]{1,0:T(8,128)S(1)} collective-permute-done((f32[24,128]{1,0:T(8,128)S(1)}, f32[24,128]{1,0:T(8,128)S(1)}, u32[]{:S(2)}, u32[]{:S(2)}) %collective-permute-start.1) | collective-permute-done | bytes 12320 | tf_op jit(solution)/shard_map/ppermute | solution.py:401
  7.1 2.9 %collective-permute-start.4 = (f32[16,128]{1,0:T(8,128)S(1)}, f32[16,128]{1,0:T(8,128)S(1)}, u32[]{:S(2)}, u32[]{:S(2)}) collective-permute-start(f32[16,128]{1,0:T(8,128)S(1)} %get-tuple-element.38.p0), channel_id=1, source_target_pairs={{0,3},{1,0},{2,1},{3,2},{4,7},{5,4},{6,5},{7,6},{8,11},{9,8},{10,9... | collective-permute-start | bytes 24584 | tf_op jit(solution)/shard_map/ppermute | solution.py:399
  10.0 0.8 %collective-permute-start.3 = (f32[16,128]{1,0:T(8,128)S(1)}, f32[16,128]{1,0:T(8,128)S(1)}, u32[]{:S(2)}, u32[]{:S(2)}) collective-permute-start(f32[16,128]{1,0:T(8,128)S(1)} %get-tuple-element.38.p0), channel_id=1, source_target_pairs={{0,2},{1,3},{2,0},{3,1},{4,6},{5,7},{6,4},{7,5},{8,10},{9,11},{10,... | collective-permute-start | bytes 24584 | tf_op jit(solution)/shard_map/ppermute | solution.py:399
  10.8 0.9 %collective-permute-start.2 = (f32[16,128]{1,0:T(8,128)S(1)}, f32[16,128]{1,0:T(8,128)S(1)}, u32[]{:S(2)}, u32[]{:S(2)}) collective-permute-start(f32[16,128]{1,0:T(8,128)S(1)} %get-tuple-element.38.p0), channel_id=1, source_target_pairs={{0,1},{1,2},{2,3},{3,0},{4,5},{5,6},{6,7},{7,4},{8,9},{9,10},{10,1... | collective-permute-start | bytes 24584 | tf_op jit(solution)/shard_map/ppermute | solution.py:399
  11.7 2.4 %shard_map.87.k_mat = bf16[1024,4096]{1,0:T(8,128)(2,1)S(1)} custom-call(bf16[128,1024]{1,0:T(8,128)(2,1)S(1)} %get-tuple-element.40.a_t, bf16[128,4096]{1,0:T(8,128)(2,1)S(1)} %get-tuple-element.34.b_t), custom_call_target="tpu_custom_call" | custom-call | flops 1073741824 | tf_op jit(solution)/shard_map/pallas_call | solution.py:402
  14.0 0.0 collective-permute-done.4.p3
  14.1 1.1 %collective-permute-done.3.p2 = f32[16,128]{1,0:T(8,128)S(1)} collective-permute-done((f32[16,128]{1,0:T(8,128)S(1)}, f32[16,128]{1,0:T(8,128)S(1)}, u32[]{:S(2)}, u32[]{:S(2)}) %collective-permute-start.3) | collective-permute-done | bytes 8224 | tf_op jit(solution)/shard_map/ppermute | solution.py:399
  15.1 0.5 collective-permute-done.2.p1
  15.6 1.3 %shard_map.88 = (f32[16,40,128]{2,1,0:T(8,128)S(1)}, f32[8,128]{1,0:T(8,128)S(1)}) custom-call(f32[16,128]{1,0:T(8,128)S(1)} %get-tuple-element.38.p0, f32[16,128]{1,0:T(8,128)S(1)} %collective-permute-done.2.p1, f32[16,128]{1,0:T(8,128)S(1)} %collective-permute-done.3.p2, f32[16,128]{1,0:T(8,128)S(1)} %collective-permute-done.4.p3, ...), custom_call_target="tpu_custom_call" | custom-call | flops 134217728 | tf_op jit(solution)/shard_map/pallas_call | solution.py:405
  17.0 16.9 %all_to_all.15.parts = f32[16,40,128]{2,1,0:T(8,128)S(1)} all-to-all(f32[16,40,128]{2,1,0:T(8,128)S(1)} %get-tuple-element.41), channel_id=1, replica_groups=mesh['zy'=16,'core'=2,'x'=4] {'zy'}, dimensions={0} | all-to-all | bytes 655360 | tf_op jit(solution)/shard_map/all_to_all | solution.py:413
  33.8 1.3 %shard_map.89 = (f32[16,128]{1,0:T(8,128)S(1)}, f32[8,128]{1,0:T(8,128)S(1)}) custom-call(f32[16,40,128]{2,1,0:T(8,128)S(1)} %all_to_all.15.parts, f32[32,128]{1,0:T(8,128)S(1)} %get-tuple-element.42.lb, bf16[4096,1024]{1,0:T(8,128)(2,1)S(1)} %get-tuple-element.43.kt_mat, f32[8,128]{1,0:T(8,128)S(1)} %get-tuple-element.44.base), custom_call_target="tpu_custom_call" | custom-call | flops 134217728 | tf_op jit(solution)/shard_map/pallas_call | solution.py:414
  35.2 0.0 collective-permute-start.5
  35.2 1.2 %collective-permute-done.5.received = f32[16,128]{1,0:T(8,128)S(1)} collective-permute-done((f32[16,128]{1,0:T(8,128)S(1)}, f32[16,128]{1,0:T(8,128)S(1)}, u32[]{:S(2)}, u32[]{:S(2)}) %collective-permute-start.5) | collective-permute-done | bytes 8224 | tf_op jit(solution)/shard_map/ppermute | solution.py:422
  36.4 0.9 %collective-permute-start.8 = (f32[16,128]{1,0:T(8,128)S(1)}, f32[16,128]{1,0:T(8,128)S(1)}, u32[]{:S(2)}, u32[]{:S(2)}) collective-permute-start(f32[16,128]{1,0:T(8,128)S(1)} %shard_map.90.p0), channel_id=1, source_target_pairs={{0,3},{1,0},{2,1},{3,2},{4,7},{5,4},{6,5},{7,6},{8,11},{9,8},{10,9... | collective-permute-start | bytes 24584 | tf_op jit(solution)/shard_map/ppermute | solution.py:399
  37.2 1.5 %collective-permute-start.7 = (f32[16,128]{1,0:T(8,128)S(1)}, f32[16,128]{1,0:T(8,128)S(1)}, u32[]{:S(2)}, u32[]{:S(2)}) collective-permute-start(f32[16,128]{1,0:T(8,128)S(1)} %shard_map.90.p0), channel_id=1, source_target_pairs={{0,2},{1,3},{2,0},{3,1},{4,6},{5,7},{6,4},{7,5},{8,10},{9,11},{10,... | collective-permute-start | bytes 24584 | tf_op jit(solution)/shard_map/ppermute | solution.py:399
  38.7 0.6 collective-permute-start.6
  39.4 0.7 collective-permute-done.8.p3
  40.1 2.3 %collective-permute-done.7.p2 = f32[16,128]{1,0:T(8,128)S(1)} collective-permute-done((f32[16,128]{1,0:T(8,128)S(1)}, f32[16,128]{1,0:T(8,128)S(1)}, u32[]{:S(2)}, u32[]{:S(2)}) %collective-permute-start.7) | collective-permute-done | bytes 8224 | tf_op jit(solution)/shard_map/ppermute | solution.py:399
  42.4 1.2 %collective-permute-done.6.p1 = f32[16,128]{1,0:T(8,128)S(1)} collective-permute-done((f32[16,128]{1,0:T(8,128)S(1)}, f32[16,128]{1,0:T(8,128)S(1)}, u32[]{:S(2)}, u32[]{:S(2)}) %collective-permute-start.6) | collective-permute-done | bytes 8224 | tf_op jit(solution)/shard_map/ppermute | solution.py:399
  43.6 1.5 %shard_map.91 = (f32[16,40,128]{2,1,0:T(8,128)S(1)}, bf16[16,128,256]{2,1,0:T(8,128)(2,1)S(1)}, f32[8,128]{1,0:T(8,128)S(1)}) custom-call(f32[16,128]{1,0:T(8,128)S(1)} %shard_map.90.p0, f32[16,128]{1,0:T(8,128)S(1)} %collective-permute-done.6.p1, f32[16,128]{1,0:T(8,128)S(1)} %collective-permute-done.7.p2, f32[16,128]{1,0:T(8,128)S(1)} %collective-permute-done.8.p3, ...), custom_call_target="tpu_custom_call" | custom-call | flops 1207959552 | tf_op jit(solution)/shard_map/pallas_call | solution.py:423
  45.1 11.9 %all_to_all.16.parts = f32[16,40,128]{2,1,0:T(8,128)S(1)} all-to-all(f32[16,40,128]{2,1,0:T(8,128)S(1)} %get-tuple-element.47), channel_id=1, replica_groups=mesh['zy'=16,'core'=2,'x'=4] {'zy'}, dimensions={0} | all-to-all | bytes 655360 | tf_op jit(solution)/shard_map/all_to_all | solution.py:430
  57.1 1.7 %shard_map.92 = (bf16[144,512]{1,0:T(8,128)(2,1)S(1)}, bf16[144,512]{1,0:T(8,128)(2,1)S(1)}, f32[32,128]{1,0:T(8,128)S(1)}, f32[32,128]{1,0:T(8,128)S(1)}, f32[8...) custom-call(f32[16,40,128]{2,1,0:T(8,128)S(1)} %all_to_all.16.parts, f32[32,128]{1,0:T(8,128)S(1)} %get-tuple-element.42.lb, ...), custom_call_target="tpu_custom_call" | custom-call | flops 1207959552 | tf_op jit(solution)/shard_map/pallas_call | solution.py:431
  58.7 3.7 %all-to-all-start.2 = ((bf16[16,128,256]{2,1,0:T(8,128)(2,1)}), bf16[16,128,256]{2,1,0:T(8,128)(2,1)S(1)}, u32[]{:S(2)}, u32[]{:S(2)}) async-start(bf16[16,128,256]{2,1,0:T(8,128)(2,1)} %get-tuple-element.53), calls=%async_computation.2 | async-start | bytes 2097152 | tf_op jit(solution)/shard_map/all_to_all | solution.py:448
  62.4 0.1 collective-permute-start.9
  62.5 1.4 %collective-permute-done.9.received = bf16[144,512]{1,0:T(8,128)(2,1)S(1)} collective-permute-done((bf16[144,512]{1,0:T(8,128)(2,1)S(1)}, bf16[144,512]{1,0:T(8,128)(2,1)S(1)}, u32[]{:S(2)}, u32[]{:S(2)}) %collective-permute-start.9) | collective-permute-done | bytes 147488 | tf_op jit(solution)/shard_map/ppermute | solution.py:447
  63.9 0.1 shard_map.93.p0
  64.0 1.2 %collective-permute-start.12 = (bf16[144,512]{1,0:T(8,128)(2,1)S(1)}, bf16[144,512]{1,0:T(8,128)(2,1)S(1)}, u32[]{:S(2)}, u32[]{:S(2)}) collective-permute-start(bf16[144,512]{1,0:T(8,128)(2,1)S(1)} %shard_map.93.p0), channel_id=1, source_target_pairs={{0,3},{1,0},{2,1},{3,2},{4,7},{5,4},{6,5},{7,6},{8,11},{9,8},{10,9... | collective-permute-start | bytes 442376 | tf_op jit(solution)/shard_map/ppermute | solution.py:399
  65.2 0.9 %collective-permute-start.11 = (bf16[144,512]{1,0:T(8,128)(2,1)S(1)}, bf16[144,512]{1,0:T(8,128)(2,1)S(1)}, u32[]{:S(2)}, u32[]{:S(2)}) collective-permute-start(bf16[144,512]{1,0:T(8,128)(2,1)S(1)} %shard_map.93.p0), channel_id=1, source_target_pairs={{0,2},{1,3},{2,0},{3,1},{4,6},{5,7},{6,4},{7,5},{8,10},{9,11},{10,... | collective-permute-start | bytes 442376 | tf_op jit(solution)/shard_map/ppermute | solution.py:399
  66.1 0.1 collective-permute-start.10
  66.2 0.0 collective-permute-start.13
  66.2 1.2 %collective-permute-done.13.other_pot = f32[32,128]{1,0:T(8,128)S(1)} collective-permute-done((f32[32,128]{1,0:T(8,128)S(1)}, f32[32,128]{1,0:T(8,128)S(1)}, u32[]{:S(2)}, u32[]{:S(2)}) %collective-permute-start.13) | collective-permute-done | bytes 16416 | tf_op jit(solution)/shard_map/ppermute | solution.py:449
  67.4 3.3 %collective-permute-done.12.p3 = bf16[144,512]{1,0:T(8,128)(2,1)S(1)} collective-permute-done((bf16[144,512]{1,0:T(8,128)(2,1)S(1)}, bf16[144,512]{1,0:T(8,128)(2,1)S(1)}, u32[]{:S(2)}, u32[]{:S(2)}) %collective-permute-start.12) | collective-permute-done | bytes 147488 | tf_op jit(solution)/shard_map/ppermute | solution.py:399
  70.7 2.7 %collective-permute-done.11.p2 = bf16[144,512]{1,0:T(8,128)(2,1)S(1)} collective-permute-done((bf16[144,512]{1,0:T(8,128)(2,1)S(1)}, bf16[144,512]{1,0:T(8,128)(2,1)S(1)}, u32[]{:S(2)}, u32[]{:S(2)}) %collective-permute-start.11) | collective-permute-done | bytes 147488 | tf_op jit(solution)/shard_map/ppermute | solution.py:399
  73.5 2.0 %collective-permute-done.10.p1 = bf16[144,512]{1,0:T(8,128)(2,1)S(1)} collective-permute-done((bf16[144,512]{1,0:T(8,128)(2,1)S(1)}, bf16[144,512]{1,0:T(8,128)(2,1)S(1)}, u32[]{:S(2)}, u32[]{:S(2)}) %collective-permute-start.10) | collective-permute-done | bytes 147488 | tf_op jit(solution)/shard_map/ppermute | solution.py:399
  75.5 2.4 %all-to-all-done.2.sums = bf16[16,128,256]{2,1,0:T(8,128)(2,1)S(1)} async-done(((bf16[16,128,256]{2,1,0:T(8,128)(2,1)}), bf16[16,128,256]{2,1,0:T(8,128)(2,1)S(1)}, u32[]{:S(2)}, u32[]{:S(2)}) %all-to-all-start.2) | async-done | bytes 1048608 | tf_op jit(solution)/shard_map/all_to_all | solution.py:448
  77.9 1.2 %shard_map.94 = (f32[512,128]{1,0:T(8,128)}, f32[4,128]{1,0:T(4,128)}, f32[256,128]{1,0:T(8,128)}, f32[64,128]{1,0:T(8,128)}) custom-call(bf16[144,512]{1,0:T(8,128)(2,1)S(1)} %shard_map.93.p0, bf16[144,512]{1,0:T(8,128)(2,1)S(1)} %collective-permute-done.10.p1, bf16[144,512]{1,0:T(8,128)(2,1)S(1)} %collective-permute-done.11.p2, ...), custom_call_target="tpu_custom_call" | custom-call | tf_op jit(solution)/shard_map/pallas_call | solution.py:452
  (2 shorter events, 0.0 us)
Async XLA Ops:
  0.6 2.4 %collective-permute-start = (bf16[512,128]{1,0:T(8,128)(2,1)}, bf16[512,128]{1,0:T(8,128)(2,1)S(1)}, u32[]{:S(2)}, u32[]{:S(2)}) collective-permute-start(bf16[512,128]{1,0:T(8,128)(2,1)} %desc_a.1), channel_id=1, source_target_pairs={{0,4},{4,0},{1,5},{5,1},{2,6},{6,2},{3,7},{7,3},{8,12},{12,8},{9,1... | collective-permute-start | bytes 393224 | tf_op jit(solution)/shard_map/ppermute | solution.py:358
  5.7 1.4 %collective-permute-start.1 = (f32[24,128]{1,0:T(8,128)S(1)}, f32[24,128]{1,0:T(8,128)S(1)}, u32[]{:S(2)}, u32[]{:S(2)}) collective-permute-start(f32[24,128]{1,0:T(8,128)S(1)} %get-tuple-element.37.own), channel_id=1, source_target_pairs={{0,4},{4,0},{1,5},{5,1},{2,6},{6,2},{3,7},{7,3},{8,12},{12,8},{9,1... | collective-permute-start | bytes 36872 | tf_op jit(solution)/shard_map/ppermute | solution.py:401
  7.1 7.0 %collective-permute-start.4 = (f32[16,128]{1,0:T(8,128)S(1)}, f32[16,128]{1,0:T(8,128)S(1)}, u32[]{:S(2)}, u32[]{:S(2)}) collective-permute-start(f32[16,128]{1,0:T(8,128)S(1)} %get-tuple-element.38.p0), channel_id=1, source_target_pairs={{0,3},{1,0},{2,1},{3,2},{4,7},{5,4},{6,5},{7,6},{8,11},{9,8},{10,9... | collective-permute-start | bytes 24584 | tf_op jit(solution)/shard_map/ppermute | solution.py:399
  10.0 5.2 %collective-permute-start.3 = (f32[16,128]{1,0:T(8,128)S(1)}, f32[16,128]{1,0:T(8,128)S(1)}, u32[]{:S(2)}, u32[]{:S(2)}) collective-permute-start(f32[16,128]{1,0:T(8,128)S(1)} %get-tuple-element.38.p0), channel_id=1, source_target_pairs={{0,2},{1,3},{2,0},{3,1},{4,6},{5,7},{6,4},{7,5},{8,10},{9,11},{10,... | collective-permute-start | bytes 24584 | tf_op jit(solution)/shard_map/ppermute | solution.py:399
  10.8 4.9 %collective-permute-start.2 = (f32[16,128]{1,0:T(8,128)S(1)}, f32[16,128]{1,0:T(8,128)S(1)}, u32[]{:S(2)}, u32[]{:S(2)}) collective-permute-start(f32[16,128]{1,0:T(8,128)S(1)} %get-tuple-element.38.p0), channel_id=1, source_target_pairs={{0,1},{1,2},{2,3},{3,0},{4,5},{5,6},{6,7},{7,4},{8,9},{9,10},{10,1... | collective-permute-start | bytes 24584 | tf_op jit(solution)/shard_map/ppermute | solution.py:399
  35.2 1.2 %collective-permute-start.5 = (f32[16,128]{1,0:T(8,128)S(1)}, f32[16,128]{1,0:T(8,128)S(1)}, u32[]{:S(2)}, u32[]{:S(2)}) collective-permute-start(f32[16,128]{1,0:T(8,128)S(1)} %get-tuple-element.45.own), channel_id=1, source_target_pairs={{0,4},{4,0},{1,5},{5,1},{2,6},{6,2},{3,7},{7,3},{8,12},{12,8},{9,1... | collective-permute-start | bytes 24584 | tf_op jit(solution)/shard_map/ppermute | solution.py:422
  36.4 3.7 %collective-permute-start.8 = (f32[16,128]{1,0:T(8,128)S(1)}, f32[16,128]{1,0:T(8,128)S(1)}, u32[]{:S(2)}, u32[]{:S(2)}) collective-permute-start(f32[16,128]{1,0:T(8,128)S(1)} %shard_map.90.p0), channel_id=1, source_target_pairs={{0,3},{1,0},{2,1},{3,2},{4,7},{5,4},{6,5},{7,6},{8,11},{9,8},{10,9... | collective-permute-start | bytes 24584 | tf_op jit(solution)/shard_map/ppermute | solution.py:399
  37.2 5.2 %collective-permute-start.7 = (f32[16,128]{1,0:T(8,128)S(1)}, f32[16,128]{1,0:T(8,128)S(1)}, u32[]{:S(2)}, u32[]{:S(2)}) collective-permute-start(f32[16,128]{1,0:T(8,128)S(1)} %shard_map.90.p0), channel_id=1, source_target_pairs={{0,2},{1,3},{2,0},{3,1},{4,6},{5,7},{6,4},{7,5},{8,10},{9,11},{10,... | collective-permute-start | bytes 24584 | tf_op jit(solution)/shard_map/ppermute | solution.py:399
  38.7 4.9 %collective-permute-start.6 = (f32[16,128]{1,0:T(8,128)S(1)}, f32[16,128]{1,0:T(8,128)S(1)}, u32[]{:S(2)}, u32[]{:S(2)}) collective-permute-start(f32[16,128]{1,0:T(8,128)S(1)} %shard_map.90.p0), channel_id=1, source_target_pairs={{0,1},{1,2},{2,3},{3,0},{4,5},{5,6},{6,7},{7,4},{8,9},{9,10},{10,1... | collective-permute-start | bytes 24584 | tf_op jit(solution)/shard_map/ppermute | solution.py:399
  58.7 19.1 %all-to-all-start.2 = ((bf16[16,128,256]{2,1,0:T(8,128)(2,1)}), bf16[16,128,256]{2,1,0:T(8,128)(2,1)S(1)}, u32[]{:S(2)}, u32[]{:S(2)}) async-start(bf16[16,128,256]{2,1,0:T(8,128)(2,1)} %get-tuple-element.53), calls=%async_computation.2 | async-start | bytes 2097152 | tf_op jit(solution)/shard_map/all_to_all | solution.py:448
  62.4 1.5 %collective-permute-start.9 = (bf16[144,512]{1,0:T(8,128)(2,1)S(1)}, bf16[144,512]{1,0:T(8,128)(2,1)S(1)}, u32[]{:S(2)}, u32[]{:S(2)}) collective-permute-start(bf16[144,512]{1,0:T(8,128)(2,1)S(1)} %get-tuple-element.51), channel_id=1, source_target_pairs={{0,4},{4,0},{1,5},{5,1},{2,6},{6,2},{3,7},{7,3},{8,12},{12,8},{9,1... | collective-permute-start | bytes 442376 | tf_op jit(solution)/shard_map/ppermute | solution.py:447
  64.0 6.8 %collective-permute-start.12 = (bf16[144,512]{1,0:T(8,128)(2,1)S(1)}, bf16[144,512]{1,0:T(8,128)(2,1)S(1)}, u32[]{:S(2)}, u32[]{:S(2)}) collective-permute-start(bf16[144,512]{1,0:T(8,128)(2,1)S(1)} %shard_map.93.p0), channel_id=1, source_target_pairs={{0,3},{1,0},{2,1},{3,2},{4,7},{5,4},{6,5},{7,6},{8,11},{9,8},{10,9... | collective-permute-start | bytes 442376 | tf_op jit(solution)/shard_map/ppermute | solution.py:399
  65.2 8.3 %collective-permute-start.11 = (bf16[144,512]{1,0:T(8,128)(2,1)S(1)}, bf16[144,512]{1,0:T(8,128)(2,1)S(1)}, u32[]{:S(2)}, u32[]{:S(2)}) collective-permute-start(bf16[144,512]{1,0:T(8,128)(2,1)S(1)} %shard_map.93.p0), channel_id=1, source_target_pairs={{0,2},{1,3},{2,0},{3,1},{4,6},{5,7},{6,4},{7,5},{8,10},{9,11},{10,... | collective-permute-start | bytes 442376 | tf_op jit(solution)/shard_map/ppermute | solution.py:399
  66.1 9.4 %collective-permute-start.10 = (bf16[144,512]{1,0:T(8,128)(2,1)S(1)}, bf16[144,512]{1,0:T(8,128)(2,1)S(1)}, u32[]{:S(2)}, u32[]{:S(2)}) collective-permute-start(bf16[144,512]{1,0:T(8,128)(2,1)S(1)} %shard_map.93.p0), channel_id=1, source_target_pairs={{0,1},{1,2},{2,3},{3,0},{4,5},{5,6},{6,7},{7,4},{8,9},{9,10},{10,1... | collective-permute-start | bytes 442376 | tf_op jit(solution)/shard_map/ppermute | solution.py:399
  66.2 1.2 %collective-permute-start.13 = (f32[32,128]{1,0:T(8,128)S(1)}, f32[32,128]{1,0:T(8,128)S(1)}, u32[]{:S(2)}, u32[]{:S(2)}) collective-permute-start(f32[32,128]{1,0:T(8,128)S(1)} %get-tuple-element.55.own_pot), channel_id=1, source_target_pairs={{0,4},{4,0},{1,5},{5,1},{2,6},{6,2},{3,7},{7,3},{8,12},{12,8},{9,1... | collective-permute-start | bytes 49160 | tf_op jit(solution)/shard_map/ppermute | solution.py:449

commit v6 on v5

--- a/solution.py
+++ b/solution.py
@@ -70,7 +70,13 @@
     return (raw / norm).astype(BF16)
 
 
-def prep_kernel(desc_b, g_all, lb_all, desc_a, la_all, bt_out, at_out, scale_out, shift_out, lb_out, la_out,
+def two_parts(unit):
+    scaled = unit.astype(F32) * (2.0 * C2)
+    high = scaled.astype(BF16)
+    return jnp.concatenate([high, (scaled - high.astype(F32)).astype(BF16)], axis=0)
+
+
+def prep_kernel(desc_b, g_all, lb_all, desc_a, la_all, bt_out, at_out, right_out, scale_out, shift_out, lb_out, la_out,
                 b_raw, a_raw, g_raw, lb_raw, vec, sems):
     core = lax.axis_index("core")
     half = NK // 2
@@ -95,7 +101,9 @@
     load_a.wait()
     for m in range(2):
         span = slice(m * 256, (m + 1) * 256)
-        at_out[:, span] = unit_t(a_raw[span, :].T.astype(F32))
+        unit = unit_t(a_raw[span, :].T.astype(F32))
+        at_out[:, span] = unit
+        right_out[:, span] = two_parts(unit)
     for q in range(2):
         loads[q].wait()
         for k in range(q * half, (q + 1) * half):
@@ -117,16 +125,17 @@
             out[q * 512 : (q + 1) * 512, span] = jnp.exp2(tn(left, right_t[:, span]) * (2.0 * C2)).astype(BF16)
 
 
-def first_kernel(at_own, other_a, la_own, b_t, scales, shift, kt_out, at_out, msg, right):
+def first_kernel(at_own, right_own, other_a, la_own, b_t, scales, shift, kt_out, at_out, msg, right):
     core = lax.axis_index("core")
     for m in range(2):
         span = slice(m * 256, (m + 1) * 256)
-        for half, unit in ((core, at_own[:, span]), (1 - core, unit_t(other_a[span, :].T.astype(F32)))):
-            at_out[:, pl.ds(pl.multiple_of(half * 512 + m * 256, 256), 256)] = unit
-    scaled = at_out[...].astype(F32) * (2.0 * C2)
-    high = scaled.astype(BF16)
-    right[0:DIM, :] = high
-    right[DIM : 2 * DIM, :] = (scaled - high.astype(F32)).astype(BF16)
+        unit = unit_t(other_a[span, :].T.astype(F32))
+        own = pl.ds(pl.multiple_of(core * 512 + m * 256, 256), 256)
+        other = pl.ds(pl.multiple_of((1 - core) * 512 + m * 256, 256), 256)
+        at_out[:, own] = at_own[:, span]
+        at_out[:, other] = unit
+        right[:, own] = right_own[:, span]
+        right[:, other] = two_parts(unit)
     sums = [jnp.zeros((8, 256), F32)] * 4
     for q in range(NC // 512):
         here = slice(q * 512, (q + 1) * 512)
@@ -357,12 +366,13 @@
     stay = lambda x: pltpu.with_memory_space_constraint(x, pltpu.HBM)
     other_a = lax.ppermute(desc_a, "core", swap)
 
-    b_t, at_own, scales, shift, lb, la_own = call(
+    b_t, at_own, right_own, scales, shift, lb, la_own = call(
         prep_kernel,
         [HB] * 5,
         [
             sds(DIM, NC, dtype=BF16),
             sds(DIM, 512, dtype=BF16),
+            sds(2 * DIM, 512, dtype=BF16),
             sds(NC, 128),
             sds(8, 128),
             sds(32, 128),
@@ -388,12 +398,12 @@
 
     kt_mat, a_t, msg = call(
         first_kernel,
-        [VM] * 6,
+        [VM] * 7,
         [pltpu.VMEM((NC, NR), BF16), sds(DIM, NR, dtype=BF16), sds(24, 128)],
         [pltpu.VMEM((2 * DIM, NR), BF16)],
         flops=2 * PASS * DIM,
         trans=PASS,
-    )(at_own, other_a, la_own, b_t, scales, shift)
+    )(at_own, right_own, other_a, la_own, b_t, scales, shift)
 
     def over_x(pair):
         return [pair] + [lax.ppermute(pair, "x", ring[s]) for s in (1, 2, 3)]

time: 79.4 us -> 79.4 us (level)
  no operation moved by 1% of the time
where the time goes in v6:
time: 79.4 us; the launch traced here: 79.1 us
  blocking collectives  28.8 us (36%)
  waiting for transfers between devices  20.8 us (26%)
  Pallas kernels  14.5 us (18%)
  starting transfers between devices  14.3 us (18%)
    all_to_all x2, blocking collectives, on_device(): parts = lax.all_to_all(msg, 'zy', 0, 0)  28.8 us
    ppermute x9, waiting for transfers between devices, over_x(): return [pair] + [lax.ppermute(pair, 'x', ring[s]) for s in (1, 2, 3)]  13.9 us
    ppermute x9, starting transfers between devices, over_x(): return [pair] + [lax.ppermute(pair, 'x', ring[s]) for s in (1, 2, 3)]  9.9 us
    all_to_all x1, starting transfers between devices, on_device(): sums = lax.all_to_all(sums, 'zy', 0, 0)  3.66 us
    pallas_call x1, Pallas kernels, on_device(): call(first_kernel, [VM] * 7, [pltpu.VMEM((NC, NR), BF16), sds(DIM, NR, dt...  2.65 us
    all_to_all x1, waiting for transfers between devices, on_device(): sums = lax.all_to_all(sums, 'zy', 0, 0)  2.37 us
    pallas_call x1, Pallas kernels, on_device(): call(kernel_matrix, [VM] * 2, [pltpu.VMEM((NR, NC), BF16)], flops=2 * PAS...  2.36 us
    pallas_call x1, Pallas kernels, on_device(): call(prep_kernel, [HB] * 5, [sds(DIM, NC, dtype=BF16), sds(DIM, 512, dtyp...  2.31 us
  transfers between devices with their start and end apart: 15, of which 13 were waited for; matrix products, arithmetic and copies ran while one was open for 0% of the time, Pallas kernels for 6%

profile of v6, /device:TPU:0, one launch (start us, length us, event | category | flops | bytes accessed | tf_op | source)
XLA Modules:
  0.0 79.1 jit_solution(7399566182467417503)
XLA Ops:
  0.6 0.1 collective-permute-start
  0.7 2.3 %shard_map.84 = (bf16[128,4096]{1,0:T(8,128)(2,1)S(1)}, bf16[128,512]{1,0:T(8,128)(2,1)S(1)}, bf16[256,512]{1,0:T(8,128)(2,1)S(1)}, f32[4096,128]{1,0:T(8,128)S(...) custom-call(bf16[16,2,256,128]{3,2,1,0:T(8,128)(2,1)} %bitcast.6, f32[64,128]{1,0:T(8,128)} %bitcast.7, ...), custom_call_target="tpu_custom_call" | custom-call | flops 4194304 | bytes 1048576 | tf_op jit(solution)/shard_map/pallas_call | solution.py:369
  3.0 0.0 collective-permute-done.other_a
  3.1 2.6 %shard_map.85 = (bf16[4096,1024]{1,0:T(8,128)(2,1)S(1)}, bf16[128,1024]{1,0:T(8,128)(2,1)S(1)}, f32[24,128]{1,0:T(8,128)S(1)}) custom-call(bf16[128,512]{1,0:T(8,128)(2,1)S(1)} %get-tuple-element.33.at_own, bf16[256,512]{1,0:T(8,128)(2,1)S(1)} %get-tuple-element.34.right_own, bf16[512,128]{1,0:T(8,128)(2,1)S(1)} %collective-permute-done.other_a, ...), custom_call_target="tpu_custom_call" | custom-call | flops 1073741824 | tf_op jit(solution)/shard_map/pallas_call | solution.py:399
  5.7 0.6 collective-permute-start.1
  6.3 0.8 %collective-permute-done.1.received = f32[24,128]{1,0:T(8,128)S(1)} collective-permute-done((f32[24,128]{1,0:T(8,128)S(1)}, f32[24,128]{1,0:T(8,128)S(1)}, u32[]{:S(2)}, u32[]{:S(2)}) %collective-permute-start.1) | collective-permute-done | bytes 12320 | tf_op jit(solution)/shard_map/ppermute | solution.py:411
  7.1 2.9 %collective-permute-start.4 = (f32[16,128]{1,0:T(8,128)S(1)}, f32[16,128]{1,0:T(8,128)S(1)}, u32[]{:S(2)}, u32[]{:S(2)}) collective-permute-start(f32[16,128]{1,0:T(8,128)S(1)} %get-tuple-element.40.p0), channel_id=1, source_target_pairs={{0,3},{1,0},{2,1},{3,2},{4,7},{5,4},{6,5},{7,6},{8,11},{9,8},{10,9... | collective-permute-start | bytes 24584 | tf_op jit(solution)/shard_map/ppermute | solution.py:409
  10.0 0.8 %collective-permute-start.3 = (f32[16,128]{1,0:T(8,128)S(1)}, f32[16,128]{1,0:T(8,128)S(1)}, u32[]{:S(2)}, u32[]{:S(2)}) collective-permute-start(f32[16,128]{1,0:T(8,128)S(1)} %get-tuple-element.40.p0), channel_id=1, source_target_pairs={{0,2},{1,3},{2,0},{3,1},{4,6},{5,7},{6,4},{7,5},{8,10},{9,11},{10,... | collective-permute-start | bytes 24584 | tf_op jit(solution)/shard_map/ppermute | solution.py:409
  10.8 0.9 %collective-permute-start.2 = (f32[16,128]{1,0:T(8,128)S(1)}, f32[16,128]{1,0:T(8,128)S(1)}, u32[]{:S(2)}, u32[]{:S(2)}) collective-permute-start(f32[16,128]{1,0:T(8,128)S(1)} %get-tuple-element.40.p0), channel_id=1, source_target_pairs={{0,1},{1,2},{2,3},{3,0},{4,5},{5,6},{6,7},{7,4},{8,9},{9,10},{10,1... | collective-permute-start | bytes 24584 | tf_op jit(solution)/shard_map/ppermute | solution.py:409
  11.7 2.4 %shard_map.87.k_mat = bf16[1024,4096]{1,0:T(8,128)(2,1)S(1)} custom-call(bf16[128,1024]{1,0:T(8,128)(2,1)S(1)} %get-tuple-element.42.a_t, bf16[128,4096]{1,0:T(8,128)(2,1)S(1)} %get-tuple-element.36.b_t), custom_call_target="tpu_custom_call" | custom-call | flops 1073741824 | tf_op jit(solution)/shard_map/pallas_call | solution.py:412
  14.1 0.0 collective-permute-done.4.p3
  14.1 1.1 %collective-permute-done.3.p2 = f32[16,128]{1,0:T(8,128)S(1)} collective-permute-done((f32[16,128]{1,0:T(8,128)S(1)}, f32[16,128]{1,0:T(8,128)S(1)}, u32[]{:S(2)}, u32[]{:S(2)}) %collective-permute-start.3) | collective-permute-done | bytes 8224 | tf_op jit(solution)/shard_map/ppermute | solution.py:409
  15.2 0.5 collective-permute-done.2.p1
  15.7 1.3 %shard_map.88 = (f32[16,40,128]{2,1,0:T(8,128)S(1)}, f32[8,128]{1,0:T(8,128)S(1)}) custom-call(f32[16,128]{1,0:T(8,128)S(1)} %get-tuple-element.40.p0, f32[16,128]{1,0:T(8,128)S(1)} %collective-permute-done.2.p1, f32[16,128]{1,0:T(8,128)S(1)} %collective-permute-done.3.p2, f32[16,128]{1,0:T(8,128)S(1)} %collective-permute-done.4.p3, ...), custom_call_target="tpu_custom_call" | custom-call | flops 134217728 | tf_op jit(solution)/shard_map/pallas_call | solution.py:415
  17.0 16.9 %all_to_all.15.parts = f32[16,40,128]{2,1,0:T(8,128)S(1)} all-to-all(f32[16,40,128]{2,1,0:T(8,128)S(1)} %get-tuple-element.43), channel_id=1, replica_groups=mesh['zy'=16,'core'=2,'x'=4] {'zy'}, dimensions={0} | all-to-all | bytes 655360 | tf_op jit(solution)/shard_map/all_to_all | solution.py:423
  33.9 1.3 %shard_map.89 = (f32[16,128]{1,0:T(8,128)S(1)}, f32[8,128]{1,0:T(8,128)S(1)}) custom-call(f32[16,40,128]{2,1,0:T(8,128)S(1)} %all_to_all.15.parts, f32[32,128]{1,0:T(8,128)S(1)} %get-tuple-element.44.lb, bf16[4096,1024]{1,0:T(8,128)(2,1)S(1)} %get-tuple-element.45.kt_mat, f32[8,128]{1,0:T(8,128)S(1)} %get-tuple-element.46.base), custom_call_target="tpu_custom_call" | custom-call | flops 134217728 | tf_op jit(solution)/shard_map/pallas_call | solution.py:424
  35.2 0.0 collective-permute-start.5
  35.2 1.2 %collective-permute-done.5.received = f32[16,128]{1,0:T(8,128)S(1)} collective-permute-done((f32[16,128]{1,0:T(8,128)S(1)}, f32[16,128]{1,0:T(8,128)S(1)}, u32[]{:S(2)}, u32[]{:S(2)}) %collective-permute-start.5) | collective-permute-done | bytes 8224 | tf_op jit(solution)/shard_map/ppermute | solution.py:432
  36.4 0.9 %collective-permute-start.8 = (f32[16,128]{1,0:T(8,128)S(1)}, f32[16,128]{1,0:T(8,128)S(1)}, u32[]{:S(2)}, u32[]{:S(2)}) collective-permute-start(f32[16,128]{1,0:T(8,128)S(1)} %shard_map.90.p0), channel_id=1, source_target_pairs={{0,3},{1,0},{2,1},{3,2},{4,7},{5,4},{6,5},{7,6},{8,11},{9,8},{10,9... | collective-permute-start | bytes 24584 | tf_op jit(solution)/shard_map/ppermute | solution.py:409
  37.3 1.5 %collective-permute-start.7 = (f32[16,128]{1,0:T(8,128)S(1)}, f32[16,128]{1,0:T(8,128)S(1)}, u32[]{:S(2)}, u32[]{:S(2)}) collective-permute-start(f32[16,128]{1,0:T(8,128)S(1)} %shard_map.90.p0), channel_id=1, source_target_pairs={{0,2},{1,3},{2,0},{3,1},{4,6},{5,7},{6,4},{7,5},{8,10},{9,11},{10,... | collective-permute-start | bytes 24584 | tf_op jit(solution)/shard_map/ppermute | solution.py:409
  38.8 0.6 collective-permute-start.6
  39.4 0.7 collective-permute-done.8.p3
  40.1 2.3 %collective-permute-done.7.p2 = f32[16,128]{1,0:T(8,128)S(1)} collective-permute-done((f32[16,128]{1,0:T(8,128)S(1)}, f32[16,128]{1,0:T(8,128)S(1)}, u32[]{:S(2)}, u32[]{:S(2)}) %collective-permute-start.7) | collective-permute-done | bytes 8224 | tf_op jit(solution)/shard_map/ppermute | solution.py:409
  42.4 1.2 %collective-permute-done.6.p1 = f32[16,128]{1,0:T(8,128)S(1)} collective-permute-done((f32[16,128]{1,0:T(8,128)S(1)}, f32[16,128]{1,0:T(8,128)S(1)}, u32[]{:S(2)}, u32[]{:S(2)}) %collective-permute-start.6) | collective-permute-done | bytes 8224 | tf_op jit(solution)/shard_map/ppermute | solution.py:409
  43.7 1.5 %shard_map.91 = (f32[16,40,128]{2,1,0:T(8,128)S(1)}, bf16[16,128,256]{2,1,0:T(8,128)(2,1)S(1)}, f32[8,128]{1,0:T(8,128)S(1)}) custom-call(f32[16,128]{1,0:T(8,128)S(1)} %shard_map.90.p0, f32[16,128]{1,0:T(8,128)S(1)} %collective-permute-done.6.p1, f32[16,128]{1,0:T(8,128)S(1)} %collective-permute-done.7.p2, f32[16,128]{1,0:T(8,128)S(1)} %collective-permute-done.8.p3, ...), custom_call_target="tpu_custom_call" | custom-call | flops 1207959552 | tf_op jit(solution)/shard_map/pallas_call | solution.py:433
  45.2 11.9 %all_to_all.16.parts = f32[16,40,128]{2,1,0:T(8,128)S(1)} all-to-all(f32[16,40,128]{2,1,0:T(8,128)S(1)} %get-tuple-element.49), channel_id=1, replica_groups=mesh['zy'=16,'core'=2,'x'=4] {'zy'}, dimensions={0} | all-to-all | bytes 655360 | tf_op jit(solution)/shard_map/all_to_all | solution.py:440
  57.1 1.7 %shard_map.92 = (bf16[144,512]{1,0:T(8,128)(2,1)S(1)}, bf16[144,512]{1,0:T(8,128)(2,1)S(1)}, f32[32,128]{1,0:T(8,128)S(1)}, f32[32,128]{1,0:T(8,128)S(1)}, f32[8...) custom-call(f32[16,40,128]{2,1,0:T(8,128)S(1)} %all_to_all.16.parts, f32[32,128]{1,0:T(8,128)S(1)} %get-tuple-element.44.lb, ...), custom_call_target="tpu_custom_call" | custom-call | flops 1207959552 | tf_op jit(solution)/shard_map/pallas_call | solution.py:441
  58.8 3.7 %all-to-all-start.2 = ((bf16[16,128,256]{2,1,0:T(8,128)(2,1)}), bf16[16,128,256]{2,1,0:T(8,128)(2,1)S(1)}, u32[]{:S(2)}, u32[]{:S(2)}) async-start(bf16[16,128,256]{2,1,0:T(8,128)(2,1)} %get-tuple-element.55), calls=%async_computation.2 | async-start | bytes 2097152 | tf_op jit(solution)/shard_map/all_to_all | solution.py:458
  62.5 0.1 collective-permute-start.9
  62.6 1.4 %collective-permute-done.9.received = bf16[144,512]{1,0:T(8,128)(2,1)S(1)} collective-permute-done((bf16[144,512]{1,0:T(8,128)(2,1)S(1)}, bf16[144,512]{1,0:T(8,128)(2,1)S(1)}, u32[]{:S(2)}, u32[]{:S(2)}) %collective-permute-start.9) | collective-permute-done | bytes 147488 | tf_op jit(solution)/shard_map/ppermute | solution.py:457
  63.9 0.1 shard_map.93.p0
  64.0 1.2 %collective-permute-start.12 = (bf16[144,512]{1,0:T(8,128)(2,1)S(1)}, bf16[144,512]{1,0:T(8,128)(2,1)S(1)}, u32[]{:S(2)}, u32[]{:S(2)}) collective-permute-start(bf16[144,512]{1,0:T(8,128)(2,1)S(1)} %shard_map.93.p0), channel_id=1, source_target_pairs={{0,3},{1,0},{2,1},{3,2},{4,7},{5,4},{6,5},{7,6},{8,11},{9,8},{10,9... | collective-permute-start | bytes 442376 | tf_op jit(solution)/shard_map/ppermute | solution.py:409
  65.3 0.9 %collective-permute-start.11 = (bf16[144,512]{1,0:T(8,128)(2,1)S(1)}, bf16[144,512]{1,0:T(8,128)(2,1)S(1)}, u32[]{:S(2)}, u32[]{:S(2)}) collective-permute-start(bf16[144,512]{1,0:T(8,128)(2,1)S(1)} %shard_map.93.p0), channel_id=1, source_target_pairs={{0,2},{1,3},{2,0},{3,1},{4,6},{5,7},{6,4},{7,5},{8,10},{9,11},{10,... | collective-permute-start | bytes 442376 | tf_op jit(solution)/shard_map/ppermute | solution.py:409
  66.2 0.1 collective-permute-start.10
  66.3 0.0 collective-permute-start.13
  66.3 1.2 %collective-permute-done.13.other_pot = f32[32,128]{1,0:T(8,128)S(1)} collective-permute-done((f32[32,128]{1,0:T(8,128)S(1)}, f32[32,128]{1,0:T(8,128)S(1)}, u32[]{:S(2)}, u32[]{:S(2)}) %collective-permute-start.13) | collective-permute-done | bytes 16416 | tf_op jit(solution)/shard_map/ppermute | solution.py:459
  67.5 3.3 %collective-permute-done.12.p3 = bf16[144,512]{1,0:T(8,128)(2,1)S(1)} collective-permute-done((bf16[144,512]{1,0:T(8,128)(2,1)S(1)}, bf16[144,512]{1,0:T(8,128)(2,1)S(1)}, u32[]{:S(2)}, u32[]{:S(2)}) %collective-permute-start.12) | collective-permute-done | bytes 147488 | tf_op jit(solution)/shard_map/ppermute | solution.py:409
  70.8 2.7 %collective-permute-done.11.p2 = bf16[144,512]{1,0:T(8,128)(2,1)S(1)} collective-permute-done((bf16[144,512]{1,0:T(8,128)(2,1)S(1)}, bf16[144,512]{1,0:T(8,128)(2,1)S(1)}, u32[]{:S(2)}, u32[]{:S(2)}) %collective-permute-start.11) | collective-permute-done | bytes 147488 | tf_op jit(solution)/shard_map/ppermute | solution.py:409
  73.5 2.0 %collective-permute-done.10.p1 = bf16[144,512]{1,0:T(8,128)(2,1)S(1)} collective-permute-done((bf16[144,512]{1,0:T(8,128)(2,1)S(1)}, bf16[144,512]{1,0:T(8,128)(2,1)S(1)}, u32[]{:S(2)}, u32[]{:S(2)}) %collective-permute-start.10) | collective-permute-done | bytes 147488 | tf_op jit(solution)/shard_map/ppermute | solution.py:409
  75.5 2.4 %all-to-all-done.2.sums = bf16[16,128,256]{2,1,0:T(8,128)(2,1)S(1)} async-done(((bf16[16,128,256]{2,1,0:T(8,128)(2,1)}), bf16[16,128,256]{2,1,0:T(8,128)(2,1)S(1)}, u32[]{:S(2)}, u32[]{:S(2)}) %all-to-all-start.2) | async-done | bytes 1048608 | tf_op jit(solution)/shard_map/all_to_all | solution.py:458
  77.9 1.2 %shard_map.94 = (f32[512,128]{1,0:T(8,128)}, f32[4,128]{1,0:T(4,128)}, f32[256,128]{1,0:T(8,128)}, f32[64,128]{1,0:T(8,128)}) custom-call(bf16[144,512]{1,0:T(8,128)(2,1)S(1)} %shard_map.93.p0, bf16[144,512]{1,0:T(8,128)(2,1)S(1)} %collective-permute-done.10.p1, bf16[144,512]{1,0:T(8,128)(2,1)S(1)} %collective-permute-done.11.p2, ...), custom_call_target="tpu_custom_call" | custom-call | tf_op jit(solution)/shard_map/pallas_call | solution.py:462
  (2 shorter events, 0.0 us)
Async XLA Ops:
  0.6 2.4 %collective-permute-start = (bf16[512,128]{1,0:T(8,128)(2,1)}, bf16[512,128]{1,0:T(8,128)(2,1)S(1)}, u32[]{:S(2)}, u32[]{:S(2)}) collective-permute-start(bf16[512,128]{1,0:T(8,128)(2,1)} %desc_a.1), channel_id=1, source_target_pairs={{0,4},{4,0},{1,5},{5,1},{2,6},{6,2},{3,7},{7,3},{8,12},{12,8},{9,1... | collective-permute-start | bytes 393224 | tf_op jit(solution)/shard_map/ppermute | solution.py:367
  5.7 1.4 %collective-permute-start.1 = (f32[24,128]{1,0:T(8,128)S(1)}, f32[24,128]{1,0:T(8,128)S(1)}, u32[]{:S(2)}, u32[]{:S(2)}) collective-permute-start(f32[24,128]{1,0:T(8,128)S(1)} %get-tuple-element.39.own), channel_id=1, source_target_pairs={{0,4},{4,0},{1,5},{5,1},{2,6},{6,2},{3,7},{7,3},{8,12},{12,8},{9,1... | collective-permute-start | bytes 36872 | tf_op jit(solution)/shard_map/ppermute | solution.py:411
  7.1 7.0 %collective-permute-start.4 = (f32[16,128]{1,0:T(8,128)S(1)}, f32[16,128]{1,0:T(8,128)S(1)}, u32[]{:S(2)}, u32[]{:S(2)}) collective-permute-start(f32[16,128]{1,0:T(8,128)S(1)} %get-tuple-element.40.p0), channel_id=1, source_target_pairs={{0,3},{1,0},{2,1},{3,2},{4,7},{5,4},{6,5},{7,6},{8,11},{9,8},{10,9... | collective-permute-start | bytes 24584 | tf_op jit(solution)/shard_map/ppermute | solution.py:409
  10.0 5.2 %collective-permute-start.3 = (f32[16,128]{1,0:T(8,128)S(1)}, f32[16,128]{1,0:T(8,128)S(1)}, u32[]{:S(2)}, u32[]{:S(2)}) collective-permute-start(f32[16,128]{1,0:T(8,128)S(1)} %get-tuple-element.40.p0), channel_id=1, source_target_pairs={{0,2},{1,3},{2,0},{3,1},{4,6},{5,7},{6,4},{7,5},{8,10},{9,11},{10,... | collective-permute-start | bytes 24584 | tf_op jit(solution)/shard_map/ppermute | solution.py:409
  10.8 4.9 %collective-permute-start.2 = (f32[16,128]{1,0:T(8,128)S(1)}, f32[16,128]{1,0:T(8,128)S(1)}, u32[]{:S(2)}, u32[]{:S(2)}) collective-permute-start(f32[16,128]{1,0:T(8,128)S(1)} %get-tuple-element.40.p0), channel_id=1, source_target_pairs={{0,1},{1,2},{2,3},{3,0},{4,5},{5,6},{6,7},{7,4},{8,9},{9,10},{10,1... | collective-permute-start | bytes 24584 | tf_op jit(solution)/shard_map/ppermute | solution.py:409
  35.2 1.2 %collective-permute-start.5 = (f32[16,128]{1,0:T(8,128)S(1)}, f32[16,128]{1,0:T(8,128)S(1)}, u32[]{:S(2)}, u32[]{:S(2)}) collective-permute-start(f32[16,128]{1,0:T(8,128)S(1)} %get-tuple-element.47.own), channel_id=1, source_target_pairs={{0,4},{4,0},{1,5},{5,1},{2,6},{6,2},{3,7},{7,3},{8,12},{12,8},{9,1... | collective-permute-start | bytes 24584 | tf_op jit(solution)/shard_map/ppermute | solution.py:432
  36.4 3.7 %collective-permute-start.8 = (f32[16,128]{1,0:T(8,128)S(1)}, f32[16,128]{1,0:T(8,128)S(1)}, u32[]{:S(2)}, u32[]{:S(2)}) collective-permute-start(f32[16,128]{1,0:T(8,128)S(1)} %shard_map.90.p0), channel_id=1, source_target_pairs={{0,3},{1,0},{2,1},{3,2},{4,7},{5,4},{6,5},{7,6},{8,11},{9,8},{10,9... | collective-permute-start | bytes 24584 | tf_op jit(solution)/shard_map/ppermute | solution.py:409
  37.3 5.2 %collective-permute-start.7 = (f32[16,128]{1,0:T(8,128)S(1)}, f32[16,128]{1,0:T(8,128)S(1)}, u32[]{:S(2)}, u32[]{:S(2)}) collective-permute-start(f32[16,128]{1,0:T(8,128)S(1)} %shard_map.90.p0), channel_id=1, source_target_pairs={{0,2},{1,3},{2,0},{3,1},{4,6},{5,7},{6,4},{7,5},{8,10},{9,11},{10,... | collective-permute-start | bytes 24584 | tf_op jit(solution)/shard_map/ppermute | solution.py:409
  38.8 4.9 %collective-permute-start.6 = (f32[16,128]{1,0:T(8,128)S(1)}, f32[16,128]{1,0:T(8,128)S(1)}, u32[]{:S(2)}, u32[]{:S(2)}) collective-permute-start(f32[16,128]{1,0:T(8,128)S(1)} %shard_map.90.p0), channel_id=1, source_target_pairs={{0,1},{1,2},{2,3},{3,0},{4,5},{5,6},{6,7},{7,4},{8,9},{9,10},{10,1... | collective-permute-start | bytes 24584 | tf_op jit(solution)/shard_map/ppermute | solution.py:409
  58.8 19.1 %all-to-all-start.2 = ((bf16[16,128,256]{2,1,0:T(8,128)(2,1)}), bf16[16,128,256]{2,1,0:T(8,128)(2,1)S(1)}, u32[]{:S(2)}, u32[]{:S(2)}) async-start(bf16[16,128,256]{2,1,0:T(8,128)(2,1)} %get-tuple-element.55), calls=%async_computation.2 | async-start | bytes 2097152 | tf_op jit(solution)/shard_map/all_to_all | solution.py:458
  62.5 1.5 %collective-permute-start.9 = (bf16[144,512]{1,0:T(8,128)(2,1)S(1)}, bf16[144,512]{1,0:T(8,128)(2,1)S(1)}, u32[]{:S(2)}, u32[]{:S(2)}) collective-permute-start(bf16[144,512]{1,0:T(8,128)(2,1)S(1)} %get-tuple-element.53), channel_id=1, source_target_pairs={{0,4},{4,0},{1,5},{5,1},{2,6},{6,2},{3,7},{7,3},{8,12},{12,8},{9,1... | collective-permute-start | bytes 442376 | tf_op jit(solution)/shard_map/ppermute | solution.py:457
  64.0 6.8 %collective-permute-start.12 = (bf16[144,512]{1,0:T(8,128)(2,1)S(1)}, bf16[144,512]{1,0:T(8,128)(2,1)S(1)}, u32[]{:S(2)}, u32[]{:S(2)}) collective-permute-start(bf16[144,512]{1,0:T(8,128)(2,1)S(1)} %shard_map.93.p0), channel_id=1, source_target_pairs={{0,3},{1,0},{2,1},{3,2},{4,7},{5,4},{6,5},{7,6},{8,11},{9,8},{10,9... | collective-permute-start | bytes 442376 | tf_op jit(solution)/shard_map/ppermute | solution.py:409
  65.3 8.3 %collective-permute-start.11 = (bf16[144,512]{1,0:T(8,128)(2,1)S(1)}, bf16[144,512]{1,0:T(8,128)(2,1)S(1)}, u32[]{:S(2)}, u32[]{:S(2)}) collective-permute-start(bf16[144,512]{1,0:T(8,128)(2,1)S(1)} %shard_map.93.p0), channel_id=1, source_target_pairs={{0,2},{1,3},{2,0},{3,1},{4,6},{5,7},{6,4},{7,5},{8,10},{9,11},{10,... | collective-permute-start | bytes 442376 | tf_op jit(solution)/shard_map/ppermute | solution.py:409
  66.2 9.4 %collective-permute-start.10 = (bf16[144,512]{1,0:T(8,128)(2,1)S(1)}, bf16[144,512]{1,0:T(8,128)(2,1)S(1)}, u32[]{:S(2)}, u32[]{:S(2)}) collective-permute-start(bf16[144,512]{1,0:T(8,128)(2,1)S(1)} %shard_map.93.p0), channel_id=1, source_target_pairs={{0,1},{1,2},{2,3},{3,0},{4,5},{5,6},{6,7},{7,4},{8,9},{9,10},{10,1... | collective-permute-start | bytes 442376 | tf_op jit(solution)/shard_map/ppermute | solution.py:409
  66.3 1.2 %collective-permute-start.13 = (f32[32,128]{1,0:T(8,128)S(1)}, f32[32,128]{1,0:T(8,128)S(1)}, u32[]{:S(2)}, u32[]{:S(2)}) collective-permute-start(f32[32,128]{1,0:T(8,128)S(1)} %get-tuple-element.57.own_pot), channel_id=1, source_target_pairs={{0,4},{4,0},{1,5},{5,1},{2,6},{6,2},{3,7},{7,3},{8,12},{12,8},{9,1... | collective-permute-start | bytes 49160 | tf_op jit(solution)/shard_map/ppermute | solution.py:459

commit v7 on v6

--- a/solution.py
+++ b/solution.py
@@ -79,16 +79,12 @@
 def prep_kernel(desc_b, g_all, lb_all, desc_a, la_all, bt_out, at_out, right_out, scale_out, shift_out, lb_out, la_out,
                 b_raw, a_raw, g_raw, lb_raw, vec, sems):
     core = lax.axis_index("core")
-    half = NK // 2
     load_g = pltpu.make_async_copy(g_all, g_raw, sems.at[0])
     load_a = pltpu.make_async_copy(desc_a, a_raw, sems.at[1])
     load_lb = pltpu.make_async_copy(lb_all, lb_raw, sems.at[2])
     load_la = pltpu.make_async_copy(la_all, la_out, sems.at[3])
-    loads = [
-        pltpu.make_async_copy(desc_b.at[pl.ds(q * half, half), core], b_raw.at[pl.ds(q * half, half)], sems.at[4 + q])
-        for q in range(2)
-    ]
-    for copy in (load_g, loads[0], load_a, loads[1], load_lb, load_la):
+    load_b = pltpu.make_async_copy(desc_b.at[:, core], b_raw, sems.at[4])
+    for copy in (load_g, load_a, load_b, load_lb, load_la):
         copy.start()
     load_g.wait()
     pick_cols(g_raw, core, vec)
@@ -104,10 +100,9 @@
         unit = unit_t(a_raw[span, :].T.astype(F32))
         at_out[:, span] = unit
         right_out[:, span] = two_parts(unit)
-    for q in range(2):
-        loads[q].wait()
-        for k in range(q * half, (q + 1) * half):
-            bt_out[:, k * CH : (k + 1) * CH] = unit_t(b_raw[k].T.astype(F32))
+    load_b.wait()
+    for k in range(NK):
+        bt_out[:, k * CH : (k + 1) * CH] = unit_t(b_raw[k].T.astype(F32))
     load_lb.wait()
     load_la.wait()
     pick_cols(lb_raw, core, lb_out)
@@ -384,7 +379,7 @@
             pltpu.VMEM((64, 128), F32),
             pltpu.VMEM((64, 128), F32),
             pltpu.VMEM((32, 128), F32),
-            pltpu.SemaphoreType.DMA((6,)),
+            pltpu.SemaphoreType.DMA((5,)),
         ],
         flops=8 * NC * DIM,
         bytes_accessed=2 * NC * DIM,

time: 79.4 us -> 79.3 us (level)
  no operation moved by 1% of the time
where the time goes in v7:
time: 79.3 us; the launch traced here: 79.1 us
  blocking collectives  28.8 us (36%)
  waiting for transfers between devices  20.8 us (26%)
  Pallas kernels  14.4 us (18%)
  starting transfers between devices  14.3 us (18%)
    all_to_all x2, blocking collectives, on_device(): parts = lax.all_to_all(msg, 'zy', 0, 0)  28.8 us
    ppermute x9, waiting for transfers between devices, over_x(): return [pair] + [lax.ppermute(pair, 'x', ring[s]) for s in (1, 2, 3)]  13.9 us
    ppermute x9, starting transfers between devices, over_x(): return [pair] + [lax.ppermute(pair, 'x', ring[s]) for s in (1, 2, 3)]  9.89 us
    all_to_all x1, starting transfers between devices, on_device(): sums = lax.all_to_all(sums, 'zy', 0, 0)  3.66 us
    pallas_call x1, Pallas kernels, on_device(): call(first_kernel, [VM] * 7, [pltpu.VMEM((NC, NR), BF16), sds(DIM, NR, dt...  2.65 us
    all_to_all x1, waiting for transfers between devices, on_device(): sums = lax.all_to_all(sums, 'zy', 0, 0)  2.37 us
    pallas_call x1, Pallas kernels, on_device(): call(kernel_matrix, [VM] * 2, [pltpu.VMEM((NR, NC), BF16)], flops=2 * PAS...  2.36 us
    pallas_call x1, Pallas kernels, on_device(): call(prep_kernel, [HB] * 5, [sds(DIM, NC, dtype=BF16), sds(DIM, 512, dtyp...  2.22 us
  transfers between devices with their start and end apart: 15, of which 13 were waited for; matrix products, arithmetic and copies ran while one was open for 0% of the time, Pallas kernels for 6%

profile of v7, /device:TPU:0, one launch (start us, length us, event | category | flops | bytes accessed | tf_op | source)
XLA Modules:
  0.0 79.1 jit_solution(15558264160982295387)
XLA Ops:
  0.6 0.1 collective-permute-start
  0.7 2.2 %shard_map.84 = (bf16[128,4096]{1,0:T(8,128)(2,1)S(1)}, bf16[128,512]{1,0:T(8,128)(2,1)S(1)}, bf16[256,512]{1,0:T(8,128)(2,1)S(1)}, f32[4096,128]{1,0:T(8,128)S(...) custom-call(bf16[16,2,256,128]{3,2,1,0:T(8,128)(2,1)} %bitcast.6, f32[64,128]{1,0:T(8,128)} %bitcast.7, ...), custom_call_target="tpu_custom_call" | custom-call | flops 4194304 | bytes 1048576 | tf_op jit(solution)/shard_map/pallas_call | solution.py:364
  2.9 0.0 collective-permute-done.other_a
  3.0 2.6 %shard_map.85 = (bf16[4096,1024]{1,0:T(8,128)(2,1)S(1)}, bf16[128,1024]{1,0:T(8,128)(2,1)S(1)}, f32[24,128]{1,0:T(8,128)S(1)}) custom-call(bf16[128,512]{1,0:T(8,128)(2,1)S(1)} %get-tuple-element.33.at_own, bf16[256,512]{1,0:T(8,128)(2,1)S(1)} %get-tuple-element.34.right_own, bf16[512,128]{1,0:T(8,128)(2,1)S(1)} %collective-permute-done.other_a, ...), custom_call_target="tpu_custom_call" | custom-call | flops 1073741824 | tf_op jit(solution)/shard_map/pallas_call | solution.py:394
  5.6 0.6 collective-permute-start.1
  6.2 0.8 %collective-permute-done.1.received = f32[24,128]{1,0:T(8,128)S(1)} collective-permute-done((f32[24,128]{1,0:T(8,128)S(1)}, f32[24,128]{1,0:T(8,128)S(1)}, u32[]{:S(2)}, u32[]{:S(2)}) %collective-permute-start.1) | collective-permute-done | bytes 12320 | tf_op jit(solution)/shard_map/ppermute | solution.py:406
  7.0 2.9 %collective-permute-start.4 = (f32[16,128]{1,0:T(8,128)S(1)}, f32[16,128]{1,0:T(8,128)S(1)}, u32[]{:S(2)}, u32[]{:S(2)}) collective-permute-start(f32[16,128]{1,0:T(8,128)S(1)} %get-tuple-element.40.p0), channel_id=1, source_target_pairs={{0,3},{1,0},{2,1},{3,2},{4,7},{5,4},{6,5},{7,6},{8,11},{9,8},{10,9... | collective-permute-start | bytes 24584 | tf_op jit(solution)/shard_map/ppermute | solution.py:404
  9.9 0.8 %collective-permute-start.3 = (f32[16,128]{1,0:T(8,128)S(1)}, f32[16,128]{1,0:T(8,128)S(1)}, u32[]{:S(2)}, u32[]{:S(2)}) collective-permute-start(f32[16,128]{1,0:T(8,128)S(1)} %get-tuple-element.40.p0), channel_id=1, source_target_pairs={{0,2},{1,3},{2,0},{3,1},{4,6},{5,7},{6,4},{7,5},{8,10},{9,11},{10,... | collective-permute-start | bytes 24584 | tf_op jit(solution)/shard_map/ppermute | solution.py:404
  10.7 0.9 %collective-permute-start.2 = (f32[16,128]{1,0:T(8,128)S(1)}, f32[16,128]{1,0:T(8,128)S(1)}, u32[]{:S(2)}, u32[]{:S(2)}) collective-permute-start(f32[16,128]{1,0:T(8,128)S(1)} %get-tuple-element.40.p0), channel_id=1, source_target_pairs={{0,1},{1,2},{2,3},{3,0},{4,5},{5,6},{6,7},{7,4},{8,9},{9,10},{10,1... | collective-permute-start | bytes 24584 | tf_op jit(solution)/shard_map/ppermute | solution.py:404
  11.6 2.4 %shard_map.87.k_mat = bf16[1024,4096]{1,0:T(8,128)(2,1)S(1)} custom-call(bf16[128,1024]{1,0:T(8,128)(2,1)S(1)} %get-tuple-element.42.a_t, bf16[128,4096]{1,0:T(8,128)(2,1)S(1)} %get-tuple-element.36.b_t), custom_call_target="tpu_custom_call" | custom-call | flops 1073741824 | tf_op jit(solution)/shard_map/pallas_call | solution.py:407
  14.0 0.0 collective-permute-done.4.p3
  14.0 1.1 %collective-permute-done.3.p2 = f32[16,128]{1,0:T(8,128)S(1)} collective-permute-done((f32[16,128]{1,0:T(8,128)S(1)}, f32[16,128]{1,0:T(8,128)S(1)}, u32[]{:S(2)}, u32[]{:S(2)}) %collective-permute-start.3) | collective-permute-done | bytes 8224 | tf_op jit(solution)/shard_map/ppermute | solution.py:404
  15.1 0.5 collective-permute-done.2.p1
  15.6 1.3 %shard_map.88 = (f32[16,40,128]{2,1,0:T(8,128)S(1)}, f32[8,128]{1,0:T(8,128)S(1)}) custom-call(f32[16,128]{1,0:T(8,128)S(1)} %get-tuple-element.40.p0, f32[16,128]{1,0:T(8,128)S(1)} %collective-permute-done.2.p1, f32[16,128]{1,0:T(8,128)S(1)} %collective-permute-done.3.p2, f32[16,128]{1,0:T(8,128)S(1)} %collective-permute-done.4.p3, ...), custom_call_target="tpu_custom_call" | custom-call | flops 134217728 | tf_op jit(solution)/shard_map/pallas_call | solution.py:410
  16.9 16.9 %all_to_all.15.parts = f32[16,40,128]{2,1,0:T(8,128)S(1)} all-to-all(f32[16,40,128]{2,1,0:T(8,128)S(1)} %get-tuple-element.43), channel_id=1, replica_groups=mesh['zy'=16,'core'=2,'x'=4] {'zy'}, dimensions={0} | all-to-all | bytes 655360 | tf_op jit(solution)/shard_map/all_to_all | solution.py:418
  33.8 1.3 %shard_map.89 = (f32[16,128]{1,0:T(8,128)S(1)}, f32[8,128]{1,0:T(8,128)S(1)}) custom-call(f32[16,40,128]{2,1,0:T(8,128)S(1)} %all_to_all.15.parts, f32[32,128]{1,0:T(8,128)S(1)} %get-tuple-element.44.lb, bf16[4096,1024]{1,0:T(8,128)(2,1)S(1)} %get-tuple-element.45.kt_mat, f32[8,128]{1,0:T(8,128)S(1)} %get-tuple-element.46.base), custom_call_target="tpu_custom_call" | custom-call | flops 134217728 | tf_op jit(solution)/shard_map/pallas_call | solution.py:419
  35.1 0.0 collective-permute-start.5
  35.1 1.2 %collective-permute-done.5.received = f32[16,128]{1,0:T(8,128)S(1)} collective-permute-done((f32[16,128]{1,0:T(8,128)S(1)}, f32[16,128]{1,0:T(8,128)S(1)}, u32[]{:S(2)}, u32[]{:S(2)}) %collective-permute-start.5) | collective-permute-done | bytes 8224 | tf_op jit(solution)/shard_map/ppermute | solution.py:427
  36.3 0.9 %collective-permute-start.8 = (f32[16,128]{1,0:T(8,128)S(1)}, f32[16,128]{1,0:T(8,128)S(1)}, u32[]{:S(2)}, u32[]{:S(2)}) collective-permute-start(f32[16,128]{1,0:T(8,128)S(1)} %shard_map.90.p0), channel_id=1, source_target_pairs={{0,3},{1,0},{2,1},{3,2},{4,7},{5,4},{6,5},{7,6},{8,11},{9,8},{10,9... | collective-permute-start | bytes 24584 | tf_op jit(solution)/shard_map/ppermute | solution.py:404
  37.2 1.5 %collective-permute-start.7 = (f32[16,128]{1,0:T(8,128)S(1)}, f32[16,128]{1,0:T(8,128)S(1)}, u32[]{:S(2)}, u32[]{:S(2)}) collective-permute-start(f32[16,128]{1,0:T(8,128)S(1)} %shard_map.90.p0), channel_id=1, source_target_pairs={{0,2},{1,3},{2,0},{3,1},{4,6},{5,7},{6,4},{7,5},{8,10},{9,11},{10,... | collective-permute-start | bytes 24584 | tf_op jit(solution)/shard_map/ppermute | solution.py:404
  38.7 0.6 collective-permute-start.6
  39.3 0.7 collective-permute-done.8.p3
  40.0 2.3 %collective-permute-done.7.p2 = f32[16,128]{1,0:T(8,128)S(1)} collective-permute-done((f32[16,128]{1,0:T(8,128)S(1)}, f32[16,128]{1,0:T(8,128)S(1)}, u32[]{:S(2)}, u32[]{:S(2)}) %collective-permute-start.7) | collective-permute-done | bytes 8224 | tf_op jit(solution)/shard_map/ppermute | solution.py:404
  42.3 1.2 %collective-permute-done.6.p1 = f32[16,128]{1,0:T(8,128)S(1)} collective-permute-done((f32[16,128]{1,0:T(8,128)S(1)}, f32[16,128]{1,0:T(8,128)S(1)}, u32[]{:S(2)}, u32[]{:S(2)}) %collective-permute-start.6) | collective-permute-done | bytes 8224 | tf_op jit(solution)/shard_map/ppermute | solution.py:404
  43.6 1.5 %shard_map.91 = (f32[16,40,128]{2,1,0:T(8,128)S(1)}, bf16[16,128,256]{2,1,0:T(8,128)(2,1)S(1)}, f32[8,128]{1,0:T(8,128)S(1)}) custom-call(f32[16,128]{1,0:T(8,128)S(1)} %shard_map.90.p0, f32[16,128]{1,0:T(8,128)S(1)} %collective-permute-done.6.p1, f32[16,128]{1,0:T(8,128)S(1)} %collective-permute-done.7.p2, f32[16,128]{1,0:T(8,128)S(1)} %collective-permute-done.8.p3, ...), custom_call_target="tpu_custom_call" | custom-call | flops 1207959552 | tf_op jit(solution)/shard_map/pallas_call | solution.py:428
  45.1 11.9 %all_to_all.16.parts = f32[16,40,128]{2,1,0:T(8,128)S(1)} all-to-all(f32[16,40,128]{2,1,0:T(8,128)S(1)} %get-tuple-element.49), channel_id=1, replica_groups=mesh['zy'=16,'core'=2,'x'=4] {'zy'}, dimensions={0} | all-to-all | bytes 655360 | tf_op jit(solution)/shard_map/all_to_all | solution.py:435
  57.0 1.7 %shard_map.92 = (bf16[144,512]{1,0:T(8,128)(2,1)S(1)}, bf16[144,512]{1,0:T(8,128)(2,1)S(1)}, f32[32,128]{1,0:T(8,128)S(1)}, f32[32,128]{1,0:T(8,128)S(1)}, f32[8...) custom-call(f32[16,40,128]{2,1,0:T(8,128)S(1)} %all_to_all.16.parts, f32[32,128]{1,0:T(8,128)S(1)} %get-tuple-element.44.lb, ...), custom_call_target="tpu_custom_call" | custom-call | flops 1207959552 | tf_op jit(solution)/shard_map/pallas_call | solution.py:436
  58.7 3.7 %all-to-all-start.2 = ((bf16[16,128,256]{2,1,0:T(8,128)(2,1)}), bf16[16,128,256]{2,1,0:T(8,128)(2,1)S(1)}, u32[]{:S(2)}, u32[]{:S(2)}) async-start(bf16[16,128,256]{2,1,0:T(8,128)(2,1)} %get-tuple-element.55), calls=%async_computation.2 | async-start | bytes 2097152 | tf_op jit(solution)/shard_map/all_to_all | solution.py:453
  62.4 0.1 collective-permute-start.9
  62.5 1.4 %collective-permute-done.9.received = bf16[144,512]{1,0:T(8,128)(2,1)S(1)} collective-permute-done((bf16[144,512]{1,0:T(8,128)(2,1)S(1)}, bf16[144,512]{1,0:T(8,128)(2,1)S(1)}, u32[]{:S(2)}, u32[]{:S(2)}) %collective-permute-start.9) | collective-permute-done | bytes 147488 | tf_op jit(solution)/shard_map/ppermute | solution.py:452
  63.8 0.1 shard_map.93.p0
  63.9 1.2 %collective-permute-start.12 = (bf16[144,512]{1,0:T(8,128)(2,1)S(1)}, bf16[144,512]{1,0:T(8,128)(2,1)S(1)}, u32[]{:S(2)}, u32[]{:S(2)}) collective-permute-start(bf16[144,512]{1,0:T(8,128)(2,1)S(1)} %shard_map.93.p0), channel_id=1, source_target_pairs={{0,3},{1,0},{2,1},{3,2},{4,7},{5,4},{6,5},{7,6},{8,11},{9,8},{10,9... | collective-permute-start | bytes 442376 | tf_op jit(solution)/shard_map/ppermute | solution.py:404
  65.2 0.9 %collective-permute-start.11 = (bf16[144,512]{1,0:T(8,128)(2,1)S(1)}, bf16[144,512]{1,0:T(8,128)(2,1)S(1)}, u32[]{:S(2)}, u32[]{:S(2)}) collective-permute-start(bf16[144,512]{1,0:T(8,128)(2,1)S(1)} %shard_map.93.p0), channel_id=1, source_target_pairs={{0,2},{1,3},{2,0},{3,1},{4,6},{5,7},{6,4},{7,5},{8,10},{9,11},{10,... | collective-permute-start | bytes 442376 | tf_op jit(solution)/shard_map/ppermute | solution.py:404
  66.1 0.1 collective-permute-start.10
  66.2 0.0 collective-permute-start.13
  66.2 1.2 %collective-permute-done.13.other_pot = f32[32,128]{1,0:T(8,128)S(1)} collective-permute-done((f32[32,128]{1,0:T(8,128)S(1)}, f32[32,128]{1,0:T(8,128)S(1)}, u32[]{:S(2)}, u32[]{:S(2)}) %collective-permute-start.13) | collective-permute-done | bytes 16416 | tf_op jit(solution)/shard_map/ppermute | solution.py:454
  67.4 3.3 %collective-permute-done.12.p3 = bf16[144,512]{1,0:T(8,128)(2,1)S(1)} collective-permute-done((bf16[144,512]{1,0:T(8,128)(2,1)S(1)}, bf16[144,512]{1,0:T(8,128)(2,1)S(1)}, u32[]{:S(2)}, u32[]{:S(2)}) %collective-permute-start.12) | collective-permute-done | bytes 147488 | tf_op jit(solution)/shard_map/ppermute | solution.py:404
  70.7 2.7 %collective-permute-done.11.p2 = bf16[144,512]{1,0:T(8,128)(2,1)S(1)} collective-permute-done((bf16[144,512]{1,0:T(8,128)(2,1)S(1)}, bf16[144,512]{1,0:T(8,128)(2,1)S(1)}, u32[]{:S(2)}, u32[]{:S(2)}) %collective-permute-start.11) | collective-permute-done | bytes 147488 | tf_op jit(solution)/shard_map/ppermute | solution.py:404
  73.4 2.0 %collective-permute-done.10.p1 = bf16[144,512]{1,0:T(8,128)(2,1)S(1)} collective-permute-done((bf16[144,512]{1,0:T(8,128)(2,1)S(1)}, bf16[144,512]{1,0:T(8,128)(2,1)S(1)}, u32[]{:S(2)}, u32[]{:S(2)}) %collective-permute-start.10) | collective-permute-done | bytes 147488 | tf_op jit(solution)/shard_map/ppermute | solution.py:404
  75.4 2.4 %all-to-all-done.2.sums = bf16[16,128,256]{2,1,0:T(8,128)(2,1)S(1)} async-done(((bf16[16,128,256]{2,1,0:T(8,128)(2,1)}), bf16[16,128,256]{2,1,0:T(8,128)(2,1)S(1)}, u32[]{:S(2)}, u32[]{:S(2)}) %all-to-all-start.2) | async-done | bytes 1048608 | tf_op jit(solution)/shard_map/all_to_all | solution.py:453
  77.8 1.2 %shard_map.94 = (f32[512,128]{1,0:T(8,128)}, f32[4,128]{1,0:T(4,128)}, f32[256,128]{1,0:T(8,128)}, f32[64,128]{1,0:T(8,128)}) custom-call(bf16[144,512]{1,0:T(8,128)(2,1)S(1)} %shard_map.93.p0, bf16[144,512]{1,0:T(8,128)(2,1)S(1)} %collective-permute-done.10.p1, bf16[144,512]{1,0:T(8,128)(2,1)S(1)} %collective-permute-done.11.p2, ...), custom_call_target="tpu_custom_call" | custom-call | tf_op jit(solution)/shard_map/pallas_call | solution.py:457
  (2 shorter events, 0.0 us)
Async XLA Ops:
  0.6 2.3 %collective-permute-start = (bf16[512,128]{1,0:T(8,128)(2,1)}, bf16[512,128]{1,0:T(8,128)(2,1)S(1)}, u32[]{:S(2)}, u32[]{:S(2)}) collective-permute-start(bf16[512,128]{1,0:T(8,128)(2,1)} %desc_a.1), channel_id=1, source_target_pairs={{0,4},{4,0},{1,5},{5,1},{2,6},{6,2},{3,7},{7,3},{8,12},{12,8},{9,1... | collective-permute-start | bytes 393224 | tf_op jit(solution)/shard_map/ppermute | solution.py:362
  5.6 1.4 %collective-permute-start.1 = (f32[24,128]{1,0:T(8,128)S(1)}, f32[24,128]{1,0:T(8,128)S(1)}, u32[]{:S(2)}, u32[]{:S(2)}) collective-permute-start(f32[24,128]{1,0:T(8,128)S(1)} %get-tuple-element.39.own), channel_id=1, source_target_pairs={{0,4},{4,0},{1,5},{5,1},{2,6},{6,2},{3,7},{7,3},{8,12},{12,8},{9,1... | collective-permute-start | bytes 36872 | tf_op jit(solution)/shard_map/ppermute | solution.py:406
  7.0 7.0 %collective-permute-start.4 = (f32[16,128]{1,0:T(8,128)S(1)}, f32[16,128]{1,0:T(8,128)S(1)}, u32[]{:S(2)}, u32[]{:S(2)}) collective-permute-start(f32[16,128]{1,0:T(8,128)S(1)} %get-tuple-element.40.p0), channel_id=1, source_target_pairs={{0,3},{1,0},{2,1},{3,2},{4,7},{5,4},{6,5},{7,6},{8,11},{9,8},{10,9... | collective-permute-start | bytes 24584 | tf_op jit(solution)/shard_map/ppermute | solution.py:404
  9.9 5.2 %collective-permute-start.3 = (f32[16,128]{1,0:T(8,128)S(1)}, f32[16,128]{1,0:T(8,128)S(1)}, u32[]{:S(2)}, u32[]{:S(2)}) collective-permute-start(f32[16,128]{1,0:T(8,128)S(1)} %get-tuple-element.40.p0), channel_id=1, source_target_pairs={{0,2},{1,3},{2,0},{3,1},{4,6},{5,7},{6,4},{7,5},{8,10},{9,11},{10,... | collective-permute-start | bytes 24584 | tf_op jit(solution)/shard_map/ppermute | solution.py:404
  10.7 4.9 %collective-permute-start.2 = (f32[16,128]{1,0:T(8,128)S(1)}, f32[16,128]{1,0:T(8,128)S(1)}, u32[]{:S(2)}, u32[]{:S(2)}) collective-permute-start(f32[16,128]{1,0:T(8,128)S(1)} %get-tuple-element.40.p0), channel_id=1, source_target_pairs={{0,1},{1,2},{2,3},{3,0},{4,5},{5,6},{6,7},{7,4},{8,9},{9,10},{10,1... | collective-permute-start | bytes 24584 | tf_op jit(solution)/shard_map/ppermute | solution.py:404
  35.1 1.2 %collective-permute-start.5 = (f32[16,128]{1,0:T(8,128)S(1)}, f32[16,128]{1,0:T(8,128)S(1)}, u32[]{:S(2)}, u32[]{:S(2)}) collective-permute-start(f32[16,128]{1,0:T(8,128)S(1)} %get-tuple-element.47.own), channel_id=1, source_target_pairs={{0,4},{4,0},{1,5},{5,1},{2,6},{6,2},{3,7},{7,3},{8,12},{12,8},{9,1... | collective-permute-start | bytes 24584 | tf_op jit(solution)/shard_map/ppermute | solution.py:427
  36.3 3.7 %collective-permute-start.8 = (f32[16,128]{1,0:T(8,128)S(1)}, f32[16,128]{1,0:T(8,128)S(1)}, u32[]{:S(2)}, u32[]{:S(2)}) collective-permute-start(f32[16,128]{1,0:T(8,128)S(1)} %shard_map.90.p0), channel_id=1, source_target_pairs={{0,3},{1,0},{2,1},{3,2},{4,7},{5,4},{6,5},{7,6},{8,11},{9,8},{10,9... | collective-permute-start | bytes 24584 | tf_op jit(solution)/shard_map/ppermute | solution.py:404
  37.2 5.2 %collective-permute-start.7 = (f32[16,128]{1,0:T(8,128)S(1)}, f32[16,128]{1,0:T(8,128)S(1)}, u32[]{:S(2)}, u32[]{:S(2)}) collective-permute-start(f32[16,128]{1,0:T(8,128)S(1)} %shard_map.90.p0), channel_id=1, source_target_pairs={{0,2},{1,3},{2,0},{3,1},{4,6},{5,7},{6,4},{7,5},{8,10},{9,11},{10,... | collective-permute-start | bytes 24584 | tf_op jit(solution)/shard_map/ppermute | solution.py:404
  38.7 4.9 %collective-permute-start.6 = (f32[16,128]{1,0:T(8,128)S(1)}, f32[16,128]{1,0:T(8,128)S(1)}, u32[]{:S(2)}, u32[]{:S(2)}) collective-permute-start(f32[16,128]{1,0:T(8,128)S(1)} %shard_map.90.p0), channel_id=1, source_target_pairs={{0,1},{1,2},{2,3},{3,0},{4,5},{5,6},{6,7},{7,4},{8,9},{9,10},{10,1... | collective-permute-start | bytes 24584 | tf_op jit(solution)/shard_map/ppermute | solution.py:404
  58.7 19.1 %all-to-all-start.2 = ((bf16[16,128,256]{2,1,0:T(8,128)(2,1)}), bf16[16,128,256]{2,1,0:T(8,128)(2,1)S(1)}, u32[]{:S(2)}, u32[]{:S(2)}) async-start(bf16[16,128,256]{2,1,0:T(8,128)(2,1)} %get-tuple-element.55), calls=%async_computation.2 | async-start | bytes 2097152 | tf_op jit(solution)/shard_map/all_to_all | solution.py:453
  62.4 1.5 %collective-permute-start.9 = (bf16[144,512]{1,0:T(8,128)(2,1)S(1)}, bf16[144,512]{1,0:T(8,128)(2,1)S(1)}, u32[]{:S(2)}, u32[]{:S(2)}) collective-permute-start(bf16[144,512]{1,0:T(8,128)(2,1)S(1)} %get-tuple-element.53), channel_id=1, source_target_pairs={{0,4},{4,0},{1,5},{5,1},{2,6},{6,2},{3,7},{7,3},{8,12},{12,8},{9,1... | collective-permute-start | bytes 442376 | tf_op jit(solution)/shard_map/ppermute | solution.py:452
  63.9 6.8 %collective-permute-start.12 = (bf16[144,512]{1,0:T(8,128)(2,1)S(1)}, bf16[144,512]{1,0:T(8,128)(2,1)S(1)}, u32[]{:S(2)}, u32[]{:S(2)}) collective-permute-start(bf16[144,512]{1,0:T(8,128)(2,1)S(1)} %shard_map.93.p0), channel_id=1, source_target_pairs={{0,3},{1,0},{2,1},{3,2},{4,7},{5,4},{6,5},{7,6},{8,11},{9,8},{10,9... | collective-permute-start | bytes 442376 | tf_op jit(solution)/shard_map/ppermute | solution.py:404
  65.2 8.3 %collective-permute-start.11 = (bf16[144,512]{1,0:T(8,128)(2,1)S(1)}, bf16[144,512]{1,0:T(8,128)(2,1)S(1)}, u32[]{:S(2)}, u32[]{:S(2)}) collective-permute-start(bf16[144,512]{1,0:T(8,128)(2,1)S(1)} %shard_map.93.p0), channel_id=1, source_target_pairs={{0,2},{1,3},{2,0},{3,1},{4,6},{5,7},{6,4},{7,5},{8,10},{9,11},{10,... | collective-permute-start | bytes 442376 | tf_op jit(solution)/shard_map/ppermute | solution.py:404
  66.1 9.4 %collective-permute-start.10 = (bf16[144,512]{1,0:T(8,128)(2,1)S(1)}, bf16[144,512]{1,0:T(8,128)(2,1)S(1)}, u32[]{:S(2)}, u32[]{:S(2)}) collective-permute-start(bf16[144,512]{1,0:T(8,128)(2,1)S(1)} %shard_map.93.p0), channel_id=1, source_target_pairs={{0,1},{1,2},{2,3},{3,0},{4,5},{5,6},{6,7},{7,4},{8,9},{9,10},{10,1... | collective-permute-start | bytes 442376 | tf_op jit(solution)/shard_map/ppermute | solution.py:404
  66.2 1.2 %collective-permute-start.13 = (f32[32,128]{1,0:T(8,128)S(1)}, f32[32,128]{1,0:T(8,128)S(1)}, u32[]{:S(2)}, u32[]{:S(2)}) collective-permute-start(f32[32,128]{1,0:T(8,128)S(1)} %get-tuple-element.57.own_pot), channel_id=1, source_target_pairs={{0,4},{4,0},{1,5},{5,1},{2,6},{6,2},{3,7},{7,3},{8,12},{12,8},{9,1... | collective-permute-start | bytes 49160 | tf_op jit(solution)/shard_map/ppermute | solution.py:454
